TPU v7x, 128 devices: a whole 4x4x4 slice. The times are simulated.
128 devices in a mesh: rows: 16 (over y, x), cols: 8 (over z, core).
Axes of the slice: x: 4, y: 4, z: 4, core: 2. Of those that a mesh axis runs over, the one named last changes fastest.
Arguments:
- embeddings: bfloat16 [12288, 1024], P('rows'), may hold values from -6 to 6
- landmarks: bfloat16 [8192, 1024], P('cols', 'rows'), may hold values from -6 to 6
- factor_rows: bfloat16 [8192, 16, 512], P('cols', None, 'rows'), may hold values from -0.0625 to 0.0625
- diag_inverse: bfloat16 [16, 512, 512], P('cols'), as said below
Outputs:
- features: bfloat16 [12288, 8192], P('rows', 'cols')
Inputs may be any that keep to these rules, and one draw needn't show every extreme that they name: `diag_inverse`: each block is lower triangular with a positive diagonal.
All inputs are finite; a program needn't handle non-finite values.
Results may differ from a plain program's by a relative error of at most 0.011.
Values may be sent and summed in bfloat16 or wider, within the bound.
No kernel may reach another device: no remote copies, remote signals or barrier semaphores. Data moves between devices by JAX's collectives and lax.ppermute only.
A program may use at most 128 MiB of HBM per device.

v0:
```python
import functools
import math

import jax
import jax.numpy as jnp
from jax import lax
from jax.experimental import pallas as pl
from jax.experimental.pallas import tpu as pltpu
from jax.sharding import PartitionSpec as P

CHUNKS = 2
SIDE = 4
LEAD = 64
SLAB = 32
BF = jnp.bfloat16
F32 = jnp.float32
ANY = pl.BlockSpec(memory_space=pl.ANY)
SMEM = pl.BlockSpec(memory_space=pltpu.SMEM)
VMEM = pl.BlockSpec(memory_space=pltpu.VMEM)


def mm(a, b):
    return jnp.dot(a, b, preferred_element_type=F32)


def after(x, *deps):
    return lax.optimization_barrier((x, *deps))[0]


PIECES = ((0, (0, 1, 2, 3)), (1, (0, 1, 2, 3)), (3, (0, 1, 2, 3)), (2, (0, 1)), (2, (2, 3)))
N_PIECES = 2 * len(PIECES)


def piece_places(info):
    core, y, x = info[1], info[2], info[3]
    for which, parity in ((0, core), (1, 1 - core)):
        for i, (e, along) in enumerate(PIECES):
            for j, d in enumerate(along):
                dy, dx = jnp.where(parity == 0, e, d), jnp.where(parity == 0, d, e)
                yield which * len(PIECES) + i, j, parity, ((y + dy) % SIDE) * SIDE + (x + dx) % SIDE


def start_pieces(info, pieces, r, lv, acc, sems):
    blocks = lv.shape[2] // SLAB
    for i, d, parity, place in piece_places(info):
        pltpu.make_async_copy(pieces[i].at[d], lv.at[parity, place], sems.at[parity]).start()
    copies = [[] for _ in range(2 * blocks)]
    for half in range(2):
        copies[half * blocks].append(pltpu.make_async_copy(r.at[half], acc.at[half], sems.at[2 * blocks + half]))
        copies[half * blocks][0].start()
        copies[half * blocks].append(pltpu.make_async_copy(lv.at[half], lv.at[half], sems.at[half]))
    return copies


def start_diag(info, head, dt_own, dt_oth, gv, dv, sem):
    core = info[1]
    depth = gv.shape[2]
    pltpu.make_async_copy(head.at[:, :, pl.ds(LEAD, depth)], gv, sem.at[0]).start()
    pltpu.make_async_copy(dt_own, dv.at[core], sem.at[1]).start()
    pltpu.make_async_copy(dt_oth, dv.at[1 - core], sem.at[1]).start()


def wait_diag(gv, dv, sem):
    pltpu.make_async_copy(gv, gv, sem.at[0]).wait()
    pltpu.make_async_copy(dv, dv, sem.at[1]).wait()


def solve(running, diag, dt, f):
    size = dt.shape[-1]

    def column(i):
        return running[i // 2, :, (i % 2) * size:(i % 2 + 1) * size]

    def store(i, value):
        f[i // 2, :, (i % 2) * size:(i % 2 + 1) * size] = value

    def left(i, k):
        block = diag[i // 2, :, k * SLAB:(k + 1) * SLAB, (i % 2) * size:(i % 2 + 1) * size]
        return block.reshape(size, size)

    f0 = mm_t(column(0).astype(BF), dt[0, 0]).astype(BF)
    store(0, f0)
    f1 = mm_t((column(1) - mm(f0, left(1, 0))).astype(BF), dt[0, 1]).astype(BF)
    store(1, f1)
    f2 = mm_t((column(2) - mm(f0, left(2, 0)) - mm(f1, left(2, 1))).astype(BF), dt[1, 0]).astype(BF)
    store(2, f2)
    f3 = column(3) - mm(f0, left(3, 0)) - mm(f1, left(3, 1)) - mm(f2, left(3, 2))
    store(3, mm_t(f3.astype(BF), dt[1, 1]).astype(BF))


def hold_kernel(*refs):
    pass


def pick_kernel(info, first, other, out):
    out[...] = jnp.where(info[0] == 1, first[...], other[...])


def scores_kernel(scale, first, info, embeddings, dt_own, dt_oth, head, out, f, emb, lm, gv, dv, sem):
    plane, core = info[0], info[1]
    tokens = embeddings.shape[0] // 2
    ce = pltpu.make_async_copy(embeddings.at[pl.ds(core * tokens + first, emb.shape[0])], emb, sem.at[4])
    ce.start()
    lead = lm.shape[2]
    copies = [pltpu.make_async_copy(head.at[i, :, pl.ds(0, lead)], lm.at[i], sem.at[2 + i]) for i in range(2)]
    for copy in copies:
        copy.start()
    pl.when(plane == 0)(lambda: start_diag(info, head, dt_own, dt_oth, gv, dv, sem))
    ce.wait()
    for half in range(2):
        copies[half].wait()
        points = lm[half].reshape(emb.shape[1], lm.shape[3])
        out[half] = jnp.exp(mm(emb[...], points) * scale)

    @pl.when(plane == 0)
    def _():
        wait_diag(gv, dv, sem)
        solve(out, gv, dv, f)


def start_factor(factor, r, lv, acc, sems):
    depth = lv.shape[2]
    first = factor.shape[2] - depth
    blocks = depth // SLAB
    copies = []
    for half in range(2):
        for k in range(blocks):
            source = factor.at[half, :, pl.ds(first + k * SLAB, SLAB)]
            target = lv.at[half, :, pl.ds(k * SLAB, SLAB)]
            copies.append([pltpu.make_async_copy(source, target, sems.at[half * blocks + k])])
            copies[-1][0].start()
            if k == 0 and r is not None:
                copies[-1].append(pltpu.make_async_copy(r.at[half], acc.at[half], sems.at[2 * blocks + half]))
                copies[-1][1].start()
    return copies


def subtract(acc, a, lv, copies):
    size = lv.shape[1] * SLAB
    blocks = lv.shape[2] // SLAB
    for half in range(2):
        for k in range(blocks):
            for copy in copies[half * blocks + k]:
                copy.wait()
            left = a[k // 2, :, (k % 2) * size:(k % 2 + 1) * size]
            acc[half] -= mm(left, lv[half, :, k * SLAB:(k + 1) * SLAB].reshape(size, -1))


def finish_kernel(role, info, r, a, head, dt_own, dt_oth, *refs):
    last = role == SIDE - 1
    n_factor = N_PIECES if role == 1 else 1
    factor, refs = refs[:n_factor], refs[n_factor:]
    if last:
        part, earlier, (keep, give, f, acc, lv, gv, dv, sems, sem) = refs[0], refs[1:SIDE], refs[SIDE:]
    else:
        f, acc, lv, gv, dv, sems, sem = refs
    plane, core = info[0], info[1]

    @pl.when(plane == role)
    def _():
        if role == 1:
            copies = start_pieces(info, factor, r, lv, acc, sems)
        else:
            copies = start_factor(factor[0], r, lv, acc, sems)
        start_diag(info, head, dt_own, dt_oth, gv, dv, sem)
        subtract(acc, a, lv, copies)
        if last:
            acc[...] += part[...].astype(F32)
        wait_diag(gv, dv, sem)
        solve(acc, gv, dv, f)
        if last:
            keep[...] = f[pl.ds(core, 1)][0]
            give[...] = f[pl.ds(1 - core, 1)][0]

    if last:
        for z, done in enumerate(earlier):

            @pl.when(plane == z)
            def _():
                c0 = pltpu.make_async_copy(done.at[core], keep, sems.at[0])
                c1 = pltpu.make_async_copy(done.at[1 - core], give, sems.at[1])
                c0.start()
                c1.start()
                c0.wait()
                c1.wait()


def partial_kernel(info, factor, own, p, acc, lv, sems):
    @pl.when(info[0] == 1)
    def _():
        copies = start_factor(factor, None, lv, acc, sems)
        acc[...] = jnp.zeros_like(acc)
        subtract(acc, own, lv, copies)
        p[...] = acc[...].astype(BF)


def update_kernel(info, r, to_3, to_2, *refs):
    pieces, (r_out, acc, lv, av, sems, sem) = refs[:N_PIECES], refs[N_PIECES:]

    @pl.when(info[0] >= 2)
    def _():
        for plane, a in ((2, to_2), (3, to_3)):
            pl.when(info[0] == plane)(lambda a=a: pltpu.make_async_copy(a, av, sem).start())
        copies = start_pieces(info, pieces, r, lv, acc, sems)
        pltpu.make_async_copy(to_2, av, sem).wait()
        subtract(acc, av, lv, copies)
        out = pltpu.make_async_copy(acc, r_out, sem)
        out.start()
        out.wait()


def mm_t(a, b):
    return lax.dot_general(a, b, (((1,), (1,)), ((), ())), preferred_element_type=F32)


def params(mib=60):
    return pltpu.CompilerParams(vmem_limit_bytes=mib << 20)


def cost(us):
    return pl.CostEstimate(flops=int(us * 1e9), bytes_accessed=1 << 10, transcendentals=0)


def per_device(embeddings, landmarks, factor_rows, diag_inverse):
    tokens, depth = embeddings.shape
    rows = lax.axis_size("rows")
    planes = lax.axis_size("cols") // 2
    here = lax.axis_index("cols")
    plane, core = here // 2, here % 2
    row = lax.axis_index("rows")
    own_rows, blocks, slab = factor_rows.shape
    size = diag_inverse.shape[1]
    lead = landmarks.shape[1]
    n = CHUNKS
    half = tokens // 2
    t = half // n
    scale = 0.5 / math.sqrt(depth)
    per_plane = blocks // planes
    info = jnp.stack([plane, core, row // SIDE, row % SIDE]).astype(jnp.int32)

    def send(x, source, target):
        return lax.ppermute(x, "cols", [(2 * source + k, 2 * target + k) for k in range(2)])

    def swap(x):
        return lax.ppermute(x, "cols", [(c, c ^ 1) for c in range(2 * planes)])

    def fetch(x, by, second):
        pairs = []
        for y in range(SIDE):
            for q in range(SIDE):
                for c in range(2, 2 * planes):
                    along_x = (c % 2 == 0) != second
                    sy, sx = (y, (q + by) % SIDE) if along_x else ((y + by) % SIDE, q)
                    pairs.append(((sy * SIDE + sx) * 2 * planes + c, (y * SIDE + q) * 2 * planes + c))
        return lax.ppermute(x, ("rows", "cols"), pairs)

    def hold(x, *deps):
        return pl.pallas_call(
            hold_kernel,
            in_specs=[ANY] * (1 + len(deps)),
            out_specs=ANY,
            out_shape=jax.ShapeDtypeStruct(x.shape, x.dtype),
            input_output_aliases={0: 0},
            cost_estimate=cost(5),
            name="hold",
        )(x, *deps)

    ft = factor_rows.transpose(1, 2, 0)
    groups = [[r * 2 * planes + 2 * z + k for k in range(2) for r in range(rows)] for z in range(planes)]

    def gather(x):
        everyone = lax.all_gather(x, ("rows", "cols"), axis=0, axis_index_groups=groups)
        return everyone.reshape(2, rows, *x.shape)

    diag = lax.dynamic_slice_in_dim(ft, per_plane * plane, per_plane - 1, 0)
    head = gather(jnp.concatenate([landmarks.T, diag.reshape(-1, own_rows)], axis=0))
    dt_own, dt_oth = diag_inverse, swap(diag_inverse)

    near = ft[:per_plane].reshape(-1, own_rows)
    line = jnp.stack([near] + [fetch(near, by, False) for by in range(1, SIDE)])
    up, down = fetch(line, 1, True), fetch(line, 3, True)
    turn = hold(info, line)
    mid = SIDE // 2
    far = [fetch(up[:mid], 1, True), fetch(down[mid:], 3, True)]
    own = [line, up, down]
    oth = [swap(x) for x in own]
    middle = turn = hold(turn, up, down)
    near = own + far + oth + [swap(x) for x in far]
    turn = hold(turn, *far)

    first = send(ft[per_plane:2 * per_plane], 3, 1)
    other = lax.dynamic_slice_in_dim(ft, per_plane * jnp.maximum(plane - 1, 0), per_plane, 0)
    factor = gather(
        pl.pallas_call(
            pick_kernel,
            in_specs=[SMEM, VMEM, VMEM],
            out_specs=VMEM,
            out_shape=jax.ShapeDtypeStruct((per_plane * slab, own_rows), BF),
            cost_estimate=cost(0),
            name="pick",
        )(middle, first.reshape(-1, own_rows), other.reshape(-1, own_rows))
    )

    chunk_f32 = jax.ShapeDtypeStruct((2, t, own_rows), F32)
    chunk_bf = jax.ShapeDtypeStruct((2, t, own_rows), BF)
    whole_bf = jax.ShapeDtypeStruct((2, half, own_rows), BF)
    diag_scratch = [
        pltpu.VMEM((2, rows, (per_plane - 1) * slab, own_rows), BF),
        pltpu.VMEM((2, 2, size, size), BF),
    ]
    factor_scratch = [
        pltpu.VMEM(chunk_f32.shape, F32),
        pltpu.VMEM((2, rows, per_plane * slab, own_rows), BF),
        pltpu.SemaphoreType.DMA((2 * per_plane + 2,)),
    ]
    r, f0 = [], []
    for q in range(n):
        out = pl.pallas_call(
            functools.partial(scores_kernel, scale, q * t),
            in_specs=[SMEM] + [ANY] * 4,
            out_specs=[VMEM] * 2,
            out_shape=[chunk_f32, chunk_bf],
            scratch_shapes=[pltpu.VMEM((t, depth), BF), pltpu.VMEM((2, rows, lead, own_rows), BF)]
            + diag_scratch
            + [pltpu.SemaphoreType.DMA((5,))],
            compiler_params=params(),
            cost_estimate=cost(5),
            name="scores",
        )(turn, after(embeddings, f0[-1]) if q else embeddings, dt_own, dt_oth, head)
        r.append(out[0])
        f0.append(out[1])
    f0_to_1 = [send(x, 0, 1) for x in f0]
    f0_to_3 = [send(x, 0, 3) for x in f0]
    f0_to_2 = [send(x, 3, 2) for x in f0_to_3]
    r[0] = hold(r[0], f0[-1])

    def finish(role, r, a, more=()):
        last = role == planes - 1
        rows_of = near if role == 1 else [factor]
        one = jax.ShapeDtypeStruct((t, own_rows), BF)
        return pl.pallas_call(
            functools.partial(finish_kernel, role),
            in_specs=[SMEM, ANY, VMEM] + [ANY] * (3 + len(rows_of)) + ([VMEM] + [ANY] * 3 if last else []),
            out_specs=[VMEM] * 2 if last else VMEM,
            out_shape=[one, one] if last else chunk_bf,
            scratch_shapes=([pltpu.VMEM(chunk_bf.shape, BF)] if last else [])
            + factor_scratch[:2]
            + diag_scratch
            + [factor_scratch[2], pltpu.SemaphoreType.DMA((2,))],
            compiler_params=params(),
            cost_estimate=cost(0.8),
            name=f"finish{role}",
        )(info, r, a, head, dt_own, dt_oth, *rows_of, *more)

    def partial(own):
        return pl.pallas_call(
            partial_kernel,
            in_specs=[SMEM, ANY, VMEM],
            out_specs=VMEM,
            out_shape=chunk_bf,
            scratch_shapes=factor_scratch,
            compiler_params=params(),
            cost_estimate=cost(0),
            name="partial",
        )(info, factor, own)

    def update(r, to_3, to_2):
        return pl.pallas_call(
            update_kernel,
            in_specs=[SMEM] + [ANY] * (3 + N_PIECES),
            out_specs=ANY,
            out_shape=chunk_f32,
            scratch_shapes=factor_scratch[:2]
            + [pltpu.VMEM(chunk_bf.shape, BF), factor_scratch[2], pltpu.SemaphoreType.DMA],
            compiler_params=params(),
            cost_estimate=cost(0),
            name="update",
        )(info, r, to_3, to_2, *near)

    f1, parts = [], []
    for q in range(n):
        f1.append(finish(1, r[q], after(f0_to_1[q], *f1)))
    f1_to_2 = [send(x, 1, 2) for x in f1]
    r2, f2 = [], []
    for q in range(n):
        r2.append(update(r[q], f0_to_3[q], after(f0_to_2[q], f1[-1], *f2)))
        f2.append(finish(2, r2[q], f1_to_2[q]))
    for i in range(n):
        parts.append(partial(after(f1[i], r2[1], *parts)))
    parts = [send(x, 1, 3) for x in parts]
    f2_to_3 = [send(x, 2, 3) for x in f2]
    done = []
    for q in range(n):
        a = after(f2_to_3[q], *[x[0] for x in done])
        done.append(finish(3, r2[q], a, (parts[q], f0[q], f1[q], f2[q])))
    keep = [x for x, _ in done]
    got = [swap(x) for _, x in done]
    return jnp.where(core == 0, jnp.concatenate(keep + got, axis=0), jnp.concatenate(got + keep, axis=0))


def solution(mesh):
    in_specs = (P("rows", None), P("cols", "rows"), P("cols", None, "rows"), P("cols", None, None))
    out_specs = P("rows", "cols")
    return jax.shard_map(
        per_device, mesh=mesh, in_specs=in_specs, out_specs=out_specs, check_vma=False
    )
```

profile of v0, /device:TPU:97, one launch (start us, length us, event | category | flops | bytes accessed | tf_op | source)
XLA Modules:
  0.0 221.2 jit_solution(17839763324855660417)
XLA Ops:
  6.5 1.0 constant_dynamic-slice_fusion.1
  7.6 1.7 pad_maximum_fusion.1
  9.3 4.6 %collective-permute-start = (bf16[128,1024]{1,0:T(8,128)(2,1)S(1)}, bf16[128,1024]{1,0:T(8,128)(2,1)S(1)}, u32[]{:S(2)}, u32[]{:S(2)}) collective-permute-start(bf16[128,1024]{1,0:T(8,128)(2,1)S(1)} %bitcast.35), channel_id=1, source_target_pairs={{10,2},{35,3},{12,4},{37,5},{14,6},{39,7},{18,10},{43,11},{20,12},... | collective-permute-start | bytes 786440 | tf_op jit(solution)/shard_map/ppermute | solution.py:255
  14.0 2.3 %collective-permute-start.1 = (bf16[128,1024]{1,0:T(8,128)(2,1)S(1)}, bf16[128,1024]{1,0:T(8,128)(2,1)S(1)}, u32[]{:S(2)}, u32[]{:S(2)}) collective-permute-start(bf16[128,1024]{1,0:T(8,128)(2,1)S(1)} %bitcast.36), channel_id=1, source_target_pairs={{18,2},{67,3},{20,4},{69,5},{22,6},{71,7},{26,10},{75,11},{28,12},... | collective-permute-start | bytes 786440 | tf_op jit(solution)/shard_map/ppermute | solution.py:255
  16.3 2.6 %collective-permute-start.2 = (bf16[128,1024]{1,0:T(8,128)(2,1)S(1)}, bf16[128,1024]{1,0:T(8,128)(2,1)S(1)}, u32[]{:S(2)}, u32[]{:S(2)}) collective-permute-start(bf16[128,1024]{1,0:T(8,128)(2,1)S(1)} %bitcast.37), channel_id=1, source_target_pairs={{26,2},{99,3},{28,4},{101,5},{30,6},{103,7},{2,10},{107,11},{4,12}... | collective-permute-start | bytes 786440 | tf_op jit(solution)/shard_map/ppermute | solution.py:255
  18.9 4.0 %collective-permute-done.1 = bf16[128,1024]{1,0:T(8,128)(2,1)S(1)} collective-permute-done((bf16[128,1024]{1,0:T(8,128)(2,1)S(1)}, bf16[128,1024]{1,0:T(8,128)(2,1)S(1)}, u32[]{:S(2)}, u32[]{:S(2)}) %collective-permute-start.1) | collective-permute-done | bytes 262176 | tf_op jit(solution)/shard_map/ppermute | solution.py:255
  22.9 3.6 %collective-permute-done.2 = bf16[128,1024]{1,0:T(8,128)(2,1)S(1)} collective-permute-done((bf16[128,1024]{1,0:T(8,128)(2,1)S(1)}, bf16[128,1024]{1,0:T(8,128)(2,1)S(1)}, u32[]{:S(2)}, u32[]{:S(2)}) %collective-permute-start.2) | collective-permute-done | bytes 262176 | tf_op jit(solution)/shard_map/ppermute | solution.py:255
  26.7 4.5 %collective-permute-start.3 = (bf16[4,128,1024]{2,1,0:T(8,128)(2,1)S(1)}, bf16[4,128,1024]{2,1,0:T(8,128)(2,1)S(1)}, u32[]{:S(2)}, u32[]{:S(2)}) collective-permute-start(bf16[4,128,1024]{2,1,0:T(8,128)(2,1)S(1)} %pad_maximum_fusion.refs_1_.refs_0_), channel_id=1, source_target_pairs={{34,2},{11,3},{36,4},{13,5},{38,6},{15,7},{42,10},{19,11},{44,12},... | collective-permute-start | bytes 3145736 | tf_op jit(solution)/shard_map/ppermute | solution.py:255
  31.2 1.9 collective-permute-start.4
  33.2 2.0 collective-permute-start.18
  35.3 0.6 copy.9.refs_0_
  35.9 0.7 constant_dynamic-slice_fusion
  36.6 7.6 %collective-permute-done.3.refs_1_ = bf16[4,128,1024]{2,1,0:T(8,128)(2,1)S(1)} collective-permute-done((bf16[4,128,1024]{2,1,0:T(8,128)(2,1)S(1)}, bf16[4,128,1024]{2,1,0:T(8,128)(2,1)S(1)}, u32[]{:S(2)}, u32[]{:S(2)}) %collective-permute-start.3) | collective-permute-done | bytes 1048608 | tf_op jit(solution)/shard_map/ppermute | solution.py:255
  44.2 6.6 %collective-permute-done.4.refs_2_ = bf16[4,128,1024]{2,1,0:T(8,128)(2,1)} collective-permute-done((bf16[4,128,1024]{2,1,0:T(8,128)(2,1)S(1)}, bf16[4,128,1024]{2,1,0:T(8,128)(2,1)}, u32[]{:S(2)}, u32[]{:S(2)}) %collective-permute-start.4) | collective-permute-done | bytes 1048608 | tf_op jit(solution)/shard_map/ppermute | solution.py:255
  50.8 1.9 pick.1
  52.7 14.6 %collective-permute-start.7 = (bf16[2,512,512]{2,1,0:T(8,128)(2,1)S(1)}, bf16[2,512,512]{2,1,0:T(8,128)(2,1)S(1)}, u32[]{:S(2)}, u32[]{:S(2)}) collective-permute-start(bf16[2,512,512]{2,1,0:T(8,128)(2,1)S(1)} %copy-done), channel_id=1, source_target_pairs={{0,1},{1,0},{2,3},{3,2},{4,5},{5,4},{6,7},{7,6},{8,9},{9,8},{10,11... | collective-permute-start | bytes 3145736 | tf_op jit(solution)/shard_map/ppermute | solution.py:245
  67.3 1.1 slice.17
  68.5 1.9 collective-permute-start.5
  70.4 1.1 slice.18
  71.5 3.4 %collective-permute-start.6 = (bf16[2,128,1024]{2,1,0:T(8,128)(2,1)S(1)}, bf16[2,128,1024]{2,1,0:T(8,128)(2,1)}, u32[]{:S(2)}, u32[]{:S(2)}) collective-permute-start(bf16[2,128,1024]{2,1,0:T(8,128)(2,1)S(1)} %slice.18), channel_id=1, source_target_pairs={{98,2},{27,3},{100,4},{29,5},{102,6},{31,7},{106,10},{3,11},{108,1... | collective-permute-start | bytes 1572872 | tf_op jit(solution)/shard_map/ppermute | solution.py:255
  74.9 0.6 collective-permute-start.12
  75.5 3.2 %collective-permute-done.5.refs_1_.refs_3_ = bf16[2,128,1024]{2,1,0:T(8,128)(2,1)} collective-permute-done((bf16[2,128,1024]{2,1,0:T(8,128)(2,1)S(1)}, bf16[2,128,1024]{2,1,0:T(8,128)(2,1)}, u32[]{:S(2)}, u32[]{:S(2)}) %collective-permute-start.5) | collective-permute-done | bytes 524320 | tf_op jit(solution)/shard_map/ppermute | solution.py:255
  78.8 0.8 collective-permute-start.14
  79.6 3.4 %collective-permute-done.6.refs_2_.refs_4_ = bf16[2,128,1024]{2,1,0:T(8,128)(2,1)} collective-permute-done((bf16[2,128,1024]{2,1,0:T(8,128)(2,1)S(1)}, bf16[2,128,1024]{2,1,0:T(8,128)(2,1)}, u32[]{:S(2)}, u32[]{:S(2)}) %collective-permute-start.6) | collective-permute-done | bytes 524320 | tf_op jit(solution)/shard_map/ppermute | solution.py:255
  83.0 1.0 copy-done.1
  84.0 5.1 %scores.2 = (f32[2,192,1024]{2,1,0:T(8,128)}, bf16[2,192,1024]{2,1,0:T(8,128)(2,1)}) custom-call(s32[4]{0:T(128)} %hold.6.info, bf16[768,1024]{1,0:T(8,128)(2,1)} %embeddings.2, bf16[2,512,512]{2,1,0:T(8,128)(2,1)} %dt_own.15, bf16[2,512,512]{2,1,0:T(8,128)(2,1)} %copy-done.1, bf16[2,16,160,1024]{3,2,1,0:T(8,128)(2,1)} %bitcast.20), custom_call_target="tpu_custom_call" | custom-call | flops 5000000000 | bytes 1024 | tf_op jit(solution)/shard_map/scores/pallas_call | solution.py:318
  89.1 0.7 collective-permute-start.11
  89.9 1.3 collective-permute-start.8
  91.2 5.2 %scores.3 = (f32[2,192,1024]{2,1,0:T(8,128)}, bf16[2,192,1024]{2,1,0:T(8,128)(2,1)}) custom-call(s32[4]{0:T(128)} %hold.6.info, bf16[768,1024]{1,0:T(8,128)(2,1)} %embeddings.2, bf16[2,512,512]{2,1,0:T(8,128)(2,1)} %dt_own.15, bf16[2,512,512]{2,1,0:T(8,128)(2,1)} %copy-done.1, bf16[2,16,160,1024]{3,2,1,0:T(8,128)(2,1)} %bitcast.21), custom_call_target="tpu_custom_call" | custom-call | flops 5000000000 | bytes 1024 | tf_op jit(solution)/shard_map/scores/pallas_call | solution.py:318
  96.3 1.6 collective-permute-start.10
  97.9 1.3 collective-permute-start.20
  99.2 0.9 collective-permute-start.15
  100.2 0.8 copy-done.16
  101.0 10.4 %collective-permute-done.8.to_3 = bf16[2,192,1024]{2,1,0:T(8,128)(2,1)S(1)} collective-permute-done((bf16[2,192,1024]{2,1,0:T(8,128)(2,1)}, bf16[2,192,1024]{2,1,0:T(8,128)(2,1)S(1)}, u32[]{:S(2)}, u32[]{:S(2)}) %collective-permute-start.8) | collective-permute-done | bytes 786464 | tf_op jit(solution)/shard_map/ppermute | solution.py:242
  111.4 1.3 collective-permute-start.9
  112.8 0.8 copy-done.5
  113.6 0.8 copy-done.6
  114.4 2.3 %finish1.2.own.refs_3_ = bf16[2,192,1024]{2,1,0:T(8,128)(2,1)} custom-call(s32[4]{0:T(128)} %copy-done.18, f32[2,192,1024]{2,1,0:T(8,128)} %hold.7.r, bf16[2,192,1024]{2,1,0:T(8,128)(2,1)} %copy-done.16, bf16[2,16,160,1024]{3,2,1,0:T(8,128)(2,1)} %bitcast.22, bf16[2,512,512]{2,1,0:T(8,128)(2,1)} %dt_own.15, bf16[2,512,512]{2,1,0:T(8,128)(2,1)} %copy-done.1, ...), custom_call_target="tpu_custom_call" | custom-call | flops 800000000 | bytes 1024 | tf_op jit(solution)/shard_map/finish1/pallas_call | solution.py:341
  116.7 1.6 collective-permute-start.17
  118.3 10.1 %collective-permute-done.20.to_3 = bf16[2,192,1024]{2,1,0:T(8,128)(2,1)S(1)} collective-permute-done((bf16[2,192,1024]{2,1,0:T(8,128)(2,1)}, bf16[2,192,1024]{2,1,0:T(8,128)(2,1)S(1)}, u32[]{:S(2)}, u32[]{:S(2)}) %collective-permute-start.20) | collective-permute-done | bytes 786464 | tf_op jit(solution)/shard_map/ppermute | solution.py:242
  128.4 1.3 collective-permute-start.21
  129.7 2.4 %finish1.3.own.refs_3_ = bf16[2,192,1024]{2,1,0:T(8,128)(2,1)} custom-call(s32[4]{0:T(128)} %copy-done.18, f32[2,192,1024]{2,1,0:T(8,128)} %get-tuple-element.24.r, bf16[2,192,1024]{2,1,0:T(8,128)(2,1)} %collective-permute-done.10.a, bf16[2,16,160,1024]{3,2,1,0:T(8,128)(2,1)} %bitcast.23, bf16[2,512,512]{2,1,0:T(8,128)(2,1)} %dt_own.15, ...), custom_call_target="tpu_custom_call" | custom-call | flops 800000000 | bytes 1024 | tf_op jit(solution)/shard_map/finish1/pallas_call | solution.py:341
  132.1 1.6 collective-permute-start.23
  133.7 0.9 copy-done.15
  134.6 8.1 %update.2.r = f32[2,192,1024]{2,1,0:T(8,128)} custom-call(s32[4]{0:T(128)} %copy-done.18, f32[2,192,1024]{2,1,0:T(8,128)} %hold.7.r, bf16[2,192,1024]{2,1,0:T(8,128)(2,1)} %copy-done.13, bf16[2,192,1024]{2,1,0:T(8,128)(2,1)} %copy-done.15, bf16[4,128,1024]{2,1,0:T(8,128)(2,1)} %copy-done.2, bf16[4,128,1024]{2,1,0:T(8,128)(2,1)} %copy-done.4, ...), custom_call_target="tpu_custom_call" | custom-call | bytes 1024 | tf_op jit(solution)/shard_map/update/pallas_call | solution.py:368
  142.7 2.2 finish2.2.refs_4_
  144.9 1.3 collective-permute-start.19
  146.2 0.9 copy-done.14
  147.1 8.0 %update.3.r = f32[2,192,1024]{2,1,0:T(8,128)} custom-call(s32[4]{0:T(128)} %copy-done.18, f32[2,192,1024]{2,1,0:T(8,128)} %get-tuple-element.24.r, bf16[2,192,1024]{2,1,0:T(8,128)(2,1)} %copy-done.12, bf16[2,192,1024]{2,1,0:T(8,128)(2,1)} %copy-done.14, bf16[4,128,1024]{2,1,0:T(8,128)(2,1)} %copy-done.2, bf16[4,128,1024]{2,1,0:T(8,128)(2,1)} %copy-done.4, ...), custom_call_target="tpu_custom_call" | custom-call | bytes 1024 | tf_op jit(solution)/shard_map/update/pallas_call | solution.py:368
  155.2 2.4 %partial.2 = bf16[2,192,1024]{2,1,0:T(8,128)(2,1)} custom-call(s32[4]{0:T(128)} %copy-done.18, bf16[2,16,128,1024]{3,2,1,0:T(8,128)(2,1)} %bitcast.29, bf16[2,192,1024]{2,1,0:T(8,128)(2,1)} %finish1.2.own.refs_3_), custom_call_target="tpu_custom_call" | custom-call | bytes 1024 | tf_op jit(solution)/shard_map/partial/pallas_call | solution.py:356
  157.5 1.3 collective-permute-start.22
  158.9 2.1 finish2.3.refs_4_
  161.0 1.3 collective-permute-start.24
  162.3 2.1 partial.3
  164.5 1.3 collective-permute-start.25
  166.3 12.3 %collective-permute-done.22.refs_1_ = bf16[2,192,1024]{2,1,0:T(8,128)(2,1)S(1)} collective-permute-done((bf16[2,192,1024]{2,1,0:T(8,128)(2,1)}, bf16[2,192,1024]{2,1,0:T(8,128)(2,1)S(1)}, u32[]{:S(2)}, u32[]{:S(2)}) %collective-permute-start.22) | collective-permute-done | bytes 786464 | tf_op jit(solution)/shard_map/ppermute | solution.py:242
  178.6 1.0 copy-done.11
  179.6 10.5 %finish3.2 = (bf16[192,1024]{1,0:T(8,128)(2,1)}, bf16[192,1024]{1,0:T(8,128)(2,1)}) custom-call(s32[4]{0:T(128)} %copy-done.18, f32[2,192,1024]{2,1,0:T(8,128)} %update.2.r, bf16[2,192,1024]{2,1,0:T(8,128)(2,1)} %copy-done.8, bf16[2,16,160,1024]{3,2,1,0:T(8,128)(2,1)} %bitcast.26, bf16[2,512,512]{2,1,0:T(8,128)(2,1)} %dt_own.15, ...), custom_call_target="tpu_custom_call" | custom-call | flops 800000000 | bytes 1024 | tf_op jit(solution)/shard_map/finish3/pallas_call | solution.py:341
  190.1 5.3 %collective-permute-done.25.refs_1_ = bf16[2,192,1024]{2,1,0:T(8,128)(2,1)S(1)} collective-permute-done((bf16[2,192,1024]{2,1,0:T(8,128)(2,1)}, bf16[2,192,1024]{2,1,0:T(8,128)(2,1)S(1)}, u32[]{:S(2)}, u32[]{:S(2)}) %collective-permute-start.25) | collective-permute-done | bytes 786464 | tf_op jit(solution)/shard_map/ppermute | solution.py:242
  195.4 0.9 copy-done.10
  196.3 10.8 %finish3.3 = (bf16[192,1024]{1,0:T(8,128)(2,1)}, bf16[192,1024]{1,0:T(8,128)(2,1)}) custom-call(s32[4]{0:T(128)} %copy-done.18, f32[2,192,1024]{2,1,0:T(8,128)} %update.3.r, bf16[2,192,1024]{2,1,0:T(8,128)(2,1)} %copy-done.9, bf16[2,16,160,1024]{3,2,1,0:T(8,128)(2,1)} %bitcast.27, bf16[2,512,512]{2,1,0:T(8,128)(2,1)} %dt_own.15, ...), custom_call_target="tpu_custom_call" | custom-call | flops 800000000 | bytes 1024 | tf_op jit(solution)/shard_map/finish3/pallas_call | solution.py:341
  207.2 2.6 %collective-permute-start.27 = (bf16[192,1024]{1,0:T(8,128)(2,1)}, bf16[192,1024]{1,0:T(8,128)(2,1)S(1)}, u32[]{:S(2)}, u32[]{:S(2)}) collective-permute-start(bf16[192,1024]{1,0:T(8,128)(2,1)} %get-tuple-element.34), channel_id=1, source_target_pairs={{0,1},{1,0},{2,3},{3,2},{4,5},{5,4},{6,7},{7,6},{8,9},{9,8},{10,11... | collective-permute-start | bytes 1179656 | tf_op jit(solution)/shard_map/ppermute | solution.py:245
  209.9 1.5 collective-permute-done.27
  211.7 2.6 %maximum_select_fusion = bf16[768,1024]{1,0:T(8,128)(2,1)} fusion(bf16[192,1024]{1,0:T(8,128)(2,1)S(1)} %collective-permute-done.27, bf16[192,1024]{1,0:T(8,128)(2,1)S(1)} %collective-permute-done.26, bf16[192,1024]{1,0:T(8,128)(2,1)} %get-tuple-element.32, bf16[192,1024]{1,0:T(8,128)(2,1)S(1)} %copy-done.17, pred[]{:T(512)S(6)} %eq.6), kind=kLoop, calls=%fused_computation | loop fusion | flops 13369344 | bytes 3145729 | tf_op jit(solution)/shard_map/jit(_where)/select_n | solution.py:398
  (65 shorter events, 1.7 us)
Async XLA Ops:
  6.5 2.8 %copy-start.7 = (bf16[1024,16,32]{0,2,1:T(8,128)(2,1)S(1)}, bf16[1024,16,32]{0,2,1:T(8,128)(2,1)}, u32[]{:S(2)}) copy-start(bf16[1024,16,32]{0,2,1:T(8,128)(2,1)} %param.6) | copy-start | bytes 3145732
  6.5 76.5 %all-gather.5.cloned.1.call-start = ((), (), s32[]{:S(2)}) async-start(), calls=%async_computation | async-start | bytes 10813440 | tf_op jit(solution)/shard_map/all_gather | solution.py:272
  9.2 133.4 %all-gather.7.cloned.1.call-start = ((), (), s32[]{:S(2)}) async-start(), calls=%async_computation.1 | async-start | bytes 8650752 | tf_op jit(solution)/shard_map/all_gather | solution.py:272
  9.3 9.5 %collective-permute-start = (bf16[128,1024]{1,0:T(8,128)(2,1)S(1)}, bf16[128,1024]{1,0:T(8,128)(2,1)S(1)}, u32[]{:S(2)}, u32[]{:S(2)}) collective-permute-start(bf16[128,1024]{1,0:T(8,128)(2,1)S(1)} %bitcast.35), channel_id=1, source_target_pairs={{10,2},{35,3},{12,4},{37,5},{14,6},{39,7},{18,10},{43,11},{20,12},... | collective-permute-start | bytes 786440 | tf_op jit(solution)/shard_map/ppermute | solution.py:255
  14.0 8.9 %collective-permute-start.1 = (bf16[128,1024]{1,0:T(8,128)(2,1)S(1)}, bf16[128,1024]{1,0:T(8,128)(2,1)S(1)}, u32[]{:S(2)}, u32[]{:S(2)}) collective-permute-start(bf16[128,1024]{1,0:T(8,128)(2,1)S(1)} %bitcast.36), channel_id=1, source_target_pairs={{18,2},{67,3},{20,4},{69,5},{22,6},{71,7},{26,10},{75,11},{28,12},... | collective-permute-start | bytes 786440 | tf_op jit(solution)/shard_map/ppermute | solution.py:255
  16.3 10.3 %collective-permute-start.2 = (bf16[128,1024]{1,0:T(8,128)(2,1)S(1)}, bf16[128,1024]{1,0:T(8,128)(2,1)S(1)}, u32[]{:S(2)}, u32[]{:S(2)}) collective-permute-start(bf16[128,1024]{1,0:T(8,128)(2,1)S(1)} %bitcast.37), channel_id=1, source_target_pairs={{26,2},{99,3},{28,4},{101,5},{30,6},{103,7},{2,10},{107,11},{4,12}... | collective-permute-start | bytes 786440 | tf_op jit(solution)/shard_map/ppermute | solution.py:255
  26.7 9.9 %copy-start.2 = (bf16[4,128,1024]{2,1,0:T(8,128)(2,1)}, bf16[4,128,1024]{2,1,0:T(8,128)(2,1)S(1)}, u32[]{:S(2)}) copy-start(bf16[4,128,1024]{2,1,0:T(8,128)(2,1)S(1)} %pad_maximum_fusion.refs_1_.refs_0_) | copy-start | bytes 3145732
  26.7 17.5 %collective-permute-start.3 = (bf16[4,128,1024]{2,1,0:T(8,128)(2,1)S(1)}, bf16[4,128,1024]{2,1,0:T(8,128)(2,1)S(1)}, u32[]{:S(2)}, u32[]{:S(2)}) collective-permute-start(bf16[4,128,1024]{2,1,0:T(8,128)(2,1)S(1)} %pad_maximum_fusion.refs_1_.refs_0_), channel_id=1, source_target_pairs={{34,2},{11,3},{36,4},{13,5},{38,6},{15,7},{42,10},{19,11},{44,12},... | collective-permute-start | bytes 3145736 | tf_op jit(solution)/shard_map/ppermute | solution.py:255
  31.2 19.5 %collective-permute-start.4 = (bf16[4,128,1024]{2,1,0:T(8,128)(2,1)S(1)}, bf16[4,128,1024]{2,1,0:T(8,128)(2,1)}, u32[]{:S(2)}, u32[]{:S(2)}) collective-permute-start(bf16[4,128,1024]{2,1,0:T(8,128)(2,1)S(1)} %pad_maximum_fusion.refs_1_.refs_0_), channel_id=1, source_target_pairs={{98,2},{27,3},{100,4},{29,5},{102,6},{31,7},{106,10},{3,11},{108,1... | collective-permute-start | bytes 3145736 | tf_op jit(solution)/shard_map/ppermute | solution.py:255
  33.2 17.6 %collective-permute-start.18 = (bf16[4,32,1024]{2,1,0:T(8,128)(2,1)S(1)}, bf16[4,32,1024]{2,1,0:T(8,128)(2,1)}, u32[]{:S(2)}, u32[]{:S(2)}) collective-permute-start(bf16[4,32,1024]{2,1,0:T(8,128)(2,1)S(1)} %get-tuple-element.35), channel_id=1, source_target_pairs={{6,2},{7,3},{14,10},{15,11},{22,18},{23,19},{30,26},{31,27},{38,34... | collective-permute-start | bytes 786440 | tf_op jit(solution)/shard_map/ppermute | solution.py:242
  35.3 1.3 copy-start.18
  36.6 16.1 %copy-start = (bf16[2,512,512]{2,1,0:T(8,128)(2,1)S(1)}, bf16[2,512,512]{2,1,0:T(8,128)(2,1)}, u32[]{:S(2)}) copy-start(bf16[2,512,512]{2,1,0:T(8,128)(2,1)} %dt_own.15) | copy-start | bytes 3145732
  44.2 6.6 %copy-start.4 = (bf16[4,128,1024]{2,1,0:T(8,128)(2,1)}, bf16[4,128,1024]{2,1,0:T(8,128)(2,1)S(1)}, u32[]{:S(2)}) copy-start(bf16[4,128,1024]{2,1,0:T(8,128)(2,1)S(1)} %collective-permute-done.3.refs_1_) | copy-start | bytes 3145732
  50.8 24.1 %copy-start.3 = (bf16[4,128,1024]{2,1,0:T(8,128)(2,1)S(1)}, bf16[4,128,1024]{2,1,0:T(8,128)(2,1)}, u32[]{:S(2)}) copy-start(bf16[4,128,1024]{2,1,0:T(8,128)(2,1)} %copy-done.2) | copy-start | bytes 3145732
  52.7 30.3 %collective-permute-start.7 = (bf16[2,512,512]{2,1,0:T(8,128)(2,1)S(1)}, bf16[2,512,512]{2,1,0:T(8,128)(2,1)S(1)}, u32[]{:S(2)}, u32[]{:S(2)}) collective-permute-start(bf16[2,512,512]{2,1,0:T(8,128)(2,1)S(1)} %copy-done), channel_id=1, source_target_pairs={{0,1},{1,0},{2,3},{3,2},{4,5},{5,4},{6,7},{7,6},{8,9},{9,8},{10,11... | collective-permute-start | bytes 3145736 | tf_op jit(solution)/shard_map/ppermute | solution.py:245
  68.5 10.3 %collective-permute-start.5 = (bf16[2,128,1024]{2,1,0:T(8,128)(2,1)S(1)}, bf16[2,128,1024]{2,1,0:T(8,128)(2,1)}, u32[]{:S(2)}, u32[]{:S(2)}) collective-permute-start(bf16[2,128,1024]{2,1,0:T(8,128)(2,1)S(1)} %slice.17), channel_id=1, source_target_pairs={{34,2},{11,3},{36,4},{13,5},{38,6},{15,7},{42,10},{19,11},{44,12},... | collective-permute-start | bytes 1572872 | tf_op jit(solution)/shard_map/ppermute | solution.py:255
  71.5 11.5 %collective-permute-start.6 = (bf16[2,128,1024]{2,1,0:T(8,128)(2,1)S(1)}, bf16[2,128,1024]{2,1,0:T(8,128)(2,1)}, u32[]{:S(2)}, u32[]{:S(2)}) collective-permute-start(bf16[2,128,1024]{2,1,0:T(8,128)(2,1)S(1)} %slice.18), channel_id=1, source_target_pairs={{98,2},{27,3},{100,4},{29,5},{102,6},{31,7},{106,10},{3,11},{108,1... | collective-permute-start | bytes 1572872 | tf_op jit(solution)/shard_map/ppermute | solution.py:255
  74.9 21.5 %collective-permute-start.12 = (bf16[4,128,1024]{2,1,0:T(8,128)(2,1)S(1)}, bf16[4,128,1024]{2,1,0:T(8,128)(2,1)}, u32[]{:S(2)}, u32[]{:S(2)}) collective-permute-start(bf16[4,128,1024]{2,1,0:T(8,128)(2,1)S(1)} %copy-done.3), channel_id=1, source_target_pairs={{0,1},{1,0},{2,3},{3,2},{4,5},{5,4},{6,7},{7,6},{8,9},{9,8},{10,11... | collective-permute-start | bytes 3145736 | tf_op jit(solution)/shard_map/ppermute | solution.py:245
  75.5 22.4 %collective-permute-start.13 = (bf16[4,128,1024]{2,1,0:T(8,128)(2,1)}, bf16[4,128,1024]{2,1,0:T(8,128)(2,1)}, u32[]{:S(2)}, u32[]{:S(2)}) collective-permute-start(bf16[4,128,1024]{2,1,0:T(8,128)(2,1)} %copy-done.4), channel_id=1, source_target_pairs={{0,1},{1,0},{2,3},{3,2},{4,5},{5,4},{6,7},{7,6},{8,9},{9,8},{10,11... | collective-permute-start | bytes 3145736 | tf_op jit(solution)/shard_map/ppermute | solution.py:245
  78.8 20.4 %collective-permute-start.14 = (bf16[4,128,1024]{2,1,0:T(8,128)(2,1)}, bf16[4,128,1024]{2,1,0:T(8,128)(2,1)}, u32[]{:S(2)}, u32[]{:S(2)}) collective-permute-start(bf16[4,128,1024]{2,1,0:T(8,128)(2,1)} %collective-permute-done.4.refs_2_), channel_id=1, source_target_pairs={{0,1},{1,0},{2,3},{3,2},{4,5},{5,4},{6,7},{7,6},{8,9},{9,8},{10,11... | collective-permute-start | bytes 3145736 | tf_op jit(solution)/shard_map/ppermute | solution.py:245
  83.0 1.0 copy-start.1
  89.1 11.0 %collective-permute-start.11 = (bf16[2,192,1024]{2,1,0:T(8,128)(2,1)}, bf16[2,192,1024]{2,1,0:T(8,128)(2,1)S(1)}, u32[]{:S(2)}, u32[]{:S(2)}) collective-permute-start(bf16[2,192,1024]{2,1,0:T(8,128)(2,1)} %get-tuple-element.21.refs_2_), channel_id=1, source_target_pairs={{0,2},{1,3},{8,10},{9,11},{16,18},{17,19},{24,26},{25,27},{32,34},... | collective-permute-start | bytes 2359304 | tf_op jit(solution)/shard_map/ppermute | solution.py:242
  89.9 21.5 %collective-permute-start.8 = (bf16[2,192,1024]{2,1,0:T(8,128)(2,1)}, bf16[2,192,1024]{2,1,0:T(8,128)(2,1)S(1)}, u32[]{:S(2)}, u32[]{:S(2)}) collective-permute-start(bf16[2,192,1024]{2,1,0:T(8,128)(2,1)} %get-tuple-element.21.refs_2_), channel_id=1, source_target_pairs={{0,6},{1,7},{8,14},{9,15},{16,22},{17,23},{24,30},{25,31},{32,38},... | collective-permute-start | bytes 2359304 | tf_op jit(solution)/shard_map/ppermute | solution.py:242
  96.3 21.9 %collective-permute-start.10 = (bf16[2,192,1024]{2,1,0:T(8,128)(2,1)}, bf16[2,192,1024]{2,1,0:T(8,128)(2,1)}, u32[]{:S(2)}, u32[]{:S(2)}) collective-permute-start(bf16[2,192,1024]{2,1,0:T(8,128)(2,1)} %get-tuple-element.23.refs_1_.refs_2_), channel_id=1, source_target_pairs={{0,2},{1,3},{8,10},{9,11},{16,18},{17,19},{24,26},{25,27},{32,34},... | collective-permute-start | bytes 2359304 | tf_op jit(solution)/shard_map/ppermute | solution.py:242
  97.9 30.5 %collective-permute-start.20 = (bf16[2,192,1024]{2,1,0:T(8,128)(2,1)}, bf16[2,192,1024]{2,1,0:T(8,128)(2,1)S(1)}, u32[]{:S(2)}, u32[]{:S(2)}) collective-permute-start(bf16[2,192,1024]{2,1,0:T(8,128)(2,1)} %get-tuple-element.23.refs_1_.refs_2_), channel_id=1, source_target_pairs={{0,6},{1,7},{8,14},{9,15},{16,22},{17,23},{24,30},{25,31},{32,38},... | collective-permute-start | bytes 2359304 | tf_op jit(solution)/shard_map/ppermute | solution.py:242
  99.2 13.6 %collective-permute-start.15 = (bf16[2,128,1024]{2,1,0:T(8,128)(2,1)}, bf16[2,128,1024]{2,1,0:T(8,128)(2,1)S(1)}, u32[]{:S(2)}, u32[]{:S(2)}) collective-permute-start(bf16[2,128,1024]{2,1,0:T(8,128)(2,1)} %collective-permute-done.5.refs_1_.refs_3_), channel_id=1, source_target_pairs={{0,1},{1,0},{2,3},{3,2},{4,5},{5,4},{6,7},{7,6},{8,9},{9,8},{10,11... | collective-permute-start | bytes 1572872 | tf_op jit(solution)/shard_map/ppermute | solution.py:245
  100.1 0.9 copy-start.16
  100.1 12.7 %collective-permute-start.16 = (bf16[2,128,1024]{2,1,0:T(8,128)(2,1)}, bf16[2,128,1024]{2,1,0:T(8,128)(2,1)S(1)}, u32[]{:S(2)}, u32[]{:S(2)}) collective-permute-start(bf16[2,128,1024]{2,1,0:T(8,128)(2,1)} %collective-permute-done.6.refs_2_.refs_4_), channel_id=1, source_target_pairs={{0,1},{1,0},{2,3},{3,2},{4,5},{5,4},{6,7},{7,6},{8,9},{9,8},{10,11... | collective-permute-start | bytes 1572872 | tf_op jit(solution)/shard_map/ppermute | solution.py:245
  111.4 5.3 %copy-start.13 = (bf16[2,192,1024]{2,1,0:T(8,128)(2,1)}, bf16[2,192,1024]{2,1,0:T(8,128)(2,1)S(1)}, u32[]{:S(2)}) copy-start(bf16[2,192,1024]{2,1,0:T(8,128)(2,1)S(1)} %collective-permute-done.8.to_3) | copy-start | bytes 2359300
  111.4 22.3 %collective-permute-start.9 = (bf16[2,192,1024]{2,1,0:T(8,128)(2,1)S(1)}, bf16[2,192,1024]{2,1,0:T(8,128)(2,1)S(1)}, u32[]{:S(2)}, u32[]{:S(2)}) collective-permute-start(bf16[2,192,1024]{2,1,0:T(8,128)(2,1)S(1)} %collective-permute-done.8.to_3), channel_id=1, source_target_pairs={{6,4},{7,5},{14,12},{15,13},{22,20},{23,21},{30,28},{31,29},{38,36... | collective-permute-start | bytes 2359304 | tf_op jit(solution)/shard_map/ppermute | solution.py:242
  112.8 0.8 copy-start.5
  113.6 0.8 copy-start.6
  116.7 26.0 %collective-permute-start.17 = (bf16[2,192,1024]{2,1,0:T(8,128)(2,1)}, bf16[2,192,1024]{2,1,0:T(8,128)(2,1)}, u32[]{:S(2)}, u32[]{:S(2)}) collective-permute-start(bf16[2,192,1024]{2,1,0:T(8,128)(2,1)} %finish1.2.own.refs_3_), channel_id=1, source_target_pairs={{2,4},{3,5},{10,12},{11,13},{18,20},{19,21},{26,28},{27,29},{34,36... | collective-permute-start | bytes 2359304 | tf_op jit(solution)/shard_map/ppermute | solution.py:242
  128.4 3.7 %copy-start.12 = (bf16[2,192,1024]{2,1,0:T(8,128)(2,1)}, bf16[2,192,1024]{2,1,0:T(8,128)(2,1)S(1)}, u32[]{:S(2)}) copy-start(bf16[2,192,1024]{2,1,0:T(8,128)(2,1)S(1)} %collective-permute-done.20.to_3) | copy-start | bytes 2359300
  128.4 17.8 %collective-permute-start.21 = (bf16[2,192,1024]{2,1,0:T(8,128)(2,1)S(1)}, bf16[2,192,1024]{2,1,0:T(8,128)(2,1)S(1)}, u32[]{:S(2)}, u32[]{:S(2)}) collective-permute-start(bf16[2,192,1024]{2,1,0:T(8,128)(2,1)S(1)} %collective-permute-done.20.to_3), channel_id=1, source_target_pairs={{6,4},{7,5},{14,12},{15,13},{22,20},{23,21},{30,28},{31,29},{38,36... | collective-permute-start | bytes 2359304 | tf_op jit(solution)/shard_map/ppermute | solution.py:242
  132.1 26.8 %collective-permute-start.23 = (bf16[2,192,1024]{2,1,0:T(8,128)(2,1)}, bf16[2,192,1024]{2,1,0:T(8,128)(2,1)}, u32[]{:S(2)}, u32[]{:S(2)}) collective-permute-start(bf16[2,192,1024]{2,1,0:T(8,128)(2,1)} %finish1.3.own.refs_3_), channel_id=1, source_target_pairs={{2,4},{3,5},{10,12},{11,13},{18,20},{19,21},{26,28},{27,29},{34,36... | collective-permute-start | bytes 2359304 | tf_op jit(solution)/shard_map/ppermute | solution.py:242
  133.7 0.9 copy-start.15
  144.9 21.4 %collective-permute-start.19 = (bf16[2,192,1024]{2,1,0:T(8,128)(2,1)}, bf16[2,192,1024]{2,1,0:T(8,128)(2,1)S(1)}, u32[]{:S(2)}, u32[]{:S(2)}) collective-permute-start(bf16[2,192,1024]{2,1,0:T(8,128)(2,1)} %finish2.2.refs_4_), channel_id=1, source_target_pairs={{4,6},{5,7},{12,14},{13,15},{20,22},{21,23},{28,30},{29,31},{36,38... | collective-permute-start | bytes 2359304 | tf_op jit(solution)/shard_map/ppermute | solution.py:242
  146.2 0.9 copy-start.14
  157.5 21.0 %collective-permute-start.22 = (bf16[2,192,1024]{2,1,0:T(8,128)(2,1)}, bf16[2,192,1024]{2,1,0:T(8,128)(2,1)S(1)}, u32[]{:S(2)}, u32[]{:S(2)}) collective-permute-start(bf16[2,192,1024]{2,1,0:T(8,128)(2,1)} %partial.2), channel_id=1, source_target_pairs={{2,6},{3,7},{10,14},{11,15},{18,22},{19,23},{26,30},{27,31},{34,38... | collective-permute-start | bytes 2359304 | tf_op jit(solution)/shard_map/ppermute | solution.py:242
  161.0 29.1 %collective-permute-start.24 = (bf16[2,192,1024]{2,1,0:T(8,128)(2,1)}, bf16[2,192,1024]{2,1,0:T(8,128)(2,1)S(1)}, u32[]{:S(2)}, u32[]{:S(2)}) collective-permute-start(bf16[2,192,1024]{2,1,0:T(8,128)(2,1)} %finish2.3.refs_4_), channel_id=1, source_target_pairs={{4,6},{5,7},{12,14},{13,15},{20,22},{21,23},{28,30},{29,31},{36,38... | collective-permute-start | bytes 2359304 | tf_op jit(solution)/shard_map/ppermute | solution.py:242
  164.5 31.0 %collective-permute-start.25 = (bf16[2,192,1024]{2,1,0:T(8,128)(2,1)}, bf16[2,192,1024]{2,1,0:T(8,128)(2,1)S(1)}, u32[]{:S(2)}, u32[]{:S(2)}) collective-permute-start(bf16[2,192,1024]{2,1,0:T(8,128)(2,1)} %partial.3), channel_id=1, source_target_pairs={{2,6},{3,7},{10,14},{11,15},{18,22},{19,23},{26,30},{27,31},{34,38... | collective-permute-start | bytes 2359304 | tf_op jit(solution)/shard_map/ppermute | solution.py:242
  166.3 12.3 %copy-start.8 = (bf16[2,192,1024]{2,1,0:T(8,128)(2,1)}, bf16[2,192,1024]{2,1,0:T(8,128)(2,1)S(1)}, u32[]{:S(2)}) copy-start(bf16[2,192,1024]{2,1,0:T(8,128)(2,1)S(1)} %collective-permute-done.19.a) | copy-start | bytes 2359300
  178.6 1.0 copy-start.11
  190.1 5.3 %copy-start.9 = (bf16[2,192,1024]{2,1,0:T(8,128)(2,1)}, bf16[2,192,1024]{2,1,0:T(8,128)(2,1)S(1)}, u32[]{:S(2)}) copy-start(bf16[2,192,1024]{2,1,0:T(8,128)(2,1)S(1)} %collective-permute-done.24.a) | copy-start | bytes 2359300
  190.1 19.6 %copy-start.19 = (bf16[192,1024]{1,0:T(8,128)(2,1)S(1)}, bf16[192,1024]{1,0:T(8,128)(2,1)}, u32[]{:S(2)}) copy-start(bf16[192,1024]{1,0:T(8,128)(2,1)} %get-tuple-element.33) | copy-start | bytes 1179652
  190.1 21.6 %copy-start.17 = (bf16[192,1024]{1,0:T(8,128)(2,1)S(1)}, bf16[192,1024]{1,0:T(8,128)(2,1)}, u32[]{:S(2)}) copy-start(bf16[192,1024]{1,0:T(8,128)(2,1)} %get-tuple-element.29) | copy-start | bytes 1179652
  195.4 0.9 copy-start.10
  207.2 4.2 %collective-permute-start.27 = (bf16[192,1024]{1,0:T(8,128)(2,1)}, bf16[192,1024]{1,0:T(8,128)(2,1)S(1)}, u32[]{:S(2)}, u32[]{:S(2)}) collective-permute-start(bf16[192,1024]{1,0:T(8,128)(2,1)} %get-tuple-element.34), channel_id=1, source_target_pairs={{0,1},{1,0},{2,3},{3,2},{4,5},{5,4},{6,7},{7,6},{8,9},{9,8},{10,11... | collective-permute-start | bytes 1179656 | tf_op jit(solution)/shard_map/ppermute | solution.py:245
  209.8 1.9 collective-permute-start.26
Sparse Core Ops, SparseCore 0:
  9.6 66.5 all-gather.4
  78.5 51.6 all-gather.6
where the time goes:
time: 222 us; the launch traced here: 221 us
  waiting for transfers between devices  69 us (31%)
  Pallas kernels  63.1 us (28%)
  starting transfers between devices  59 us (27%)
  between operations  13.9 us (6%)
  local copies, waits for them, and re-layouts  11.7 us (5%)
  other arithmetic  4.5 us (2%)
    ppermute x13, waiting for transfers between devices, send(): lax.ppermute(x, 'cols', [(2 * source + k, 2 * target + k) for k in range(...  38.6 us
    pallas_call x6, Pallas kernels, finish(): pl.pallas_call(functools.partial(finish_kernel, role), in_specs=[SMEM, AN...  30.3 us
    ppermute x7, waiting for transfers between devices, fetch(): return lax.ppermute(x, ('rows', 'cols'), pairs)  28.5 us
    ppermute x7, starting transfers between devices, fetch(): return lax.ppermute(x, ('rows', 'cols'), pairs)  21.2 us
    ppermute x8, starting transfers between devices, swap(): return lax.ppermute(x, 'cols', [(c, c ^ 1) for c in range(2 * planes)])  19.9 us
    ppermute x13, starting transfers between devices, send(): lax.ppermute(x, 'cols', [(2 * source + k, 2 * target + k) for k in range(...  17.8 us
    pallas_call x2, Pallas kernels, update(): pl.pallas_call(update_kernel, in_specs=[SMEM] + [ANY] * (3 + N_PIECES), o...  16.1 us
    pallas_call x2, Pallas kernels, per_device(): pl.pallas_call(functools.partial(scores_kernel, scale, q * t), in_specs=[...  10.3 us
  transfers between devices with their start and end apart: 30, of which 13 were waited for; matrix products, arithmetic and copies ran while one was open for 2% of the time, Pallas kernels for 24%

commit v1 on v0

--- a/solution.py
+++ b/solution.py
@@ -40,16 +40,23 @@
                 yield which * len(PIECES) + i, j, parity, ((y + dy) % SIDE) * SIDE + (x + dx) % SIDE
 
 
+def halves(info):
+    return enumerate((info[1], 1 - info[1]))
+
+
 def start_pieces(info, pieces, r, lv, acc, sems):
     blocks = lv.shape[2] // SLAB
+    for i, half in halves(info):
+        pltpu.make_async_copy(r.at[half], acc.at[half], sems.at[2 * blocks + i]).start()
     for i, d, parity, place in piece_places(info):
-        pltpu.make_async_copy(pieces[i].at[d], lv.at[parity, place], sems.at[parity]).start()
-    copies = [[] for _ in range(2 * blocks)]
-    for half in range(2):
-        copies[half * blocks].append(pltpu.make_async_copy(r.at[half], acc.at[half], sems.at[2 * blocks + half]))
-        copies[half * blocks][0].start()
-        copies[half * blocks].append(pltpu.make_async_copy(lv.at[half], lv.at[half], sems.at[half]))
-    return copies
+        pltpu.make_async_copy(pieces[i].at[d], lv.at[parity, place], sems.at[i // len(PIECES)]).start()
+
+    def wait(i, half, k):
+        if k == 0:
+            pltpu.make_async_copy(lv.at[half], lv.at[half], sems.at[i]).wait()
+            pltpu.make_async_copy(acc.at[half], acc.at[half], sems.at[2 * blocks + i]).wait()
+
+    return wait
 
 
 def start_diag(info, head, dt_own, dt_oth, gv, dv, sem):
@@ -118,32 +125,52 @@
         solve(out, gv, dv, f)
 
 
-def start_factor(factor, r, lv, acc, sems):
-    depth = lv.shape[2]
-    first = factor.shape[2] - depth
-    blocks = depth // SLAB
-    copies = []
-    for half in range(2):
+def start_factor(info, factor, r, lv, acc, sems):
+    blocks = lv.shape[2] // SLAB
+
+    def block(ref, half, k):
+        return ref.at[half, :, pl.ds(k * SLAB, SLAB)]
+
+    for i, half in halves(info):
         for k in range(blocks):
-            source = factor.at[half, :, pl.ds(first + k * SLAB, SLAB)]
-            target = lv.at[half, :, pl.ds(k * SLAB, SLAB)]
-            copies.append([pltpu.make_async_copy(source, target, sems.at[half * blocks + k])])
-            copies[-1][0].start()
+            pltpu.make_async_copy(block(factor, half, k), block(lv, half, k), sems.at[i * blocks + k]).start()
             if k == 0 and r is not None:
-                copies[-1].append(pltpu.make_async_copy(r.at[half], acc.at[half], sems.at[2 * blocks + half]))
-                copies[-1][1].start()
-    return copies
-
-
-def subtract(acc, a, lv, copies):
+                pltpu.make_async_copy(r.at[half], acc.at[half], sems.at[2 * blocks + i]).start()
+
+    def wait(i, half, k):
+        pltpu.make_async_copy(block(lv, half, k), block(lv, half, k), sems.at[i * blocks + k]).wait()
+        if k == 0 and r is not None:
+            pltpu.make_async_copy(acc.at[half], acc.at[half], sems.at[2 * blocks + i]).wait()
+
+    return wait
+
+
+def subtract(info, acc, a, lv, wait):
     size = lv.shape[1] * SLAB
-    blocks = lv.shape[2] // SLAB
-    for half in range(2):
-        for k in range(blocks):
-            for copy in copies[half * blocks + k]:
-                copy.wait()
+
+    def body(i, carry):
+        half = jnp.where(i == 0, info[1], 1 - info[1])
+        for k in range(lv.shape[2] // SLAB):
+            wait(i, half, k)
             left = a[k // 2, :, (k % 2) * size:(k % 2 + 1) * size]
-            acc[half] -= mm(left, lv[half, :, k * SLAB:(k + 1) * SLAB].reshape(size, -1))
+            acc[half] = acc[half] - mm(left, lv[half, :, k * SLAB:(k + 1) * SLAB].reshape(size, -1))
+        return carry
+
+    lax.fori_loop(0, 2, body, 0)
+
+
+def both_kernel(info, r, a, head, dt_own, dt_oth, factor, before, *refs):
+    pieces, (f, acc, lv, gv, dv, sems, sem, near, near_sems) = refs[:N_PIECES], refs[N_PIECES:]
+
+    @pl.when(info[0] == 2)
+    def _():
+        near_copies = start_pieces(info, pieces, r, near, acc, near_sems)
+        copies = start_factor(info, factor, None, lv, acc, sems)
+        start_diag(info, head, dt_own, dt_oth, gv, dv, sem)
+        subtract(info, acc, before, near, near_copies)
+        subtract(info, acc, a, lv, copies)
+        wait_diag(gv, dv, sem)
+        solve(acc, gv, dv, f)
 
 
 def finish_kernel(role, info, r, a, head, dt_own, dt_oth, *refs):
@@ -161,9 +188,9 @@
         if role == 1:
             copies = start_pieces(info, factor, r, lv, acc, sems)
         else:
-            copies = start_factor(factor[0], r, lv, acc, sems)
+            copies = start_factor(info, factor[0], r, lv, acc, sems)
         start_diag(info, head, dt_own, dt_oth, gv, dv, sem)
-        subtract(acc, a, lv, copies)
+        subtract(info, acc, a, lv, copies)
         if last:
             acc[...] += part[...].astype(F32)
         wait_diag(gv, dv, sem)
@@ -188,9 +215,9 @@
 def partial_kernel(info, factor, own, p, acc, lv, sems):
     @pl.when(info[0] == 1)
     def _():
-        copies = start_factor(factor, None, lv, acc, sems)
+        copies = start_factor(info, factor, None, lv, acc, sems)
         acc[...] = jnp.zeros_like(acc)
-        subtract(acc, own, lv, copies)
+        subtract(info, acc, own, lv, copies)
         p[...] = acc[...].astype(BF)
 
 
@@ -203,7 +230,7 @@
             pl.when(info[0] == plane)(lambda a=a: pltpu.make_async_copy(a, av, sem).start())
         copies = start_pieces(info, pieces, r, lv, acc, sems)
         pltpu.make_async_copy(to_2, av, sem).wait()
-        subtract(acc, av, lv, copies)
+        subtract(info, acc, av, lv, copies)
         out = pltpu.make_async_copy(acc, r_out, sem)
         out.start()
         out.wait()
@@ -352,6 +379,21 @@
             name=f"finish{role}",
         )(info, r, a, head, dt_own, dt_oth, *rows_of, *more)
 
+    def finish_both(r, a, before):
+        return pl.pallas_call(
+            both_kernel,
+            in_specs=[SMEM, ANY, VMEM] + [ANY] * 4 + [VMEM] + [ANY] * N_PIECES,
+            out_specs=VMEM,
+            out_shape=chunk_bf,
+            scratch_shapes=factor_scratch[:2]
+            + diag_scratch
+            + [factor_scratch[2], pltpu.SemaphoreType.DMA((2,))]
+            + factor_scratch[1:],
+            compiler_params=params(),
+            cost_estimate=cost(0.8),
+            name="both2",
+        )(info, r, a, head, dt_own, dt_oth, factor, before, *near)
+
     def partial(own):
         return pl.pallas_call(
             partial_kernel,
@@ -381,12 +423,12 @@
     for q in range(n):
         f1.append(finish(1, r[q], after(f0_to_1[q], *f1)))
     f1_to_2 = [send(x, 1, 2) for x in f1]
-    r2, f2 = [], []
-    for q in range(n):
-        r2.append(update(r[q], f0_to_3[q], after(f0_to_2[q], f1[-1], *f2)))
-        f2.append(finish(2, r2[q], f1_to_2[q]))
-    for i in range(n):
-        parts.append(partial(after(f1[i], r2[1], *parts)))
+    r2 = [update(r[0], f0_to_3[0], after(f0_to_2[0], f1[-1]))]
+    parts.append(partial(after(f1[0], r2[0])))
+    f2 = [finish(2, r2[0], f1_to_2[0])]
+    f2.append(finish_both(r[1], f1_to_2[1], after(f0_to_2[1], f2[0])))
+    parts.append(partial(after(f1[1], f2[1])))
+    r2.append(update(r[1], f0_to_3[1], after(f0_to_2[1], f2[1])))
     parts = [send(x, 1, 3) for x in parts]
     f2_to_3 = [send(x, 2, 3) for x in f2]
     done = []

time: 222 us -> 217 us (0.977)
  waiting for transfers between devices: 69 us -> 62.9 us
    ppermute x7, waiting for transfers between devices: 28.5 us -> 20.7 us  [fetch(): return lax.ppermute(x, ('rows', 'cols'), pairs)]
    ppermute x8, starting transfers between devices: 19.9 us -> 15.7 us  [swap(): return lax.ppermute(x, 'cols', [(c, c ^ 1) for c in range(2 * planes)])]
    pallas_call x0 -> x1, Pallas kernels: none -> 2.51 us  [finish_both(): pl.pallas_call(both_kernel, in_specs=[SMEM, ANY, VMEM] + [ANY] * 4 + [VME...]
    ppermute x7, starting transfers between devices: 21.2 us -> 23.7 us  [fetch(): return lax.ppermute(x, ('rows', 'cols'), pairs)]
    pallas_call x6 -> x5, Pallas kernels: 30.3 us -> 28 us  [finish(): pl.pallas_call(functools.partial(finish_kernel, role), in_specs=[SMEM, AN...]
    unnamed x41 -> x35, local copies, waits for them, and re-layouts: 7.67 us -> 6.79 us
  transfers between devices with their start and end apart: 30 -> 30, of which waited for: 13 -> 10; matrix products, arithmetic and copies ran while one was open for 2% -> 2% of each run, Pallas kernels for 24% -> 30%
where the time goes in v1:
time: 217 us; the launch traced here: 215 us
  Pallas kernels  63.5 us (29%)
  waiting for transfers between devices  62.9 us (29%)
  starting transfers between devices  59.2 us (27%)
  between operations  13.8 us (6%)
  local copies, waits for them, and re-layouts  10.8 us (5%)
  other arithmetic  4.5 us (2%)
    ppermute x13, waiting for transfers between devices, send(): lax.ppermute(x, 'cols', [(2 * source + k, 2 * target + k) for k in range(...  40.6 us
    pallas_call x5, Pallas kernels, finish(): pl.pallas_call(functools.partial(finish_kernel, role), in_specs=[SMEM, AN...  28 us
    ppermute x7, starting transfers between devices, fetch(): return lax.ppermute(x, ('rows', 'cols'), pairs)  23.7 us
    ppermute x7, waiting for transfers between devices, fetch(): return lax.ppermute(x, ('rows', 'cols'), pairs)  20.7 us
    ppermute x13, starting transfers between devices, send(): lax.ppermute(x, 'cols', [(2 * source + k, 2 * target + k) for k in range(...  19.7 us
    pallas_call x2, Pallas kernels, update(): pl.pallas_call(update_kernel, in_specs=[SMEM] + [ANY] * (3 + N_PIECES), o...  16.4 us
    ppermute x8, starting transfers between devices, swap(): return lax.ppermute(x, 'cols', [(c, c ^ 1) for c in range(2 * planes)])  15.7 us
    pallas_call x2, Pallas kernels, per_device(): pl.pallas_call(functools.partial(scores_kernel, scale, q * t), in_specs=[...  10.2 us
  transfers between devices with their start and end apart: 30, of which 10 were waited for; matrix products, arithmetic and copies ran while one was open for 2% of the time, Pallas kernels for 30%

profile of v1, /device:TPU:97, one launch (start us, length us, event | category | flops | bytes accessed | tf_op | source)
XLA Modules:
  0.0 214.7 jit_solution(18424966330814952215)
XLA Ops:
  6.5 1.0 constant_dynamic-slice_fusion.1
  7.6 1.7 pad_maximum_fusion.1
  9.3 3.2 %collective-permute-start.2 = (bf16[128,1024]{1,0:T(8,128)(2,1)S(1)}, bf16[128,1024]{1,0:T(8,128)(2,1)S(1)}, u32[]{:S(2)}, u32[]{:S(2)}) collective-permute-start(bf16[128,1024]{1,0:T(8,128)(2,1)S(1)} %bitcast.35), channel_id=1, source_target_pairs={{26,2},{99,3},{28,4},{101,5},{30,6},{103,7},{2,10},{107,11},{4,12}... | collective-permute-start | bytes 786440 | tf_op jit(solution)/shard_map/ppermute | solution.py:282
  12.6 4.5 %collective-permute-start.1 = (bf16[128,1024]{1,0:T(8,128)(2,1)S(1)}, bf16[128,1024]{1,0:T(8,128)(2,1)S(1)}, u32[]{:S(2)}, u32[]{:S(2)}) collective-permute-start(bf16[128,1024]{1,0:T(8,128)(2,1)S(1)} %bitcast.36), channel_id=1, source_target_pairs={{18,2},{67,3},{20,4},{69,5},{22,6},{71,7},{26,10},{75,11},{28,12},... | collective-permute-start | bytes 786440 | tf_op jit(solution)/shard_map/ppermute | solution.py:282
  17.1 3.0 %collective-permute-start = (bf16[128,1024]{1,0:T(8,128)(2,1)S(1)}, bf16[128,1024]{1,0:T(8,128)(2,1)S(1)}, u32[]{:S(2)}, u32[]{:S(2)}) collective-permute-start(bf16[128,1024]{1,0:T(8,128)(2,1)S(1)} %bitcast.37), channel_id=1, source_target_pairs={{10,2},{35,3},{12,4},{37,5},{14,6},{39,7},{18,10},{43,11},{20,12},... | collective-permute-start | bytes 786440 | tf_op jit(solution)/shard_map/ppermute | solution.py:282
  20.1 1.9 collective-permute-done.1
  22.0 3.2 %collective-permute-done = bf16[128,1024]{1,0:T(8,128)(2,1)S(1)} collective-permute-done((bf16[128,1024]{1,0:T(8,128)(2,1)S(1)}, bf16[128,1024]{1,0:T(8,128)(2,1)S(1)}, u32[]{:S(2)}, u32[]{:S(2)}) %collective-permute-start) | collective-permute-done | bytes 262176 | tf_op jit(solution)/shard_map/ppermute | solution.py:282
  25.3 0.1 pad_maximum_fusion.refs_1_.refs_0_
  25.4 3.2 %collective-permute-start.4 = (bf16[4,128,1024]{2,1,0:T(8,128)(2,1)S(1)}, bf16[4,128,1024]{2,1,0:T(8,128)(2,1)S(1)}, u32[]{:S(2)}, u32[]{:S(2)}) collective-permute-start(bf16[4,128,1024]{2,1,0:T(8,128)(2,1)S(1)} %pad_maximum_fusion.refs_1_.refs_0_), channel_id=1, source_target_pairs={{98,2},{27,3},{100,4},{29,5},{102,6},{31,7},{106,10},{3,11},{108,1... | collective-permute-start | bytes 3145736 | tf_op jit(solution)/shard_map/ppermute | solution.py:282
  28.6 3.3 %collective-permute-start.3 = (bf16[4,128,1024]{2,1,0:T(8,128)(2,1)S(1)}, bf16[4,128,1024]{2,1,0:T(8,128)(2,1)}, u32[]{:S(2)}, u32[]{:S(2)}) collective-permute-start(bf16[4,128,1024]{2,1,0:T(8,128)(2,1)S(1)} %pad_maximum_fusion.refs_1_.refs_0_), channel_id=1, source_target_pairs={{34,2},{11,3},{36,4},{13,5},{38,6},{15,7},{42,10},{19,11},{44,12},... | collective-permute-start | bytes 3145736 | tf_op jit(solution)/shard_map/ppermute | solution.py:282
  31.9 2.2 %collective-permute-start.18 = (bf16[4,32,1024]{2,1,0:T(8,128)(2,1)S(1)}, bf16[4,32,1024]{2,1,0:T(8,128)(2,1)}, u32[]{:S(2)}, u32[]{:S(2)}) collective-permute-start(bf16[4,32,1024]{2,1,0:T(8,128)(2,1)S(1)} %get-tuple-element.37), channel_id=1, source_target_pairs={{6,2},{7,3},{14,10},{15,11},{22,18},{23,19},{30,26},{31,27},{38,34... | collective-permute-start | bytes 786440 | tf_op jit(solution)/shard_map/ppermute | solution.py:269
  34.2 0.6 copy.9.refs_0_
  34.7 0.7 constant_dynamic-slice_fusion
  35.5 8.8 %collective-permute-done.4.refs_2_ = bf16[4,128,1024]{2,1,0:T(8,128)(2,1)S(1)} collective-permute-done((bf16[4,128,1024]{2,1,0:T(8,128)(2,1)S(1)}, bf16[4,128,1024]{2,1,0:T(8,128)(2,1)S(1)}, u32[]{:S(2)}, u32[]{:S(2)}) %collective-permute-start.4) | collective-permute-done | bytes 1048608 | tf_op jit(solution)/shard_map/ppermute | solution.py:282
  44.3 1.4 collective-permute-done.3.refs_1_
  45.7 1.9 pick.1
  47.6 10.5 %collective-permute-start.7 = (bf16[2,512,512]{2,1,0:T(8,128)(2,1)S(1)}, bf16[2,512,512]{2,1,0:T(8,128)(2,1)S(1)}, u32[]{:S(2)}, u32[]{:S(2)}) collective-permute-start(bf16[2,512,512]{2,1,0:T(8,128)(2,1)S(1)} %copy-done.2), channel_id=1, source_target_pairs={{0,1},{1,0},{2,3},{3,2},{4,5},{5,4},{6,7},{7,6},{8,9},{9,8},{10,11... | collective-permute-start | bytes 3145736 | tf_op jit(solution)/shard_map/ppermute | solution.py:272
  58.1 1.1 slice.18
  59.2 2.0 collective-permute-start.6
  61.2 1.1 slice.17
  62.3 4.5 %collective-permute-start.5 = (bf16[2,128,1024]{2,1,0:T(8,128)(2,1)S(1)}, bf16[2,128,1024]{2,1,0:T(8,128)(2,1)}, u32[]{:S(2)}, u32[]{:S(2)}) collective-permute-start(bf16[2,128,1024]{2,1,0:T(8,128)(2,1)S(1)} %slice.17), channel_id=1, source_target_pairs={{34,2},{11,3},{36,4},{13,5},{38,6},{15,7},{42,10},{19,11},{44,12},... | collective-permute-start | bytes 1572872 | tf_op jit(solution)/shard_map/ppermute | solution.py:282
  66.8 1.1 collective-permute-start.12
  68.0 5.3 %collective-permute-done.6.refs_2_.refs_4_ = bf16[2,128,1024]{2,1,0:T(8,128)(2,1)} collective-permute-done((bf16[2,128,1024]{2,1,0:T(8,128)(2,1)S(1)}, bf16[2,128,1024]{2,1,0:T(8,128)(2,1)}, u32[]{:S(2)}, u32[]{:S(2)}) %collective-permute-start.6) | collective-permute-done | bytes 524320 | tf_op jit(solution)/shard_map/ppermute | solution.py:282
  73.4 0.4 collective-permute-start.13
  73.8 1.0 copy-done.3
  74.8 5.1 %scores.2 = (f32[2,192,1024]{2,1,0:T(8,128)}, bf16[2,192,1024]{2,1,0:T(8,128)(2,1)}) custom-call(s32[4]{0:T(128)} %hold.6.info, bf16[768,1024]{1,0:T(8,128)(2,1)} %embeddings.2, bf16[2,512,512]{2,1,0:T(8,128)(2,1)} %dt_own.15, bf16[2,512,512]{2,1,0:T(8,128)(2,1)} %copy-done.3, bf16[2,16,160,1024]{3,2,1,0:T(8,128)(2,1)} %bitcast.20), custom_call_target="tpu_custom_call" | custom-call | flops 5000000000 | bytes 1024 | tf_op jit(solution)/shard_map/scores/pallas_call | solution.py:345
  79.9 1.6 collective-permute-start.11
  81.5 1.3 collective-permute-start.8
  82.8 5.1 %scores.3 = (f32[2,192,1024]{2,1,0:T(8,128)}, bf16[2,192,1024]{2,1,0:T(8,128)(2,1)}) custom-call(s32[4]{0:T(128)} %hold.6.info, bf16[768,1024]{1,0:T(8,128)(2,1)} %embeddings.2, bf16[2,512,512]{2,1,0:T(8,128)(2,1)} %dt_own.15, bf16[2,512,512]{2,1,0:T(8,128)(2,1)} %copy-done.3, bf16[2,16,160,1024]{3,2,1,0:T(8,128)(2,1)} %bitcast.21), custom_call_target="tpu_custom_call" | custom-call | flops 5000000000 | bytes 1024 | tf_op jit(solution)/shard_map/scores/pallas_call | solution.py:345
  87.9 1.5 collective-permute-start.10
  89.4 1.3 collective-permute-start.21
  90.7 1.9 collective-permute-start.16
  92.7 9.4 %collective-permute-done.8.to_3 = bf16[2,192,1024]{2,1,0:T(8,128)(2,1)S(1)} collective-permute-done((bf16[2,192,1024]{2,1,0:T(8,128)(2,1)}, bf16[2,192,1024]{2,1,0:T(8,128)(2,1)S(1)}, u32[]{:S(2)}, u32[]{:S(2)}) %collective-permute-start.8) | collective-permute-done | bytes 786464 | tf_op jit(solution)/shard_map/ppermute | solution.py:269
  102.1 2.2 %collective-permute-start.9 = (bf16[2,192,1024]{2,1,0:T(8,128)(2,1)S(1)}, bf16[2,192,1024]{2,1,0:T(8,128)(2,1)}, u32[]{:S(2)}, u32[]{:S(2)}) collective-permute-start(bf16[2,192,1024]{2,1,0:T(8,128)(2,1)S(1)} %collective-permute-done.8.to_3), channel_id=1, source_target_pairs={{6,4},{7,5},{14,12},{15,13},{22,20},{23,21},{30,28},{31,29},{38,36... | collective-permute-start | bytes 2359304 | tf_op jit(solution)/shard_map/ppermute | solution.py:269
  104.3 0.8 copy-done.5
  105.2 0.8 copy-done.6
  105.9 2.2 %finish1.2.own.refs_3_ = bf16[2,192,1024]{2,1,0:T(8,128)(2,1)} custom-call(s32[4]{0:T(128)} %copy-done.16, f32[2,192,1024]{2,1,0:T(8,128)} %hold.7.r, bf16[2,192,1024]{2,1,0:T(8,128)(2,1)} %collective-permute-done.11.a, bf16[2,16,160,1024]{3,2,1,0:T(8,128)(2,1)} %bitcast.22, bf16[2,512,512]{2,1,0:T(8,128)(2,1)} %dt_own.15, bf16[2,512,512]{2,1,0:T(8,128)(2,1)} %copy-done.3, ...), custom_call_target="tpu_custom_call" | custom-call | flops 800000000 | bytes 1024 | tf_op jit(solution)/shard_map/finish1/pallas_call | solution.py:368
  108.1 1.5 collective-permute-start.17
  109.7 9.4 %collective-permute-done.21.to_3 = bf16[2,192,1024]{2,1,0:T(8,128)(2,1)S(1)} collective-permute-done((bf16[2,192,1024]{2,1,0:T(8,128)(2,1)}, bf16[2,192,1024]{2,1,0:T(8,128)(2,1)S(1)}, u32[]{:S(2)}, u32[]{:S(2)}) %collective-permute-start.21) | collective-permute-done | bytes 786464 | tf_op jit(solution)/shard_map/ppermute | solution.py:269
  119.1 1.3 collective-permute-start.22
  120.4 2.4 %finish1.3.own.refs_3_ = bf16[2,192,1024]{2,1,0:T(8,128)(2,1)} custom-call(s32[4]{0:T(128)} %copy-done.16, f32[2,192,1024]{2,1,0:T(8,128)} %get-tuple-element.25.r, bf16[2,192,1024]{2,1,0:T(8,128)(2,1)} %collective-permute-done.10.a, bf16[2,16,160,1024]{3,2,1,0:T(8,128)(2,1)} %bitcast.23, bf16[2,512,512]{2,1,0:T(8,128)(2,1)} %dt_own.15, ...), custom_call_target="tpu_custom_call" | custom-call | flops 800000000 | bytes 1024 | tf_op jit(solution)/shard_map/finish1/pallas_call | solution.py:368
  122.8 1.6 collective-permute-start.23
  124.4 8.2 %update.2.r = f32[2,192,1024]{2,1,0:T(8,128)} custom-call(s32[4]{0:T(128)} %copy-done.16, f32[2,192,1024]{2,1,0:T(8,128)} %hold.7.r, bf16[2,192,1024]{2,1,0:T(8,128)(2,1)} %copy-done.14, bf16[2,192,1024]{2,1,0:T(8,128)(2,1)} %collective-permute-done.9.to_2, bf16[4,128,1024]{2,1,0:T(8,128)(2,1)} %copy-done, ...), custom_call_target="tpu_custom_call" | custom-call | bytes 1024 | tf_op jit(solution)/shard_map/update/pallas_call | solution.py:410
  132.6 2.2 %finish2.1.refs_4_ = bf16[2,192,1024]{2,1,0:T(8,128)(2,1)} custom-call(s32[4]{0:T(128)} %copy-done.16, f32[2,192,1024]{2,1,0:T(8,128)} %update.2.r, bf16[2,192,1024]{2,1,0:T(8,128)(2,1)} %collective-permute-done.17.a, bf16[2,16,160,1024]{3,2,1,0:T(8,128)(2,1)} %bitcast.24, bf16[2,512,512]{2,1,0:T(8,128)(2,1)} %dt_own.15, bf16[2,512,512]{2,1,0:T(8,128)(2,1)} %copy-done.3, ...), custom_call_target="tpu_custom_call" | custom-call | flops 800000000 | bytes 1024 | tf_op jit(solution)/shard_map/finish2/pallas_call | solution.py:368
  134.8 1.3 collective-permute-start.19
  136.1 2.4 %partial.2 = bf16[2,192,1024]{2,1,0:T(8,128)(2,1)} custom-call(s32[4]{0:T(128)} %copy-done.16, bf16[2,16,128,1024]{3,2,1,0:T(8,128)(2,1)} %bitcast.29, bf16[2,192,1024]{2,1,0:T(8,128)(2,1)} %finish1.2.own.refs_3_), custom_call_target="tpu_custom_call" | custom-call | bytes 1024 | tf_op jit(solution)/shard_map/partial/pallas_call | solution.py:398
  138.6 1.3 collective-permute-start.20
  139.9 2.5 %both2.1.refs_4_ = bf16[2,192,1024]{2,1,0:T(8,128)(2,1)} custom-call(s32[4]{0:T(128)} %copy-done.16, f32[2,192,1024]{2,1,0:T(8,128)} %get-tuple-element.25.r, bf16[2,192,1024]{2,1,0:T(8,128)(2,1)} %collective-permute-done.23.a, bf16[2,16,160,1024]{3,2,1,0:T(8,128)(2,1)} %bitcast.25, bf16[2,512,512]{2,1,0:T(8,128)(2,1)} %dt_own.15, ...), custom_call_target="tpu_custom_call" | custom-call | flops 800000000 | bytes 1024 | tf_op jit(solution)/shard_map/both2/pallas_call | solution.py:383
  142.4 1.3 collective-permute-start.24
  143.7 2.1 partial.3
  145.8 1.3 collective-permute-start.25
  147.1 8.2 %update.3.r = f32[2,192,1024]{2,1,0:T(8,128)} custom-call(s32[4]{0:T(128)} %copy-done.16, f32[2,192,1024]{2,1,0:T(8,128)} %get-tuple-element.25.r, bf16[2,192,1024]{2,1,0:T(8,128)(2,1)} %copy-done.13, bf16[2,192,1024]{2,1,0:T(8,128)(2,1)} %copy-done.7, bf16[4,128,1024]{2,1,0:T(8,128)(2,1)} %copy-done, bf16[4,128,1024]{2,1,0:T(8,128)(2,1)} %collective-permute-done.3.refs_1_, ...), custom_call_target="tpu_custom_call" | custom-call | bytes 1024 | tf_op jit(solution)/shard_map/update/pallas_call | solution.py:410
  155.3 12.2 %collective-permute-done.19.a = bf16[2,192,1024]{2,1,0:T(8,128)(2,1)S(1)} collective-permute-done((bf16[2,192,1024]{2,1,0:T(8,128)(2,1)}, bf16[2,192,1024]{2,1,0:T(8,128)(2,1)S(1)}, u32[]{:S(2)}, u32[]{:S(2)}) %collective-permute-start.19) | collective-permute-done | bytes 786464 | tf_op jit(solution)/shard_map/ppermute | solution.py:269
  167.5 0.9 copy-done.11
  168.4 0.9 copy-done.12
  169.3 10.6 %finish3.2 = (bf16[192,1024]{1,0:T(8,128)(2,1)}, bf16[192,1024]{1,0:T(8,128)(2,1)}) custom-call(s32[4]{0:T(128)} %copy-done.16, f32[2,192,1024]{2,1,0:T(8,128)} %update.2.r, bf16[2,192,1024]{2,1,0:T(8,128)(2,1)} %copy-done.11, bf16[2,16,160,1024]{3,2,1,0:T(8,128)(2,1)} %bitcast.26, bf16[2,512,512]{2,1,0:T(8,128)(2,1)} %dt_own.15, ...), custom_call_target="tpu_custom_call" | custom-call | flops 800000000 | bytes 1024 | tf_op jit(solution)/shard_map/finish3/pallas_call | solution.py:368
  179.9 0.7 collective-permute-start.26
  180.7 9.6 %collective-permute-done.24.a = bf16[2,192,1024]{2,1,0:T(8,128)(2,1)S(1)} collective-permute-done((bf16[2,192,1024]{2,1,0:T(8,128)(2,1)}, bf16[2,192,1024]{2,1,0:T(8,128)(2,1)S(1)}, u32[]{:S(2)}, u32[]{:S(2)}) %collective-permute-start.24) | collective-permute-done | bytes 786464 | tf_op jit(solution)/shard_map/ppermute | solution.py:269
  190.3 0.9 copy-done.9
  191.2 0.9 copy-done.10
  192.1 10.7 %finish3.3 = (bf16[192,1024]{1,0:T(8,128)(2,1)}, bf16[192,1024]{1,0:T(8,128)(2,1)}) custom-call(s32[4]{0:T(128)} %copy-done.16, f32[2,192,1024]{2,1,0:T(8,128)} %update.3.r, bf16[2,192,1024]{2,1,0:T(8,128)(2,1)} %copy-done.9, bf16[2,16,160,1024]{3,2,1,0:T(8,128)(2,1)} %bitcast.27, bf16[2,512,512]{2,1,0:T(8,128)(2,1)} %dt_own.15, ...), custom_call_target="tpu_custom_call" | custom-call | flops 800000000 | bytes 1024 | tf_op jit(solution)/shard_map/finish3/pallas_call | solution.py:368
  202.8 0.9 collective-permute-start.27
  203.7 1.6 collective-permute-done.27
  205.2 2.6 %maximum_select_fusion = bf16[768,1024]{1,0:T(8,128)(2,1)} fusion(bf16[192,1024]{1,0:T(8,128)(2,1)S(1)} %collective-permute-done.27, bf16[192,1024]{1,0:T(8,128)(2,1)S(1)} %collective-permute-done.26, bf16[192,1024]{1,0:T(8,128)(2,1)} %get-tuple-element.34, bf16[192,1024]{1,0:T(8,128)(2,1)S(1)} %copy-done.15, pred[]{:T(512)S(6)} %eq.6), kind=kLoop, calls=%fused_computation | loop fusion | flops 13369344 | bytes 3145729 | tf_op jit(solution)/shard_map/jit(_where)/select_n | solution.py:440
  (59 shorter events, 0.5 us)
Async XLA Ops:
  6.5 2.8 %copy-start.8 = (bf16[1024,16,32]{0,2,1:T(8,128)(2,1)S(1)}, bf16[1024,16,32]{0,2,1:T(8,128)(2,1)}, u32[]{:S(2)}) copy-start(bf16[1024,16,32]{0,2,1:T(8,128)(2,1)} %param.6) | copy-start | bytes 3145732
  6.5 67.3 %all-gather.5.cloned.1.call-start = ((), (), s32[]{:S(2)}) async-start(), calls=%async_computation | async-start | bytes 10813440 | tf_op jit(solution)/shard_map/all_gather | solution.py:299
  9.2 123.3 %all-gather.7.cloned.1.call-start = ((), (), s32[]{:S(2)}) async-start(), calls=%async_computation.1 | async-start | bytes 8650752 | tf_op jit(solution)/shard_map/all_gather | solution.py:299
  9.3 10.7 %collective-permute-start.2 = (bf16[128,1024]{1,0:T(8,128)(2,1)S(1)}, bf16[128,1024]{1,0:T(8,128)(2,1)S(1)}, u32[]{:S(2)}, u32[]{:S(2)}) collective-permute-start(bf16[128,1024]{1,0:T(8,128)(2,1)S(1)} %bitcast.35), channel_id=1, source_target_pairs={{26,2},{99,3},{28,4},{101,5},{30,6},{103,7},{2,10},{107,11},{4,12}... | collective-permute-start | bytes 786440 | tf_op jit(solution)/shard_map/ppermute | solution.py:282
  12.6 9.5 %collective-permute-start.1 = (bf16[128,1024]{1,0:T(8,128)(2,1)S(1)}, bf16[128,1024]{1,0:T(8,128)(2,1)S(1)}, u32[]{:S(2)}, u32[]{:S(2)}) collective-permute-start(bf16[128,1024]{1,0:T(8,128)(2,1)S(1)} %bitcast.36), channel_id=1, source_target_pairs={{18,2},{67,3},{20,4},{69,5},{22,6},{71,7},{26,10},{75,11},{28,12},... | collective-permute-start | bytes 786440 | tf_op jit(solution)/shard_map/ppermute | solution.py:282
  17.1 8.2 %collective-permute-start = (bf16[128,1024]{1,0:T(8,128)(2,1)S(1)}, bf16[128,1024]{1,0:T(8,128)(2,1)S(1)}, u32[]{:S(2)}, u32[]{:S(2)}) collective-permute-start(bf16[128,1024]{1,0:T(8,128)(2,1)S(1)} %bitcast.37), channel_id=1, source_target_pairs={{10,2},{35,3},{12,4},{37,5},{14,6},{39,7},{18,10},{43,11},{20,12},... | collective-permute-start | bytes 786440 | tf_op jit(solution)/shard_map/ppermute | solution.py:282
  25.4 10.1 %copy-start = (bf16[4,128,1024]{2,1,0:T(8,128)(2,1)}, bf16[4,128,1024]{2,1,0:T(8,128)(2,1)S(1)}, u32[]{:S(2)}) copy-start(bf16[4,128,1024]{2,1,0:T(8,128)(2,1)S(1)} %pad_maximum_fusion.refs_1_.refs_0_) | copy-start | bytes 3145732
  25.4 18.9 %collective-permute-start.4 = (bf16[4,128,1024]{2,1,0:T(8,128)(2,1)S(1)}, bf16[4,128,1024]{2,1,0:T(8,128)(2,1)S(1)}, u32[]{:S(2)}, u32[]{:S(2)}) collective-permute-start(bf16[4,128,1024]{2,1,0:T(8,128)(2,1)S(1)} %pad_maximum_fusion.refs_1_.refs_0_), channel_id=1, source_target_pairs={{98,2},{27,3},{100,4},{29,5},{102,6},{31,7},{106,10},{3,11},{108,1... | collective-permute-start | bytes 3145736 | tf_op jit(solution)/shard_map/ppermute | solution.py:282
  28.6 17.1 %collective-permute-start.3 = (bf16[4,128,1024]{2,1,0:T(8,128)(2,1)S(1)}, bf16[4,128,1024]{2,1,0:T(8,128)(2,1)}, u32[]{:S(2)}, u32[]{:S(2)}) collective-permute-start(bf16[4,128,1024]{2,1,0:T(8,128)(2,1)S(1)} %pad_maximum_fusion.refs_1_.refs_0_), channel_id=1, source_target_pairs={{34,2},{11,3},{36,4},{13,5},{38,6},{15,7},{42,10},{19,11},{44,12},... | collective-permute-start | bytes 3145736 | tf_op jit(solution)/shard_map/ppermute | solution.py:282
  31.9 13.8 %collective-permute-start.18 = (bf16[4,32,1024]{2,1,0:T(8,128)(2,1)S(1)}, bf16[4,32,1024]{2,1,0:T(8,128)(2,1)}, u32[]{:S(2)}, u32[]{:S(2)}) collective-permute-start(bf16[4,32,1024]{2,1,0:T(8,128)(2,1)S(1)} %get-tuple-element.37), channel_id=1, source_target_pairs={{6,2},{7,3},{14,10},{15,11},{22,18},{23,19},{30,26},{31,27},{38,34... | collective-permute-start | bytes 786440 | tf_op jit(solution)/shard_map/ppermute | solution.py:269
  34.2 1.3 copy-start.16
  35.5 12.1 %copy-start.2 = (bf16[2,512,512]{2,1,0:T(8,128)(2,1)S(1)}, bf16[2,512,512]{2,1,0:T(8,128)(2,1)}, u32[]{:S(2)}) copy-start(bf16[2,512,512]{2,1,0:T(8,128)(2,1)} %dt_own.15) | copy-start | bytes 3145732
  44.3 1.4 copy-start.4
  45.7 21.1 %copy-start.1 = (bf16[4,128,1024]{2,1,0:T(8,128)(2,1)S(1)}, bf16[4,128,1024]{2,1,0:T(8,128)(2,1)}, u32[]{:S(2)}) copy-start(bf16[4,128,1024]{2,1,0:T(8,128)(2,1)} %copy-done) | copy-start | bytes 3145732
  47.6 26.2 %collective-permute-start.7 = (bf16[2,512,512]{2,1,0:T(8,128)(2,1)S(1)}, bf16[2,512,512]{2,1,0:T(8,128)(2,1)S(1)}, u32[]{:S(2)}, u32[]{:S(2)}) collective-permute-start(bf16[2,512,512]{2,1,0:T(8,128)(2,1)S(1)} %copy-done.2), channel_id=1, source_target_pairs={{0,1},{1,0},{2,3},{3,2},{4,5},{5,4},{6,7},{7,6},{8,9},{9,8},{10,11... | collective-permute-start | bytes 3145736 | tf_op jit(solution)/shard_map/ppermute | solution.py:272
  59.2 14.1 %collective-permute-start.6 = (bf16[2,128,1024]{2,1,0:T(8,128)(2,1)S(1)}, bf16[2,128,1024]{2,1,0:T(8,128)(2,1)}, u32[]{:S(2)}, u32[]{:S(2)}) collective-permute-start(bf16[2,128,1024]{2,1,0:T(8,128)(2,1)S(1)} %slice.18), channel_id=1, source_target_pairs={{98,2},{27,3},{100,4},{29,5},{102,6},{31,7},{106,10},{3,11},{108,1... | collective-permute-start | bytes 1572872 | tf_op jit(solution)/shard_map/ppermute | solution.py:282
  62.3 11.5 %collective-permute-start.5 = (bf16[2,128,1024]{2,1,0:T(8,128)(2,1)S(1)}, bf16[2,128,1024]{2,1,0:T(8,128)(2,1)}, u32[]{:S(2)}, u32[]{:S(2)}) collective-permute-start(bf16[2,128,1024]{2,1,0:T(8,128)(2,1)S(1)} %slice.17), channel_id=1, source_target_pairs={{34,2},{11,3},{36,4},{13,5},{38,6},{15,7},{42,10},{19,11},{44,12},... | collective-permute-start | bytes 1572872 | tf_op jit(solution)/shard_map/ppermute | solution.py:282
  66.8 21.0 %collective-permute-start.12 = (bf16[4,128,1024]{2,1,0:T(8,128)(2,1)S(1)}, bf16[4,128,1024]{2,1,0:T(8,128)(2,1)}, u32[]{:S(2)}, u32[]{:S(2)}) collective-permute-start(bf16[4,128,1024]{2,1,0:T(8,128)(2,1)S(1)} %copy-done.1), channel_id=1, source_target_pairs={{0,1},{1,0},{2,3},{3,2},{4,5},{5,4},{6,7},{7,6},{8,9},{9,8},{10,11... | collective-permute-start | bytes 3145736 | tf_op jit(solution)/shard_map/ppermute | solution.py:272
  67.9 21.5 %collective-permute-start.14 = (bf16[4,128,1024]{2,1,0:T(8,128)(2,1)}, bf16[4,128,1024]{2,1,0:T(8,128)(2,1)}, u32[]{:S(2)}, u32[]{:S(2)}) collective-permute-start(bf16[4,128,1024]{2,1,0:T(8,128)(2,1)} %copy-done.4), channel_id=1, source_target_pairs={{0,1},{1,0},{2,3},{3,2},{4,5},{5,4},{6,7},{7,6},{8,9},{9,8},{10,11... | collective-permute-start | bytes 3145736 | tf_op jit(solution)/shard_map/ppermute | solution.py:272
  73.4 17.3 %collective-permute-start.13 = (bf16[4,128,1024]{2,1,0:T(8,128)(2,1)}, bf16[4,128,1024]{2,1,0:T(8,128)(2,1)}, u32[]{:S(2)}, u32[]{:S(2)}) collective-permute-start(bf16[4,128,1024]{2,1,0:T(8,128)(2,1)} %collective-permute-done.3.refs_1_), channel_id=1, source_target_pairs={{0,1},{1,0},{2,3},{3,2},{4,5},{5,4},{6,7},{7,6},{8,9},{9,8},{10,11... | collective-permute-start | bytes 3145736 | tf_op jit(solution)/shard_map/ppermute | solution.py:272
  73.8 1.0 copy-start.3
  79.9 12.7 %collective-permute-start.11 = (bf16[2,192,1024]{2,1,0:T(8,128)(2,1)}, bf16[2,192,1024]{2,1,0:T(8,128)(2,1)}, u32[]{:S(2)}, u32[]{:S(2)}) collective-permute-start(bf16[2,192,1024]{2,1,0:T(8,128)(2,1)} %get-tuple-element.22.refs_2_), channel_id=1, source_target_pairs={{0,2},{1,3},{8,10},{9,11},{16,18},{17,19},{24,26},{25,27},{32,34},... | collective-permute-start | bytes 2359304 | tf_op jit(solution)/shard_map/ppermute | solution.py:269
  81.5 20.7 %collective-permute-start.8 = (bf16[2,192,1024]{2,1,0:T(8,128)(2,1)}, bf16[2,192,1024]{2,1,0:T(8,128)(2,1)S(1)}, u32[]{:S(2)}, u32[]{:S(2)}) collective-permute-start(bf16[2,192,1024]{2,1,0:T(8,128)(2,1)} %get-tuple-element.22.refs_2_), channel_id=1, source_target_pairs={{0,6},{1,7},{8,14},{9,15},{16,22},{17,23},{24,30},{25,31},{32,38},... | collective-permute-start | bytes 2359304 | tf_op jit(solution)/shard_map/ppermute | solution.py:269
  87.9 21.8 %collective-permute-start.10 = (bf16[2,192,1024]{2,1,0:T(8,128)(2,1)}, bf16[2,192,1024]{2,1,0:T(8,128)(2,1)}, u32[]{:S(2)}, u32[]{:S(2)}) collective-permute-start(bf16[2,192,1024]{2,1,0:T(8,128)(2,1)} %get-tuple-element.24.refs_1_.refs_2_), channel_id=1, source_target_pairs={{0,2},{1,3},{8,10},{9,11},{16,18},{17,19},{24,26},{25,27},{32,34},... | collective-permute-start | bytes 2359304 | tf_op jit(solution)/shard_map/ppermute | solution.py:269
  89.4 29.7 %collective-permute-start.21 = (bf16[2,192,1024]{2,1,0:T(8,128)(2,1)}, bf16[2,192,1024]{2,1,0:T(8,128)(2,1)S(1)}, u32[]{:S(2)}, u32[]{:S(2)}) collective-permute-start(bf16[2,192,1024]{2,1,0:T(8,128)(2,1)} %get-tuple-element.24.refs_1_.refs_2_), channel_id=1, source_target_pairs={{0,6},{1,7},{8,14},{9,15},{16,22},{17,23},{24,30},{25,31},{32,38},... | collective-permute-start | bytes 2359304 | tf_op jit(solution)/shard_map/ppermute | solution.py:269
  90.7 13.6 %collective-permute-start.16 = (bf16[2,128,1024]{2,1,0:T(8,128)(2,1)}, bf16[2,128,1024]{2,1,0:T(8,128)(2,1)S(1)}, u32[]{:S(2)}, u32[]{:S(2)}) collective-permute-start(bf16[2,128,1024]{2,1,0:T(8,128)(2,1)} %collective-permute-done.6.refs_2_.refs_4_), channel_id=1, source_target_pairs={{0,1},{1,0},{2,3},{3,2},{4,5},{5,4},{6,7},{7,6},{8,9},{9,8},{10,11... | collective-permute-start | bytes 1572872 | tf_op jit(solution)/shard_map/ppermute | solution.py:272
  92.6 11.7 %collective-permute-start.15 = (bf16[2,128,1024]{2,1,0:T(8,128)(2,1)}, bf16[2,128,1024]{2,1,0:T(8,128)(2,1)S(1)}, u32[]{:S(2)}, u32[]{:S(2)}) collective-permute-start(bf16[2,128,1024]{2,1,0:T(8,128)(2,1)} %collective-permute-done.5.refs_1_.refs_3_), channel_id=1, source_target_pairs={{0,1},{1,0},{2,3},{3,2},{4,5},{5,4},{6,7},{7,6},{8,9},{9,8},{10,11... | collective-permute-start | bytes 1572872 | tf_op jit(solution)/shard_map/ppermute | solution.py:272
  102.1 6.0 %copy-start.14 = (bf16[2,192,1024]{2,1,0:T(8,128)(2,1)}, bf16[2,192,1024]{2,1,0:T(8,128)(2,1)S(1)}, u32[]{:S(2)}) copy-start(bf16[2,192,1024]{2,1,0:T(8,128)(2,1)S(1)} %collective-permute-done.8.to_3) | copy-start | bytes 2359300
  102.1 22.3 %collective-permute-start.9 = (bf16[2,192,1024]{2,1,0:T(8,128)(2,1)S(1)}, bf16[2,192,1024]{2,1,0:T(8,128)(2,1)}, u32[]{:S(2)}, u32[]{:S(2)}) collective-permute-start(bf16[2,192,1024]{2,1,0:T(8,128)(2,1)S(1)} %collective-permute-done.8.to_3), channel_id=1, source_target_pairs={{6,4},{7,5},{14,12},{15,13},{22,20},{23,21},{30,28},{31,29},{38,36... | collective-permute-start | bytes 2359304 | tf_op jit(solution)/shard_map/ppermute | solution.py:269
  104.3 0.8 copy-start.5
  105.2 0.8 copy-start.6
  108.1 24.5 %collective-permute-start.17 = (bf16[2,192,1024]{2,1,0:T(8,128)(2,1)}, bf16[2,192,1024]{2,1,0:T(8,128)(2,1)}, u32[]{:S(2)}, u32[]{:S(2)}) collective-permute-start(bf16[2,192,1024]{2,1,0:T(8,128)(2,1)} %finish1.2.own.refs_3_), channel_id=1, source_target_pairs={{2,4},{3,5},{10,12},{11,13},{18,20},{19,21},{26,28},{27,29},{34,36... | collective-permute-start | bytes 2359304 | tf_op jit(solution)/shard_map/ppermute | solution.py:269
  119.1 3.7 %copy-start.13 = (bf16[2,192,1024]{2,1,0:T(8,128)(2,1)}, bf16[2,192,1024]{2,1,0:T(8,128)(2,1)S(1)}, u32[]{:S(2)}) copy-start(bf16[2,192,1024]{2,1,0:T(8,128)(2,1)S(1)} %collective-permute-done.21.to_3) | copy-start | bytes 2359300
  119.1 17.0 %collective-permute-start.22 = (bf16[2,192,1024]{2,1,0:T(8,128)(2,1)S(1)}, bf16[2,192,1024]{2,1,0:T(8,128)(2,1)S(1)}, u32[]{:S(2)}, u32[]{:S(2)}) collective-permute-start(bf16[2,192,1024]{2,1,0:T(8,128)(2,1)S(1)} %collective-permute-done.21.to_3), channel_id=1, source_target_pairs={{6,4},{7,5},{14,12},{15,13},{22,20},{23,21},{30,28},{31,29},{38,36... | collective-permute-start | bytes 2359304 | tf_op jit(solution)/shard_map/ppermute | solution.py:269
  122.8 17.1 %collective-permute-start.23 = (bf16[2,192,1024]{2,1,0:T(8,128)(2,1)}, bf16[2,192,1024]{2,1,0:T(8,128)(2,1)}, u32[]{:S(2)}, u32[]{:S(2)}) collective-permute-start(bf16[2,192,1024]{2,1,0:T(8,128)(2,1)} %finish1.3.own.refs_3_), channel_id=1, source_target_pairs={{2,4},{3,5},{10,12},{11,13},{18,20},{19,21},{26,28},{27,29},{34,36... | collective-permute-start | bytes 2359304 | tf_op jit(solution)/shard_map/ppermute | solution.py:269
  134.8 32.7 %collective-permute-start.19 = (bf16[2,192,1024]{2,1,0:T(8,128)(2,1)}, bf16[2,192,1024]{2,1,0:T(8,128)(2,1)S(1)}, u32[]{:S(2)}, u32[]{:S(2)}) collective-permute-start(bf16[2,192,1024]{2,1,0:T(8,128)(2,1)} %finish2.1.refs_4_), channel_id=1, source_target_pairs={{4,6},{5,7},{12,14},{13,15},{20,22},{21,23},{28,30},{29,31},{36,38... | collective-permute-start | bytes 2359304 | tf_op jit(solution)/shard_map/ppermute | solution.py:269
  136.1 2.4 %copy-start.7 = (bf16[2,192,1024]{2,1,0:T(8,128)(2,1)}, bf16[2,192,1024]{2,1,0:T(8,128)(2,1)S(1)}, u32[]{:S(2)}) copy-start(bf16[2,192,1024]{2,1,0:T(8,128)(2,1)S(1)} %collective-permute-done.22.before.to_2) | copy-start | bytes 2359300
  138.6 28.9 %collective-permute-start.20 = (bf16[2,192,1024]{2,1,0:T(8,128)(2,1)}, bf16[2,192,1024]{2,1,0:T(8,128)(2,1)S(1)}, u32[]{:S(2)}, u32[]{:S(2)}) collective-permute-start(bf16[2,192,1024]{2,1,0:T(8,128)(2,1)} %partial.2), channel_id=1, source_target_pairs={{2,6},{3,7},{10,14},{11,15},{18,22},{19,23},{26,30},{27,31},{34,38... | collective-permute-start | bytes 2359304 | tf_op jit(solution)/shard_map/ppermute | solution.py:269
  142.4 47.9 %collective-permute-start.24 = (bf16[2,192,1024]{2,1,0:T(8,128)(2,1)}, bf16[2,192,1024]{2,1,0:T(8,128)(2,1)S(1)}, u32[]{:S(2)}, u32[]{:S(2)}) collective-permute-start(bf16[2,192,1024]{2,1,0:T(8,128)(2,1)} %both2.1.refs_4_), channel_id=1, source_target_pairs={{4,6},{5,7},{12,14},{13,15},{20,22},{21,23},{28,30},{29,31},{36,38... | collective-permute-start | bytes 2359304 | tf_op jit(solution)/shard_map/ppermute | solution.py:269
  145.8 44.5 %collective-permute-start.25 = (bf16[2,192,1024]{2,1,0:T(8,128)(2,1)}, bf16[2,192,1024]{2,1,0:T(8,128)(2,1)S(1)}, u32[]{:S(2)}, u32[]{:S(2)}) collective-permute-start(bf16[2,192,1024]{2,1,0:T(8,128)(2,1)} %partial.3), channel_id=1, source_target_pairs={{2,6},{3,7},{10,14},{11,15},{18,22},{19,23},{26,30},{27,31},{34,38... | collective-permute-start | bytes 2359304 | tf_op jit(solution)/shard_map/ppermute | solution.py:269
  167.5 0.9 copy-start.11
  168.4 0.9 copy-start.12
  179.9 23.7 %collective-permute-start.26 = (bf16[192,1024]{1,0:T(8,128)(2,1)}, bf16[192,1024]{1,0:T(8,128)(2,1)S(1)}, u32[]{:S(2)}, u32[]{:S(2)}) collective-permute-start(bf16[192,1024]{1,0:T(8,128)(2,1)} %get-tuple-element.35), channel_id=1, source_target_pairs={{0,1},{1,0},{2,3},{3,2},{4,5},{5,4},{6,7},{7,6},{8,9},{9,8},{10,11... | collective-permute-start | bytes 1179656 | tf_op jit(solution)/shard_map/ppermute | solution.py:272
  190.3 0.9 copy-start.9
  190.3 14.9 %copy-start.15 = (bf16[192,1024]{1,0:T(8,128)(2,1)S(1)}, bf16[192,1024]{1,0:T(8,128)(2,1)}, u32[]{:S(2)}) copy-start(bf16[192,1024]{1,0:T(8,128)(2,1)} %get-tuple-element.29) | copy-start | bytes 1179652
  191.2 0.9 copy-start.10
  202.8 2.5 %collective-permute-start.27 = (bf16[192,1024]{1,0:T(8,128)(2,1)}, bf16[192,1024]{1,0:T(8,128)(2,1)S(1)}, u32[]{:S(2)}, u32[]{:S(2)}) collective-permute-start(bf16[192,1024]{1,0:T(8,128)(2,1)} %get-tuple-element.36), channel_id=1, source_target_pairs={{0,1},{1,0},{2,3},{3,2},{4,5},{5,4},{6,7},{7,6},{8,9},{9,8},{10,11... | collective-permute-start | bytes 1179656 | tf_op jit(solution)/shard_map/ppermute | solution.py:272
Sparse Core Ops, SparseCore 0:
  9.6 63.1 all-gather.4
  75.1 53.9 all-gather.6

commit v2 on v1

--- a/solution.py
+++ b/solution.py
@@ -178,7 +178,7 @@
     n_factor = N_PIECES if role == 1 else 1
     factor, refs = refs[:n_factor], refs[n_factor:]
     if last:
-        part, earlier, (keep, give, f, acc, lv, gv, dv, sems, sem) = refs[0], refs[1:SIDE], refs[SIDE:]
+        part, earlier, (keep, give, f, acc, lv, gv, dv, sems, sem, pv, part_sem) = refs[0], refs[1:SIDE], refs[SIDE:]
     else:
         f, acc, lv, gv, dv, sems, sem = refs
     plane, core = info[0], info[1]
@@ -189,10 +189,14 @@
             copies = start_pieces(info, factor, r, lv, acc, sems)
         else:
             copies = start_factor(info, factor[0], r, lv, acc, sems)
+        if last:
+            cp = pltpu.make_async_copy(part, pv, part_sem)
+            cp.start()
         start_diag(info, head, dt_own, dt_oth, gv, dv, sem)
         subtract(info, acc, a, lv, copies)
         if last:
-            acc[...] += part[...].astype(F32)
+            cp.wait()
+            acc[...] += pv[...].astype(F32)
         wait_diag(gv, dv, sem)
         solve(acc, gv, dv, f)
         if last:
@@ -240,7 +244,7 @@
     return lax.dot_general(a, b, (((1,), (1,)), ((), ())), preferred_element_type=F32)
 
 
-def params(mib=60):
+def params(mib=48):
     return pltpu.CompilerParams(vmem_limit_bytes=mib << 20)
 
 
@@ -312,7 +316,8 @@
     own = [line, up, down]
     oth = [swap(x) for x in own]
     middle = turn = hold(turn, up, down)
-    near = own + far + oth + [swap(x) for x in far]
+    far_oth = [swap(x) for x in far]
+    near = own + far + oth + far_oth
     turn = hold(turn, *far)
 
     first = send(ft[per_plane:2 * per_plane], 3, 1)
@@ -353,7 +358,7 @@
             compiler_params=params(),
             cost_estimate=cost(5),
             name="scores",
-        )(turn, after(embeddings, f0[-1]) if q else embeddings, dt_own, dt_oth, head)
+        )(turn, after(embeddings, f0[-1], *far_oth) if q else embeddings, dt_own, dt_oth, head)
         r.append(out[0])
         f0.append(out[1])
     f0_to_1 = [send(x, 0, 1) for x in f0]
@@ -367,13 +372,14 @@
         one = jax.ShapeDtypeStruct((t, own_rows), BF)
         return pl.pallas_call(
             functools.partial(finish_kernel, role),
-            in_specs=[SMEM, ANY, VMEM] + [ANY] * (3 + len(rows_of)) + ([VMEM] + [ANY] * 3 if last else []),
+            in_specs=[SMEM, ANY, VMEM] + [ANY] * (3 + len(rows_of)) + ([ANY] * 4 if last else []),
             out_specs=[VMEM] * 2 if last else VMEM,
             out_shape=[one, one] if last else chunk_bf,
             scratch_shapes=([pltpu.VMEM(chunk_bf.shape, BF)] if last else [])
             + factor_scratch[:2]
             + diag_scratch
-            + [factor_scratch[2], pltpu.SemaphoreType.DMA((2,))],
+            + [factor_scratch[2], pltpu.SemaphoreType.DMA((2,))]
+            + ([pltpu.VMEM(chunk_bf.shape, BF), pltpu.SemaphoreType.DMA] if last else []),
             compiler_params=params(),
             cost_estimate=cost(0.8),
             name=f"finish{role}",

time: 217 us -> 206 us (0.949)
  Pallas kernels: 63.5 us -> 50.4 us
  starting transfers between devices: 59.2 us -> 63.1 us
    pallas_call x5, Pallas kernels: 28 us -> 22.1 us  [finish(): pl.pallas_call(functools.partial(finish_kernel, role), in_specs=[SMEM, AN...]
    ppermute x8, starting transfers between devices: 15.7 us -> 21.2 us  [swap(): return lax.ppermute(x, 'cols', [(c, c ^ 1) for c in range(2 * planes)])]
    pallas_call x2, Pallas kernels: 16.4 us -> 13.5 us  [update(): pl.pallas_call(update_kernel, in_specs=[SMEM] + [ANY] * (3 + N_PIECES), o...]
    unnamed x35 -> x31, local copies, waits for them, and re-layouts: 6.79 us -> 7.86 us
  transfers between devices with their start and end apart: 30 -> 30, of which waited for: 10 -> 12; matrix products, arithmetic and copies ran while one was open for 2% -> 2% of each run, Pallas kernels for 30% -> 25%
where the time goes in v2:
time: 206 us; the launch traced here: 204 us
  starting transfers between devices  63.1 us (31%)
  waiting for transfers between devices  61.3 us (30%)
  Pallas kernels  50.4 us (24%)
  between operations  13.9 us (7%)
  local copies, waits for them, and re-layouts  11.8 us (6%)
  other arithmetic  3.56 us (2%)
    ppermute x13, waiting for transfers between devices, send(): lax.ppermute(x, 'cols', [(2 * source + k, 2 * target + k) for k in range(...  39.2 us
    ppermute x7, starting transfers between devices, fetch(): return lax.ppermute(x, ('rows', 'cols'), pairs)  23.7 us
    pallas_call x5, Pallas kernels, finish(): pl.pallas_call(functools.partial(finish_kernel, role), in_specs=[SMEM, AN...  22.1 us
    ppermute x8, starting transfers between devices, swap(): return lax.ppermute(x, 'cols', [(c, c ^ 1) for c in range(2 * planes)])  21.2 us
    ppermute x7, waiting for transfers between devices, fetch(): return lax.ppermute(x, ('rows', 'cols'), pairs)  20.8 us
    ppermute x13, starting transfers between devices, send(): lax.ppermute(x, 'cols', [(2 * source + k, 2 * target + k) for k in range(...  18.2 us
    pallas_call x2, Pallas kernels, update(): pl.pallas_call(update_kernel, in_specs=[SMEM] + [ANY] * (3 + N_PIECES), o...  13.5 us
    pallas_call x2, Pallas kernels, per_device(): pl.pallas_call(functools.partial(scores_kernel, scale, q * t), in_specs=[...  8.97 us
  transfers between devices with their start and end apart: 30, of which 12 were waited for; matrix products, arithmetic and copies ran while one was open for 2% of the time, Pallas kernels for 25%

profile of v2, /device:TPU:97, one launch (start us, length us, event | category | flops | bytes accessed | tf_op | source)
XLA Modules:
  0.0 204.1 jit_solution(5209391441758132530)
XLA Ops:
  6.5 1.0 constant_dynamic-slice_fusion.1
  7.6 1.7 pad_maximum_fusion.1
  9.3 3.2 %collective-permute-start.2 = (bf16[128,1024]{1,0:T(8,128)(2,1)S(1)}, bf16[128,1024]{1,0:T(8,128)(2,1)S(1)}, u32[]{:S(2)}, u32[]{:S(2)}) collective-permute-start(bf16[128,1024]{1,0:T(8,128)(2,1)S(1)} %bitcast.35), channel_id=1, source_target_pairs={{26,2},{99,3},{28,4},{101,5},{30,6},{103,7},{2,10},{107,11},{4,12}... | collective-permute-start | bytes 786440 | tf_op jit(solution)/shard_map/ppermute | solution.py:286
  12.6 4.5 %collective-permute-start.1 = (bf16[128,1024]{1,0:T(8,128)(2,1)S(1)}, bf16[128,1024]{1,0:T(8,128)(2,1)S(1)}, u32[]{:S(2)}, u32[]{:S(2)}) collective-permute-start(bf16[128,1024]{1,0:T(8,128)(2,1)S(1)} %bitcast.36), channel_id=1, source_target_pairs={{18,2},{67,3},{20,4},{69,5},{22,6},{71,7},{26,10},{75,11},{28,12},... | collective-permute-start | bytes 786440 | tf_op jit(solution)/shard_map/ppermute | solution.py:286
  17.1 3.0 %collective-permute-start = (bf16[128,1024]{1,0:T(8,128)(2,1)S(1)}, bf16[128,1024]{1,0:T(8,128)(2,1)S(1)}, u32[]{:S(2)}, u32[]{:S(2)}) collective-permute-start(bf16[128,1024]{1,0:T(8,128)(2,1)S(1)} %bitcast.37), channel_id=1, source_target_pairs={{10,2},{35,3},{12,4},{37,5},{14,6},{39,7},{18,10},{43,11},{20,12},... | collective-permute-start | bytes 786440 | tf_op jit(solution)/shard_map/ppermute | solution.py:286
  20.1 1.9 collective-permute-done.1
  22.0 3.2 %collective-permute-done = bf16[128,1024]{1,0:T(8,128)(2,1)S(1)} collective-permute-done((bf16[128,1024]{1,0:T(8,128)(2,1)S(1)}, bf16[128,1024]{1,0:T(8,128)(2,1)S(1)}, u32[]{:S(2)}, u32[]{:S(2)}) %collective-permute-start) | collective-permute-done | bytes 262176 | tf_op jit(solution)/shard_map/ppermute | solution.py:286
  25.4 3.2 %collective-permute-start.4 = (bf16[4,128,1024]{2,1,0:T(8,128)(2,1)S(1)}, bf16[4,128,1024]{2,1,0:T(8,128)(2,1)}, u32[]{:S(2)}, u32[]{:S(2)}) collective-permute-start(bf16[4,128,1024]{2,1,0:T(8,128)(2,1)S(1)} %pad_maximum_fusion.refs_1_.refs_0_), channel_id=1, source_target_pairs={{98,2},{27,3},{100,4},{29,5},{102,6},{31,7},{106,10},{3,11},{108,1... | collective-permute-start | bytes 3145736 | tf_op jit(solution)/shard_map/ppermute | solution.py:286
  28.6 3.3 %collective-permute-start.3 = (bf16[4,128,1024]{2,1,0:T(8,128)(2,1)S(1)}, bf16[4,128,1024]{2,1,0:T(8,128)(2,1)}, u32[]{:S(2)}, u32[]{:S(2)}) collective-permute-start(bf16[4,128,1024]{2,1,0:T(8,128)(2,1)S(1)} %pad_maximum_fusion.refs_1_.refs_0_), channel_id=1, source_target_pairs={{34,2},{11,3},{36,4},{13,5},{38,6},{15,7},{42,10},{19,11},{44,12},... | collective-permute-start | bytes 3145736 | tf_op jit(solution)/shard_map/ppermute | solution.py:286
  31.9 1.5 collective-permute-start.18
  33.5 0.5 copy.9.refs_0_
  34.0 0.7 constant_dynamic-slice_fusion
  34.7 9.7 %collective-permute-done.4.refs_2_ = bf16[4,128,1024]{2,1,0:T(8,128)(2,1)} collective-permute-done((bf16[4,128,1024]{2,1,0:T(8,128)(2,1)S(1)}, bf16[4,128,1024]{2,1,0:T(8,128)(2,1)}, u32[]{:S(2)}, u32[]{:S(2)}) %collective-permute-start.4) | collective-permute-done | bytes 1048608 | tf_op jit(solution)/shard_map/ppermute | solution.py:286
  44.4 1.3 collective-permute-done.3.refs_1_
  45.7 0.7 copy-done.14
  46.4 1.8 pick.1
  48.3 10.4 %collective-permute-start.7 = (bf16[2,512,512]{2,1,0:T(8,128)(2,1)S(1)}, bf16[2,512,512]{2,1,0:T(8,128)(2,1)S(1)}, u32[]{:S(2)}, u32[]{:S(2)}) collective-permute-start(bf16[2,512,512]{2,1,0:T(8,128)(2,1)S(1)} %copy-done.4), channel_id=1, source_target_pairs={{0,1},{1,0},{2,3},{3,2},{4,5},{5,4},{6,7},{7,6},{8,9},{9,8},{10,11... | collective-permute-start | bytes 3145736 | tf_op jit(solution)/shard_map/ppermute | solution.py:276
  58.7 1.1 slice.18
  59.8 2.2 %collective-permute-start.6 = (bf16[2,128,1024]{2,1,0:T(8,128)(2,1)S(1)}, bf16[2,128,1024]{2,1,0:T(8,128)(2,1)}, u32[]{:S(2)}, u32[]{:S(2)}) collective-permute-start(bf16[2,128,1024]{2,1,0:T(8,128)(2,1)S(1)} %slice.18), channel_id=1, source_target_pairs={{98,2},{27,3},{100,4},{29,5},{102,6},{31,7},{106,10},{3,11},{108,1... | collective-permute-start | bytes 1572872 | tf_op jit(solution)/shard_map/ppermute | solution.py:286
  62.0 1.1 slice.17
  63.1 4.3 %collective-permute-start.5 = (bf16[2,128,1024]{2,1,0:T(8,128)(2,1)S(1)}, bf16[2,128,1024]{2,1,0:T(8,128)(2,1)}, u32[]{:S(2)}, u32[]{:S(2)}) collective-permute-start(bf16[2,128,1024]{2,1,0:T(8,128)(2,1)S(1)} %slice.17), channel_id=1, source_target_pairs={{34,2},{11,3},{36,4},{13,5},{38,6},{15,7},{42,10},{19,11},{44,12},... | collective-permute-start | bytes 1572872 | tf_op jit(solution)/shard_map/ppermute | solution.py:286
  67.4 1.3 collective-permute-start.14
  68.7 4.7 %collective-permute-done.6.refs_2_.refs_4_ = bf16[2,128,1024]{2,1,0:T(8,128)(2,1)} collective-permute-done((bf16[2,128,1024]{2,1,0:T(8,128)(2,1)S(1)}, bf16[2,128,1024]{2,1,0:T(8,128)(2,1)}, u32[]{:S(2)}, u32[]{:S(2)}) %collective-permute-start.6) | collective-permute-done | bytes 524320 | tf_op jit(solution)/shard_map/ppermute | solution.py:286
  73.8 1.7 collective-permute-start.8
  75.5 0.6 copy-done.11
  76.1 1.4 copy-done.12
  77.5 4.5 %scores.2 = (f32[2,192,1024]{2,1,0:T(8,128)S(1)}, bf16[2,192,1024]{2,1,0:T(8,128)(2,1)}) custom-call(s32[4]{0:T(128)S(1)} %copy-done.11, bf16[768,1024]{1,0:T(8,128)(2,1)S(1)} %copy-done.12, bf16[2,512,512]{2,1,0:T(8,128)(2,1)S(1)} %copy-done.4, bf16[2,512,512]{2,1,0:T(8,128)(2,1)S(1)} %collective-permute-done.7.dt_oth, bf16[2,16,160,1024]{3,2,1,0:T(8,128)(2,1)} %bitcast.20), custom_call_target="tpu_custom_call" | custom-call | flops 5000000000 | bytes 1024 | tf_op jit(solution)/shard_map/scores/pallas_call | solution.py:350
  82.0 1.2 copy-done.8
  83.2 0.7 collective-permute-start.13
  84.5 1.3 collective-permute-start.10
  85.8 4.5 %scores.3 = (f32[2,192,1024]{2,1,0:T(8,128)S(1)}, bf16[2,192,1024]{2,1,0:T(8,128)(2,1)}) custom-call(s32[4]{0:T(128)S(1)} %copy-done.11, bf16[768,1024]{1,0:T(8,128)(2,1)S(1)} %copy-done.12, bf16[2,512,512]{2,1,0:T(8,128)(2,1)S(1)} %copy-done.4, bf16[2,512,512]{2,1,0:T(8,128)(2,1)S(1)} %collective-permute-done.7.dt_oth, bf16[2,16,160,1024]{3,2,1,0:T(8,128)(2,1)} %bitcast.21), custom_call_target="tpu_custom_call" | custom-call | flops 5000000000 | bytes 1024 | tf_op jit(solution)/shard_map/scores/pallas_call | solution.py:350
  90.3 1.1 copy-done.6
  91.4 1.5 collective-permute-start.12
  92.9 0.9 copy-done.9
  93.8 1.3 collective-permute-start.21
  95.1 11.9 %collective-permute-done.10.to_3 = bf16[2,192,1024]{2,1,0:T(8,128)(2,1)} collective-permute-done((bf16[2,192,1024]{2,1,0:T(8,128)(2,1)}, bf16[2,192,1024]{2,1,0:T(8,128)(2,1)}, u32[]{:S(2)}, u32[]{:S(2)}) %collective-permute-start.10) | collective-permute-done | bytes 786464 | tf_op jit(solution)/shard_map/ppermute | solution.py:273
  107.0 1.3 collective-permute-start.11
  108.4 1.6 finish1.2.own.refs_3_
  110.0 1.6 collective-permute-start.17
  111.5 12.3 %collective-permute-done.21.to_3 = bf16[2,192,1024]{2,1,0:T(8,128)(2,1)} collective-permute-done((bf16[2,192,1024]{2,1,0:T(8,128)(2,1)}, bf16[2,192,1024]{2,1,0:T(8,128)(2,1)}, u32[]{:S(2)}, u32[]{:S(2)}) %collective-permute-start.21) | collective-permute-done | bytes 786464 | tf_op jit(solution)/shard_map/ppermute | solution.py:273
  123.8 2.2 %collective-permute-start.22 = (bf16[2,192,1024]{2,1,0:T(8,128)(2,1)}, bf16[2,192,1024]{2,1,0:T(8,128)(2,1)}, u32[]{:S(2)}, u32[]{:S(2)}) collective-permute-start(bf16[2,192,1024]{2,1,0:T(8,128)(2,1)} %collective-permute-done.21.to_3), channel_id=1, source_target_pairs={{6,4},{7,5},{14,12},{15,13},{22,20},{23,21},{30,28},{31,29},{38,36... | collective-permute-start | bytes 2359304 | tf_op jit(solution)/shard_map/ppermute | solution.py:273
  126.1 2.4 %finish1.3.own.refs_3_ = bf16[2,192,1024]{2,1,0:T(8,128)(2,1)} custom-call(s32[4]{0:T(128)S(1)} %pad_add_fusion.info, f32[2,192,1024]{2,1,0:T(8,128)} %copy-done.6, bf16[2,192,1024]{2,1,0:T(8,128)(2,1)} %collective-permute-done.12.a, bf16[2,16,160,1024]{3,2,1,0:T(8,128)(2,1)} %bitcast.23, bf16[2,512,512]{2,1,0:T(8,128)(2,1)S(1)} %copy-done.4, ...), custom_call_target="tpu_custom_call" | custom-call | flops 800000000 | bytes 1024 | tf_op jit(solution)/shard_map/finish1/pallas_call | solution.py:373
  128.5 1.6 collective-permute-start.23
  130.1 6.6 %update.2.r = f32[2,192,1024]{2,1,0:T(8,128)} custom-call(s32[4]{0:T(128)S(1)} %pad_add_fusion.info, f32[2,192,1024]{2,1,0:T(8,128)} %hold.7.r, bf16[2,192,1024]{2,1,0:T(8,128)(2,1)} %collective-permute-done.10.to_3, bf16[2,192,1024]{2,1,0:T(8,128)(2,1)S(1)} %collective-permute-done.11.to_2, bf16[4,128,1024]{2,1,0:T(8,128)(2,1)S(1)} %copy-done.2, ...), custom_call_target="tpu_custom_call" | custom-call | bytes 1024 | tf_op jit(solution)/shard_map/update/pallas_call | solution.py:416
  136.7 1.4 copy-done.7
  138.1 1.3 finish2.1.refs_4_
  139.4 1.3 collective-permute-start.19
  140.7 1.0 collective-permute-done.22.before.to_2
  141.7 1.2 partial.2
  143.0 1.3 collective-permute-start.20
  144.3 1.6 both2.1.refs_4_
  145.9 1.4 collective-permute-start.24
  147.3 1.2 partial.3
  148.6 1.3 collective-permute-start.25
  149.9 6.9 %update.3.r = f32[2,192,1024]{2,1,0:T(8,128)} custom-call(s32[4]{0:T(128)S(1)} %pad_add_fusion.info, f32[2,192,1024]{2,1,0:T(8,128)} %copy-done.6, bf16[2,192,1024]{2,1,0:T(8,128)(2,1)} %collective-permute-done.21.to_3, bf16[2,192,1024]{2,1,0:T(8,128)(2,1)} %collective-permute-done.22.before.to_2, bf16[4,128,1024]{2,1,0:T(8,128)(2,1)S(1)} %copy-done.3, ...), custom_call_target="tpu_custom_call" | custom-call | bytes 1024 | tf_op jit(solution)/shard_map/update/pallas_call | solution.py:416
  156.8 4.4 %collective-permute-done.19.a = bf16[2,192,1024]{2,1,0:T(8,128)(2,1)S(1)} collective-permute-done((bf16[2,192,1024]{2,1,0:T(8,128)(2,1)S(1)}, bf16[2,192,1024]{2,1,0:T(8,128)(2,1)S(1)}, u32[]{:S(2)}, u32[]{:S(2)}) %collective-permute-start.19) | collective-permute-done | bytes 786464 | tf_op jit(solution)/shard_map/ppermute | solution.py:273
  161.2 2.7 %collective-permute-done.20.refs_1_ = bf16[2,192,1024]{2,1,0:T(8,128)(2,1)S(1)} collective-permute-done((bf16[2,192,1024]{2,1,0:T(8,128)(2,1)S(1)}, bf16[2,192,1024]{2,1,0:T(8,128)(2,1)S(1)}, u32[]{:S(2)}, u32[]{:S(2)}) %collective-permute-start.20) | collective-permute-done | bytes 786464 | tf_op jit(solution)/shard_map/ppermute | solution.py:273
  164.0 8.4 %finish3.2 = (bf16[192,1024]{1,0:T(8,128)(2,1)S(1)}, bf16[192,1024]{1,0:T(8,128)(2,1)S(1)}) custom-call(s32[4]{0:T(128)S(1)} %pad_add_fusion.info, f32[2,192,1024]{2,1,0:T(8,128)} %update.2.r, bf16[2,192,1024]{2,1,0:T(8,128)(2,1)S(1)} %collective-permute-done.19.a, bf16[2,16,160,1024]{3,2,1,0:T(8,128)(2,1)} %bitcast.26, bf16[2,512,512]{2,1,0:T(8,128)(2,1)S(1)} %copy-done.4, ...), custom_call_target="tpu_custom_call" | custom-call | flops 800000000 | bytes 1024 | tf_op jit(solution)/shard_map/finish3/pallas_call | solution.py:373
  172.3 4.4 %collective-permute-start.26 = (bf16[192,1024]{1,0:T(8,128)(2,1)S(1)}, bf16[192,1024]{1,0:T(8,128)(2,1)S(1)}, u32[]{:S(2)}, u32[]{:S(2)}) collective-permute-start(bf16[192,1024]{1,0:T(8,128)(2,1)S(1)} %get-tuple-element.35), channel_id=1, source_target_pairs={{0,1},{1,0},{2,3},{3,2},{4,5},{5,4},{6,7},{7,6},{8,9},{9,8},{10,11... | collective-permute-start | bytes 1179656 | tf_op jit(solution)/shard_map/ppermute | solution.py:276
  176.8 6.7 %collective-permute-done.24.a = bf16[2,192,1024]{2,1,0:T(8,128)(2,1)S(1)} collective-permute-done((bf16[2,192,1024]{2,1,0:T(8,128)(2,1)S(1)}, bf16[2,192,1024]{2,1,0:T(8,128)(2,1)S(1)}, u32[]{:S(2)}, u32[]{:S(2)}) %collective-permute-start.24) | collective-permute-done | bytes 786464 | tf_op jit(solution)/shard_map/ppermute | solution.py:273
  183.5 8.4 %finish3.3 = (bf16[192,1024]{1,0:T(8,128)(2,1)S(1)}, bf16[192,1024]{1,0:T(8,128)(2,1)S(1)}) custom-call(s32[4]{0:T(128)S(1)} %pad_add_fusion.info, f32[2,192,1024]{2,1,0:T(8,128)} %update.3.r, bf16[2,192,1024]{2,1,0:T(8,128)(2,1)S(1)} %collective-permute-done.24.a, bf16[2,16,160,1024]{3,2,1,0:T(8,128)(2,1)} %bitcast.27, bf16[2,512,512]{2,1,0:T(8,128)(2,1)S(1)} %copy-done.4, ...), custom_call_target="tpu_custom_call" | custom-call | flops 800000000 | bytes 1024 | tf_op jit(solution)/shard_map/finish3/pallas_call | solution.py:373
  191.9 2.3 %collective-permute-start.27 = (bf16[192,1024]{1,0:T(8,128)(2,1)S(1)}, bf16[192,1024]{1,0:T(8,128)(2,1)S(1)}, u32[]{:S(2)}, u32[]{:S(2)}) collective-permute-start(bf16[192,1024]{1,0:T(8,128)(2,1)S(1)} %get-tuple-element.36), channel_id=1, source_target_pairs={{0,1},{1,0},{2,3},{3,2},{4,5},{5,4},{6,7},{7,6},{8,9},{9,8},{10,11... | collective-permute-start | bytes 1179656 | tf_op jit(solution)/shard_map/ppermute | solution.py:276
  194.2 1.3 collective-permute-done.27
  195.6 1.7 maximum_select_fusion
  (55 shorter events, 1.4 us)
Async XLA Ops:
  6.5 2.8 %copy-start.13 = (bf16[1024,16,32]{0,2,1:T(8,128)(2,1)S(1)}, bf16[1024,16,32]{0,2,1:T(8,128)(2,1)}, u32[]{:S(2)}) copy-start(bf16[1024,16,32]{0,2,1:T(8,128)(2,1)} %param.6) | copy-start | bytes 3145732
  6.5 68.9 %all-gather.5.cloned.1.call-start = ((), (), s32[]{:S(2)}) async-start(), calls=%async_computation | async-start | bytes 10813440 | tf_op jit(solution)/shard_map/all_gather | solution.py:303
  9.2 127.5 %all-gather.7.cloned.1.call-start = ((), (), s32[]{:S(2)}) async-start(), calls=%async_computation.1 | async-start | bytes 8650752 | tf_op jit(solution)/shard_map/all_gather | solution.py:303
  9.3 10.7 %collective-permute-start.2 = (bf16[128,1024]{1,0:T(8,128)(2,1)S(1)}, bf16[128,1024]{1,0:T(8,128)(2,1)S(1)}, u32[]{:S(2)}, u32[]{:S(2)}) collective-permute-start(bf16[128,1024]{1,0:T(8,128)(2,1)S(1)} %bitcast.35), channel_id=1, source_target_pairs={{26,2},{99,3},{28,4},{101,5},{30,6},{103,7},{2,10},{107,11},{4,12}... | collective-permute-start | bytes 786440 | tf_op jit(solution)/shard_map/ppermute | solution.py:286
  12.6 9.5 %collective-permute-start.1 = (bf16[128,1024]{1,0:T(8,128)(2,1)S(1)}, bf16[128,1024]{1,0:T(8,128)(2,1)S(1)}, u32[]{:S(2)}, u32[]{:S(2)}) collective-permute-start(bf16[128,1024]{1,0:T(8,128)(2,1)S(1)} %bitcast.36), channel_id=1, source_target_pairs={{18,2},{67,3},{20,4},{69,5},{22,6},{71,7},{26,10},{75,11},{28,12},... | collective-permute-start | bytes 786440 | tf_op jit(solution)/shard_map/ppermute | solution.py:286
  17.1 8.2 %collective-permute-start = (bf16[128,1024]{1,0:T(8,128)(2,1)S(1)}, bf16[128,1024]{1,0:T(8,128)(2,1)S(1)}, u32[]{:S(2)}, u32[]{:S(2)}) collective-permute-start(bf16[128,1024]{1,0:T(8,128)(2,1)S(1)} %bitcast.37), channel_id=1, source_target_pairs={{10,2},{35,3},{12,4},{37,5},{14,6},{39,7},{18,10},{43,11},{20,12},... | collective-permute-start | bytes 786440 | tf_op jit(solution)/shard_map/ppermute | solution.py:286
  25.4 9.3 %copy-start = (bf16[4,128,1024]{2,1,0:T(8,128)(2,1)}, bf16[4,128,1024]{2,1,0:T(8,128)(2,1)S(1)}, u32[]{:S(2)}) copy-start(bf16[4,128,1024]{2,1,0:T(8,128)(2,1)S(1)} %pad_maximum_fusion.refs_1_.refs_0_) | copy-start | bytes 3145732
  25.4 19.0 %collective-permute-start.4 = (bf16[4,128,1024]{2,1,0:T(8,128)(2,1)S(1)}, bf16[4,128,1024]{2,1,0:T(8,128)(2,1)}, u32[]{:S(2)}, u32[]{:S(2)}) collective-permute-start(bf16[4,128,1024]{2,1,0:T(8,128)(2,1)S(1)} %pad_maximum_fusion.refs_1_.refs_0_), channel_id=1, source_target_pairs={{98,2},{27,3},{100,4},{29,5},{102,6},{31,7},{106,10},{3,11},{108,1... | collective-permute-start | bytes 3145736 | tf_op jit(solution)/shard_map/ppermute | solution.py:286
  28.6 17.1 %collective-permute-start.3 = (bf16[4,128,1024]{2,1,0:T(8,128)(2,1)S(1)}, bf16[4,128,1024]{2,1,0:T(8,128)(2,1)}, u32[]{:S(2)}, u32[]{:S(2)}) collective-permute-start(bf16[4,128,1024]{2,1,0:T(8,128)(2,1)S(1)} %pad_maximum_fusion.refs_1_.refs_0_), channel_id=1, source_target_pairs={{34,2},{11,3},{36,4},{13,5},{38,6},{15,7},{42,10},{19,11},{44,12},... | collective-permute-start | bytes 3145736 | tf_op jit(solution)/shard_map/ppermute | solution.py:286
  31.9 13.8 %collective-permute-start.18 = (bf16[4,32,1024]{2,1,0:T(8,128)(2,1)S(1)}, bf16[4,32,1024]{2,1,0:T(8,128)(2,1)S(1)}, u32[]{:S(2)}, u32[]{:S(2)}) collective-permute-start(bf16[4,32,1024]{2,1,0:T(8,128)(2,1)S(1)} %get-tuple-element.37), channel_id=1, source_target_pairs={{6,2},{7,3},{14,10},{15,11},{22,18},{23,19},{30,26},{31,27},{38,34... | collective-permute-start | bytes 786440 | tf_op jit(solution)/shard_map/ppermute | solution.py:273
  34.7 13.5 %copy-start.4 = (bf16[2,512,512]{2,1,0:T(8,128)(2,1)S(1)}, bf16[2,512,512]{2,1,0:T(8,128)(2,1)}, u32[]{:S(2)}) copy-start(bf16[2,512,512]{2,1,0:T(8,128)(2,1)} %dt_own.15) | copy-start | bytes 3145732
  45.7 0.7 copy-start.14
  46.4 21.0 %copy-start.1 = (bf16[4,128,1024]{2,1,0:T(8,128)(2,1)S(1)}, bf16[4,128,1024]{2,1,0:T(8,128)(2,1)}, u32[]{:S(2)}) copy-start(bf16[4,128,1024]{2,1,0:T(8,128)(2,1)} %copy-done) | copy-start | bytes 3145732
  48.3 27.2 %collective-permute-start.7 = (bf16[2,512,512]{2,1,0:T(8,128)(2,1)S(1)}, bf16[2,512,512]{2,1,0:T(8,128)(2,1)S(1)}, u32[]{:S(2)}, u32[]{:S(2)}) collective-permute-start(bf16[2,512,512]{2,1,0:T(8,128)(2,1)S(1)} %copy-done.4), channel_id=1, source_target_pairs={{0,1},{1,0},{2,3},{3,2},{4,5},{5,4},{6,7},{7,6},{8,9},{9,8},{10,11... | collective-permute-start | bytes 3145736 | tf_op jit(solution)/shard_map/ppermute | solution.py:276
  59.8 13.6 %collective-permute-start.6 = (bf16[2,128,1024]{2,1,0:T(8,128)(2,1)S(1)}, bf16[2,128,1024]{2,1,0:T(8,128)(2,1)}, u32[]{:S(2)}, u32[]{:S(2)}) collective-permute-start(bf16[2,128,1024]{2,1,0:T(8,128)(2,1)S(1)} %slice.18), channel_id=1, source_target_pairs={{98,2},{27,3},{100,4},{29,5},{102,6},{31,7},{106,10},{3,11},{108,1... | collective-permute-start | bytes 1572872 | tf_op jit(solution)/shard_map/ppermute | solution.py:286
  63.1 10.7 %collective-permute-start.5 = (bf16[2,128,1024]{2,1,0:T(8,128)(2,1)S(1)}, bf16[2,128,1024]{2,1,0:T(8,128)(2,1)}, u32[]{:S(2)}, u32[]{:S(2)}) collective-permute-start(bf16[2,128,1024]{2,1,0:T(8,128)(2,1)S(1)} %slice.17), channel_id=1, source_target_pairs={{34,2},{11,3},{36,4},{13,5},{38,6},{15,7},{42,10},{19,11},{44,12},... | collective-permute-start | bytes 1572872 | tf_op jit(solution)/shard_map/ppermute | solution.py:286
  67.4 24.0 %collective-permute-start.14 = (bf16[4,128,1024]{2,1,0:T(8,128)(2,1)S(1)}, bf16[4,128,1024]{2,1,0:T(8,128)(2,1)}, u32[]{:S(2)}, u32[]{:S(2)}) collective-permute-start(bf16[4,128,1024]{2,1,0:T(8,128)(2,1)S(1)} %copy-done.1), channel_id=1, source_target_pairs={{0,1},{1,0},{2,3},{3,2},{4,5},{5,4},{6,7},{7,6},{8,9},{9,8},{10,11... | collective-permute-start | bytes 3145736 | tf_op jit(solution)/shard_map/ppermute | solution.py:276
  73.4 10.6 %collective-permute-start.9 = (bf16[2,128,1024]{2,1,0:T(8,128)(2,1)}, bf16[2,128,1024]{2,1,0:T(8,128)(2,1)}, u32[]{:S(2)}, u32[]{:S(2)}) collective-permute-start(bf16[2,128,1024]{2,1,0:T(8,128)(2,1)} %collective-permute-done.6.refs_2_.refs_4_), channel_id=1, source_target_pairs={{0,1},{1,0},{2,3},{3,2},{4,5},{5,4},{6,7},{7,6},{8,9},{9,8},{10,11... | collective-permute-start | bytes 1572872 | tf_op jit(solution)/shard_map/ppermute | solution.py:276
  73.8 10.7 %collective-permute-start.8 = (bf16[2,128,1024]{2,1,0:T(8,128)(2,1)}, bf16[2,128,1024]{2,1,0:T(8,128)(2,1)}, u32[]{:S(2)}, u32[]{:S(2)}) collective-permute-start(bf16[2,128,1024]{2,1,0:T(8,128)(2,1)} %collective-permute-done.5.refs_1_.refs_3_), channel_id=1, source_target_pairs={{0,1},{1,0},{2,3},{3,2},{4,5},{5,4},{6,7},{7,6},{8,9},{9,8},{10,11... | collective-permute-start | bytes 1572872 | tf_op jit(solution)/shard_map/ppermute | solution.py:276
  75.4 61.3 %copy-start.5 = (bf16[2,512,512]{2,1,0:T(8,128)(2,1)}, bf16[2,512,512]{2,1,0:T(8,128)(2,1)S(1)}, u32[]{:S(2)}) copy-start(bf16[2,512,512]{2,1,0:T(8,128)(2,1)S(1)} %collective-permute-done.7.dt_oth) | copy-start | bytes 3145732
  75.5 0.6 copy-start.11
  76.1 1.4 copy-start.12
  82.0 1.2 copy-start.8
  83.2 9.8 %collective-permute-start.13 = (bf16[2,192,1024]{2,1,0:T(8,128)(2,1)}, bf16[2,192,1024]{2,1,0:T(8,128)(2,1)S(1)}, u32[]{:S(2)}, u32[]{:S(2)}) collective-permute-start(bf16[2,192,1024]{2,1,0:T(8,128)(2,1)} %get-tuple-element.22.refs_2_), channel_id=1, source_target_pairs={{0,2},{1,3},{8,10},{9,11},{16,18},{17,19},{24,26},{25,27},{32,34},... | collective-permute-start | bytes 2359304 | tf_op jit(solution)/shard_map/ppermute | solution.py:273
  83.9 24.4 %collective-permute-start.16 = (bf16[4,128,1024]{2,1,0:T(8,128)(2,1)}, bf16[4,128,1024]{2,1,0:T(8,128)(2,1)}, u32[]{:S(2)}, u32[]{:S(2)}) collective-permute-start(bf16[4,128,1024]{2,1,0:T(8,128)(2,1)} %collective-permute-done.4.refs_2_), channel_id=1, source_target_pairs={{0,1},{1,0},{2,3},{3,2},{4,5},{5,4},{6,7},{7,6},{8,9},{9,8},{10,11... | collective-permute-start | bytes 3145736 | tf_op jit(solution)/shard_map/ppermute | solution.py:276
  84.0 24.3 %collective-permute-start.15 = (bf16[4,128,1024]{2,1,0:T(8,128)(2,1)}, bf16[4,128,1024]{2,1,0:T(8,128)(2,1)}, u32[]{:S(2)}, u32[]{:S(2)}) collective-permute-start(bf16[4,128,1024]{2,1,0:T(8,128)(2,1)} %collective-permute-done.3.refs_1_), channel_id=1, source_target_pairs={{0,1},{1,0},{2,3},{3,2},{4,5},{5,4},{6,7},{7,6},{8,9},{9,8},{10,11... | collective-permute-start | bytes 3145736 | tf_op jit(solution)/shard_map/ppermute | solution.py:276
  84.5 22.5 %collective-permute-start.10 = (bf16[2,192,1024]{2,1,0:T(8,128)(2,1)}, bf16[2,192,1024]{2,1,0:T(8,128)(2,1)}, u32[]{:S(2)}, u32[]{:S(2)}) collective-permute-start(bf16[2,192,1024]{2,1,0:T(8,128)(2,1)} %get-tuple-element.22.refs_2_), channel_id=1, source_target_pairs={{0,6},{1,7},{8,14},{9,15},{16,22},{17,23},{24,30},{25,31},{32,38},... | collective-permute-start | bytes 2359304 | tf_op jit(solution)/shard_map/ppermute | solution.py:273
  90.2 1.1 copy-start.6
  91.4 20.1 %collective-permute-start.12 = (bf16[2,192,1024]{2,1,0:T(8,128)(2,1)}, bf16[2,192,1024]{2,1,0:T(8,128)(2,1)}, u32[]{:S(2)}, u32[]{:S(2)}) collective-permute-start(bf16[2,192,1024]{2,1,0:T(8,128)(2,1)} %get-tuple-element.24.refs_1_.refs_2_), channel_id=1, source_target_pairs={{0,2},{1,3},{8,10},{9,11},{16,18},{17,19},{24,26},{25,27},{32,34},... | collective-permute-start | bytes 2359304 | tf_op jit(solution)/shard_map/ppermute | solution.py:273
  92.9 0.9 copy-start.9
  93.8 30.0 %collective-permute-start.21 = (bf16[2,192,1024]{2,1,0:T(8,128)(2,1)}, bf16[2,192,1024]{2,1,0:T(8,128)(2,1)}, u32[]{:S(2)}, u32[]{:S(2)}) collective-permute-start(bf16[2,192,1024]{2,1,0:T(8,128)(2,1)} %get-tuple-element.24.refs_1_.refs_2_), channel_id=1, source_target_pairs={{0,6},{1,7},{8,14},{9,15},{16,22},{17,23},{24,30},{25,31},{32,38},... | collective-permute-start | bytes 2359304 | tf_op jit(solution)/shard_map/ppermute | solution.py:273
  95.1 13.3 %copy-start.10 = (bf16[2,192,1024]{2,1,0:T(8,128)(2,1)S(1)}, bf16[2,192,1024]{2,1,0:T(8,128)(2,1)}, u32[]{:S(2)}) copy-start(bf16[2,192,1024]{2,1,0:T(8,128)(2,1)} %copy-done.9) | copy-start | bytes 2359300
  107.0 23.1 %collective-permute-start.11 = (bf16[2,192,1024]{2,1,0:T(8,128)(2,1)}, bf16[2,192,1024]{2,1,0:T(8,128)(2,1)S(1)}, u32[]{:S(2)}, u32[]{:S(2)}) collective-permute-start(bf16[2,192,1024]{2,1,0:T(8,128)(2,1)} %collective-permute-done.10.to_3), channel_id=1, source_target_pairs={{6,4},{7,5},{14,12},{15,13},{22,20},{23,21},{30,28},{31,29},{38,36... | collective-permute-start | bytes 2359304 | tf_op jit(solution)/shard_map/ppermute | solution.py:273
  110.0 26.7 %collective-permute-start.17 = (bf16[2,192,1024]{2,1,0:T(8,128)(2,1)}, bf16[2,192,1024]{2,1,0:T(8,128)(2,1)}, u32[]{:S(2)}, u32[]{:S(2)}) collective-permute-start(bf16[2,192,1024]{2,1,0:T(8,128)(2,1)} %finish1.2.own.refs_3_), channel_id=1, source_target_pairs={{2,4},{3,5},{10,12},{11,13},{18,20},{19,21},{26,28},{27,29},{34,36... | collective-permute-start | bytes 2359304 | tf_op jit(solution)/shard_map/ppermute | solution.py:273
  123.8 17.9 %collective-permute-start.22 = (bf16[2,192,1024]{2,1,0:T(8,128)(2,1)}, bf16[2,192,1024]{2,1,0:T(8,128)(2,1)}, u32[]{:S(2)}, u32[]{:S(2)}) collective-permute-start(bf16[2,192,1024]{2,1,0:T(8,128)(2,1)} %collective-permute-done.21.to_3), channel_id=1, source_target_pairs={{6,4},{7,5},{14,12},{15,13},{22,20},{23,21},{30,28},{31,29},{38,36... | collective-permute-start | bytes 2359304 | tf_op jit(solution)/shard_map/ppermute | solution.py:273
  126.1 4.0 %copy-start.2 = (bf16[4,128,1024]{2,1,0:T(8,128)(2,1)S(1)}, bf16[4,128,1024]{2,1,0:T(8,128)(2,1)}, u32[]{:S(2)}) copy-start(bf16[4,128,1024]{2,1,0:T(8,128)(2,1)} %copy-done) | copy-start | bytes 3145732
  128.5 15.8 %collective-permute-start.23 = (bf16[2,192,1024]{2,1,0:T(8,128)(2,1)}, bf16[2,192,1024]{2,1,0:T(8,128)(2,1)}, u32[]{:S(2)}, u32[]{:S(2)}) collective-permute-start(bf16[2,192,1024]{2,1,0:T(8,128)(2,1)} %finish1.3.own.refs_3_), channel_id=1, source_target_pairs={{2,4},{3,5},{10,12},{11,13},{18,20},{19,21},{26,28},{27,29},{34,36... | collective-permute-start | bytes 2359304 | tf_op jit(solution)/shard_map/ppermute | solution.py:273
  136.7 1.4 copy-start.7
  139.4 21.8 %collective-permute-start.19 = (bf16[2,192,1024]{2,1,0:T(8,128)(2,1)S(1)}, bf16[2,192,1024]{2,1,0:T(8,128)(2,1)S(1)}, u32[]{:S(2)}, u32[]{:S(2)}) collective-permute-start(bf16[2,192,1024]{2,1,0:T(8,128)(2,1)S(1)} %finish2.1.refs_4_), channel_id=1, source_target_pairs={{4,6},{5,7},{12,14},{13,15},{20,22},{21,23},{28,30},{29,31},{36,38... | collective-permute-start | bytes 2359304 | tf_op jit(solution)/shard_map/ppermute | solution.py:273
  143.0 21.0 %collective-permute-start.20 = (bf16[2,192,1024]{2,1,0:T(8,128)(2,1)S(1)}, bf16[2,192,1024]{2,1,0:T(8,128)(2,1)S(1)}, u32[]{:S(2)}, u32[]{:S(2)}) collective-permute-start(bf16[2,192,1024]{2,1,0:T(8,128)(2,1)S(1)} %partial.2), channel_id=1, source_target_pairs={{2,6},{3,7},{10,14},{11,15},{18,22},{19,23},{26,30},{27,31},{34,38... | collective-permute-start | bytes 2359304 | tf_op jit(solution)/shard_map/ppermute | solution.py:273
  145.9 4.0 %copy-start.3 = (bf16[4,128,1024]{2,1,0:T(8,128)(2,1)S(1)}, bf16[4,128,1024]{2,1,0:T(8,128)(2,1)}, u32[]{:S(2)}) copy-start(bf16[4,128,1024]{2,1,0:T(8,128)(2,1)} %copy-done) | copy-start | bytes 3145732
  145.9 37.6 %collective-permute-start.24 = (bf16[2,192,1024]{2,1,0:T(8,128)(2,1)S(1)}, bf16[2,192,1024]{2,1,0:T(8,128)(2,1)S(1)}, u32[]{:S(2)}, u32[]{:S(2)}) collective-permute-start(bf16[2,192,1024]{2,1,0:T(8,128)(2,1)S(1)} %both2.1.refs_4_), channel_id=1, source_target_pairs={{4,6},{5,7},{12,14},{13,15},{20,22},{21,23},{28,30},{29,31},{36,38... | collective-permute-start | bytes 2359304 | tf_op jit(solution)/shard_map/ppermute | solution.py:273
  148.6 34.9 %collective-permute-start.25 = (bf16[2,192,1024]{2,1,0:T(8,128)(2,1)S(1)}, bf16[2,192,1024]{2,1,0:T(8,128)(2,1)S(1)}, u32[]{:S(2)}, u32[]{:S(2)}) collective-permute-start(bf16[2,192,1024]{2,1,0:T(8,128)(2,1)S(1)} %partial.3), channel_id=1, source_target_pairs={{2,6},{3,7},{10,14},{11,15},{18,22},{19,23},{26,30},{27,31},{34,38... | collective-permute-start | bytes 2359304 | tf_op jit(solution)/shard_map/ppermute | solution.py:273
  172.3 21.9 %collective-permute-start.26 = (bf16[192,1024]{1,0:T(8,128)(2,1)S(1)}, bf16[192,1024]{1,0:T(8,128)(2,1)S(1)}, u32[]{:S(2)}, u32[]{:S(2)}) collective-permute-start(bf16[192,1024]{1,0:T(8,128)(2,1)S(1)} %get-tuple-element.35), channel_id=1, source_target_pairs={{0,1},{1,0},{2,3},{3,2},{4,5},{5,4},{6,7},{7,6},{8,9},{9,8},{10,11... | collective-permute-start | bytes 1179656 | tf_op jit(solution)/shard_map/ppermute | solution.py:276
  191.9 3.7 %collective-permute-start.27 = (bf16[192,1024]{1,0:T(8,128)(2,1)S(1)}, bf16[192,1024]{1,0:T(8,128)(2,1)S(1)}, u32[]{:S(2)}, u32[]{:S(2)}) collective-permute-start(bf16[192,1024]{1,0:T(8,128)(2,1)S(1)} %get-tuple-element.36), channel_id=1, source_target_pairs={{0,1},{1,0},{2,3},{3,2},{4,5},{5,4},{6,7},{7,6},{8,9},{9,8},{10,11... | collective-permute-start | bytes 1179656 | tf_op jit(solution)/shard_map/ppermute | solution.py:276
Sparse Core Ops, SparseCore 0:
  9.6 62.0 all-gather.4
  74.0 53.6 all-gather.6

commit v3 on v2

--- a/solution.py
+++ b/solution.py
@@ -443,7 +443,9 @@
         done.append(finish(3, r2[q], a, (parts[q], f0[q], f1[q], f2[q])))
     keep = [x for x, _ in done]
     got = [swap(x) for _, x in done]
-    return jnp.where(core == 0, jnp.concatenate(keep + got, axis=0), jnp.concatenate(got + keep, axis=0))
+    ahead = [jnp.where(core == 0, x, y) for x, y in zip(keep, got)]
+    behind = [jnp.where(core == 0, y, x) for x, y in zip(keep, got)]
+    return jnp.concatenate(ahead + behind, axis=0)
 
 
 def solution(mesh):

time: 206 us -> 210 us (1.019)
  waiting for transfers between devices: 61.3 us -> 69.5 us
  starting transfers between devices: 63.1 us -> 60.5 us
    ppermute x7, waiting for transfers between devices: 20.8 us -> 29.1 us  [fetch(): return lax.ppermute(x, ('rows', 'cols'), pairs)]
    ppermute x7, starting transfers between devices: 23.7 us -> 21.2 us  [fetch(): return lax.ppermute(x, ('rows', 'cols'), pairs)]
  transfers between devices with their start and end apart: 30 -> 30, of which waited for: 12 -> 11; matrix products, arithmetic and copies ran while one was open for 2% -> 2% of each run, Pallas kernels for 25% -> 24%
where the time goes in v3:
time: 210 us
  waiting for transfers between devices  69.5 us (33%)
  starting transfers between devices  60.5 us (29%)
  Pallas kernels  50.4 us (24%)
  between operations  13.9 us (7%)
  local copies, waits for them, and re-layouts  11.9 us (6%)
  other arithmetic  3.32 us (2%)
    ppermute x13, waiting for transfers between devices, send(): lax.ppermute(x, 'cols', [(2 * source + k, 2 * target + k) for k in range(...  38.8 us
    ppermute x7, waiting for transfers between devices, fetch(): return lax.ppermute(x, ('rows', 'cols'), pairs)  29.1 us
    pallas_call x5, Pallas kernels, finish(): pl.pallas_call(functools.partial(finish_kernel, role), in_specs=[SMEM, AN...  22.3 us
    ppermute x8, starting transfers between devices, swap(): return lax.ppermute(x, 'cols', [(c, c ^ 1) for c in range(2 * planes)])  21.2 us
    ppermute x7, starting transfers between devices, fetch(): return lax.ppermute(x, ('rows', 'cols'), pairs)  21.2 us
    ppermute x13, starting transfers between devices, send(): lax.ppermute(x, 'cols', [(2 * source + k, 2 * target + k) for k in range(...  18 us
    pallas_call x2, Pallas kernels, update(): pl.pallas_call(update_kernel, in_specs=[SMEM] + [ANY] * (3 + N_PIECES), o...  13.2 us
    pallas_call x2, Pallas kernels, per_device(): pl.pallas_call(functools.partial(scores_kernel, scale, q * t), in_specs=[...  9.01 us
  transfers between devices with their start and end apart: 30, of which 11 were waited for; matrix products, arithmetic and copies ran while one was open for 2% of the time, Pallas kernels for 24%

profile of v3, /device:TPU:97, one launch (start us, length us, event | category | flops | bytes accessed | tf_op | source)
XLA Modules:
  0.0 209.5 jit_solution(295603864090988032)
XLA Ops:
  6.5 1.0 constant_dynamic-slice_fusion.1
  7.6 1.7 pad_maximum_fusion.2
  9.3 4.6 %collective-permute-start = (bf16[128,1024]{1,0:T(8,128)(2,1)S(1)}, bf16[128,1024]{1,0:T(8,128)(2,1)S(1)}, u32[]{:S(2)}, u32[]{:S(2)}) collective-permute-start(bf16[128,1024]{1,0:T(8,128)(2,1)S(1)} %bitcast.35), channel_id=1, source_target_pairs={{10,2},{35,3},{12,4},{37,5},{14,6},{39,7},{18,10},{43,11},{20,12},... | collective-permute-start | bytes 786440 | tf_op jit(solution)/shard_map/ppermute | solution.py:286
  14.0 2.3 %collective-permute-start.1 = (bf16[128,1024]{1,0:T(8,128)(2,1)S(1)}, bf16[128,1024]{1,0:T(8,128)(2,1)S(1)}, u32[]{:S(2)}, u32[]{:S(2)}) collective-permute-start(bf16[128,1024]{1,0:T(8,128)(2,1)S(1)} %bitcast.36), channel_id=1, source_target_pairs={{18,2},{67,3},{20,4},{69,5},{22,6},{71,7},{26,10},{75,11},{28,12},... | collective-permute-start | bytes 786440 | tf_op jit(solution)/shard_map/ppermute | solution.py:286
  16.3 2.6 %collective-permute-start.2 = (bf16[128,1024]{1,0:T(8,128)(2,1)S(1)}, bf16[128,1024]{1,0:T(8,128)(2,1)S(1)}, u32[]{:S(2)}, u32[]{:S(2)}) collective-permute-start(bf16[128,1024]{1,0:T(8,128)(2,1)S(1)} %bitcast.37), channel_id=1, source_target_pairs={{26,2},{99,3},{28,4},{101,5},{30,6},{103,7},{2,10},{107,11},{4,12}... | collective-permute-start | bytes 786440 | tf_op jit(solution)/shard_map/ppermute | solution.py:286
  18.9 4.0 %collective-permute-done.1 = bf16[128,1024]{1,0:T(8,128)(2,1)S(1)} collective-permute-done((bf16[128,1024]{1,0:T(8,128)(2,1)S(1)}, bf16[128,1024]{1,0:T(8,128)(2,1)S(1)}, u32[]{:S(2)}, u32[]{:S(2)}) %collective-permute-start.1) | collective-permute-done | bytes 262176 | tf_op jit(solution)/shard_map/ppermute | solution.py:286
  22.9 3.6 %collective-permute-done.2 = bf16[128,1024]{1,0:T(8,128)(2,1)S(1)} collective-permute-done((bf16[128,1024]{1,0:T(8,128)(2,1)S(1)}, bf16[128,1024]{1,0:T(8,128)(2,1)S(1)}, u32[]{:S(2)}, u32[]{:S(2)}) %collective-permute-start.2) | collective-permute-done | bytes 262176 | tf_op jit(solution)/shard_map/ppermute | solution.py:286
  26.7 4.5 %collective-permute-start.3 = (bf16[4,128,1024]{2,1,0:T(8,128)(2,1)S(1)}, bf16[4,128,1024]{2,1,0:T(8,128)(2,1)}, u32[]{:S(2)}, u32[]{:S(2)}) collective-permute-start(bf16[4,128,1024]{2,1,0:T(8,128)(2,1)S(1)} %pad_maximum_fusion.1.refs_1_.refs_0_), channel_id=1, source_target_pairs={{34,2},{11,3},{36,4},{13,5},{38,6},{15,7},{42,10},{19,11},{44,12},... | collective-permute-start | bytes 3145736 | tf_op jit(solution)/shard_map/ppermute | solution.py:286
  31.2 1.9 collective-permute-start.4
  33.2 1.3 collective-permute-start.18
  34.6 0.5 copy.9.refs_0_
  35.1 0.7 constant_dynamic-slice_fusion
  35.9 8.3 %collective-permute-done.3.refs_1_ = bf16[4,128,1024]{2,1,0:T(8,128)(2,1)} collective-permute-done((bf16[4,128,1024]{2,1,0:T(8,128)(2,1)S(1)}, bf16[4,128,1024]{2,1,0:T(8,128)(2,1)}, u32[]{:S(2)}, u32[]{:S(2)}) %collective-permute-start.3) | collective-permute-done | bytes 1048608 | tf_op jit(solution)/shard_map/ppermute | solution.py:286
  44.2 6.5 %collective-permute-done.4.refs_2_ = bf16[4,128,1024]{2,1,0:T(8,128)(2,1)} collective-permute-done((bf16[4,128,1024]{2,1,0:T(8,128)(2,1)S(1)}, bf16[4,128,1024]{2,1,0:T(8,128)(2,1)}, u32[]{:S(2)}, u32[]{:S(2)}) %collective-permute-start.4) | collective-permute-done | bytes 1048608 | tf_op jit(solution)/shard_map/ppermute | solution.py:286
  50.7 0.7 copy-done.14
  51.4 1.8 pick.1
  53.3 14.7 %collective-permute-start.7 = (bf16[2,512,512]{2,1,0:T(8,128)(2,1)S(1)}, bf16[2,512,512]{2,1,0:T(8,128)(2,1)S(1)}, u32[]{:S(2)}, u32[]{:S(2)}) collective-permute-start(bf16[2,512,512]{2,1,0:T(8,128)(2,1)S(1)} %copy-done.4), channel_id=1, source_target_pairs={{0,1},{1,0},{2,3},{3,2},{4,5},{5,4},{6,7},{7,6},{8,9},{9,8},{10,11... | collective-permute-start | bytes 3145736 | tf_op jit(solution)/shard_map/ppermute | solution.py:276
  68.0 1.1 slice.17
  69.1 1.9 collective-permute-start.5
  71.0 1.1 slice.18
  72.2 3.3 %collective-permute-start.6 = (bf16[2,128,1024]{2,1,0:T(8,128)(2,1)S(1)}, bf16[2,128,1024]{2,1,0:T(8,128)(2,1)}, u32[]{:S(2)}, u32[]{:S(2)}) collective-permute-start(bf16[2,128,1024]{2,1,0:T(8,128)(2,1)S(1)} %slice.18), channel_id=1, source_target_pairs={{98,2},{27,3},{100,4},{29,5},{102,6},{31,7},{106,10},{3,11},{108,1... | collective-permute-start | bytes 1572872 | tf_op jit(solution)/shard_map/ppermute | solution.py:286
  75.5 0.7 collective-permute-start.14
  76.2 3.2 %collective-permute-done.5.refs_1_.refs_3_ = bf16[2,128,1024]{2,1,0:T(8,128)(2,1)} collective-permute-done((bf16[2,128,1024]{2,1,0:T(8,128)(2,1)S(1)}, bf16[2,128,1024]{2,1,0:T(8,128)(2,1)}, u32[]{:S(2)}, u32[]{:S(2)}) %collective-permute-start.5) | collective-permute-done | bytes 524320 | tf_op jit(solution)/shard_map/ppermute | solution.py:286
  79.4 0.9 collective-permute-start.8
  80.4 3.4 %collective-permute-done.6.refs_2_.refs_4_ = bf16[2,128,1024]{2,1,0:T(8,128)(2,1)} collective-permute-done((bf16[2,128,1024]{2,1,0:T(8,128)(2,1)S(1)}, bf16[2,128,1024]{2,1,0:T(8,128)(2,1)}, u32[]{:S(2)}, u32[]{:S(2)}) %collective-permute-start.6) | collective-permute-done | bytes 524320 | tf_op jit(solution)/shard_map/ppermute | solution.py:286
  83.7 0.9 collective-permute-start.9
  84.6 0.6 copy-done.11
  85.2 1.5 copy-done.12
  86.7 4.5 %scores.2 = (f32[2,192,1024]{2,1,0:T(8,128)S(1)}, bf16[2,192,1024]{2,1,0:T(8,128)(2,1)}) custom-call(s32[4]{0:T(128)S(1)} %copy-done.11, bf16[768,1024]{1,0:T(8,128)(2,1)S(1)} %copy-done.12, bf16[2,512,512]{2,1,0:T(8,128)(2,1)S(1)} %copy-done.4, bf16[2,512,512]{2,1,0:T(8,128)(2,1)S(1)} %collective-permute-done.7.dt_oth, bf16[2,16,160,1024]{3,2,1,0:T(8,128)(2,1)} %bitcast.20), custom_call_target="tpu_custom_call" | custom-call | flops 5000000000 | bytes 1024 | tf_op jit(solution)/shard_map/scores/pallas_call | solution.py:350
  91.2 1.1 copy-done.8
  92.3 0.7 collective-permute-start.13
  93.1 0.5 collective-permute-start.16
  93.6 1.3 collective-permute-start.10
  94.9 4.5 %scores.3 = (f32[2,192,1024]{2,1,0:T(8,128)S(1)}, bf16[2,192,1024]{2,1,0:T(8,128)(2,1)}) custom-call(s32[4]{0:T(128)S(1)} %copy-done.11, bf16[768,1024]{1,0:T(8,128)(2,1)S(1)} %copy-done.12, bf16[2,512,512]{2,1,0:T(8,128)(2,1)S(1)} %copy-done.4, bf16[2,512,512]{2,1,0:T(8,128)(2,1)S(1)} %collective-permute-done.7.dt_oth, bf16[2,16,160,1024]{3,2,1,0:T(8,128)(2,1)} %bitcast.21), custom_call_target="tpu_custom_call" | custom-call | flops 5000000000 | bytes 1024 | tf_op jit(solution)/shard_map/scores/pallas_call | solution.py:350
  99.4 1.1 copy-done.6
  100.6 1.5 collective-permute-start.12
  102.1 0.9 copy-done.9
  103.0 1.3 collective-permute-start.22
  104.3 11.8 %collective-permute-done.10.to_3 = bf16[2,192,1024]{2,1,0:T(8,128)(2,1)} collective-permute-done((bf16[2,192,1024]{2,1,0:T(8,128)(2,1)}, bf16[2,192,1024]{2,1,0:T(8,128)(2,1)}, u32[]{:S(2)}, u32[]{:S(2)}) %collective-permute-start.10) | collective-permute-done | bytes 786464 | tf_op jit(solution)/shard_map/ppermute | solution.py:273
  116.1 1.3 collective-permute-start.11
  117.5 1.6 finish1.2.own.refs_3_
  119.1 1.6 collective-permute-start.17
  120.7 12.3 %collective-permute-done.22.to_3 = bf16[2,192,1024]{2,1,0:T(8,128)(2,1)} collective-permute-done((bf16[2,192,1024]{2,1,0:T(8,128)(2,1)}, bf16[2,192,1024]{2,1,0:T(8,128)(2,1)}, u32[]{:S(2)}, u32[]{:S(2)}) %collective-permute-start.22) | collective-permute-done | bytes 786464 | tf_op jit(solution)/shard_map/ppermute | solution.py:273
  133.0 2.2 %collective-permute-start.23 = (bf16[2,192,1024]{2,1,0:T(8,128)(2,1)}, bf16[2,192,1024]{2,1,0:T(8,128)(2,1)}, u32[]{:S(2)}, u32[]{:S(2)}) collective-permute-start(bf16[2,192,1024]{2,1,0:T(8,128)(2,1)} %collective-permute-done.22.to_3), channel_id=1, source_target_pairs={{6,4},{7,5},{14,12},{15,13},{22,20},{23,21},{30,28},{31,29},{38,36... | collective-permute-start | bytes 2359304 | tf_op jit(solution)/shard_map/ppermute | solution.py:273
  135.2 2.4 %finish1.3.own.refs_3_ = bf16[2,192,1024]{2,1,0:T(8,128)(2,1)} custom-call(s32[4]{0:T(128)S(1)} %pad_add_fusion.info, f32[2,192,1024]{2,1,0:T(8,128)} %copy-done.6, bf16[2,192,1024]{2,1,0:T(8,128)(2,1)} %collective-permute-done.12.a, bf16[2,16,160,1024]{3,2,1,0:T(8,128)(2,1)} %bitcast.23, bf16[2,512,512]{2,1,0:T(8,128)(2,1)S(1)} %copy-done.4, ...), custom_call_target="tpu_custom_call" | custom-call | flops 800000000 | bytes 1024 | tf_op jit(solution)/shard_map/finish1/pallas_call | solution.py:373
  137.6 1.5 collective-permute-start.24
  139.2 6.6 %update.2.r = f32[2,192,1024]{2,1,0:T(8,128)} custom-call(s32[4]{0:T(128)S(1)} %pad_add_fusion.info, f32[2,192,1024]{2,1,0:T(8,128)} %hold.7.r, bf16[2,192,1024]{2,1,0:T(8,128)(2,1)} %collective-permute-done.10.to_3, bf16[2,192,1024]{2,1,0:T(8,128)(2,1)S(1)} %collective-permute-done.11.to_2, bf16[4,128,1024]{2,1,0:T(8,128)(2,1)S(1)} %copy-done.2, ...), custom_call_target="tpu_custom_call" | custom-call | bytes 1024 | tf_op jit(solution)/shard_map/update/pallas_call | solution.py:416
  145.9 1.4 copy-done.7
  147.3 1.3 finish2.1.refs_4_
  148.6 1.3 collective-permute-start.19
  149.9 1.2 partial.2
  151.1 1.3 collective-permute-start.20
  152.4 1.6 both2.1.refs_4_
  154.0 1.3 collective-permute-start.25
  155.3 1.2 partial.3
  156.6 1.4 collective-permute-start.26
  158.0 11.1 %collective-permute-done.19.a = bf16[2,192,1024]{2,1,0:T(8,128)(2,1)S(1)} collective-permute-done((bf16[2,192,1024]{2,1,0:T(8,128)(2,1)S(1)}, bf16[2,192,1024]{2,1,0:T(8,128)(2,1)S(1)}, u32[]{:S(2)}, u32[]{:S(2)}) %collective-permute-start.19) | collective-permute-done | bytes 786464 | tf_op jit(solution)/shard_map/ppermute | solution.py:273
  169.1 3.6 %collective-permute-done.20.refs_1_ = bf16[2,192,1024]{2,1,0:T(8,128)(2,1)S(1)} collective-permute-done((bf16[2,192,1024]{2,1,0:T(8,128)(2,1)S(1)}, bf16[2,192,1024]{2,1,0:T(8,128)(2,1)S(1)}, u32[]{:S(2)}, u32[]{:S(2)}) %collective-permute-start.20) | collective-permute-done | bytes 786464 | tf_op jit(solution)/shard_map/ppermute | solution.py:273
  172.7 8.6 %finish3.2 = (bf16[192,1024]{1,0:T(8,128)(2,1)S(1)}, bf16[192,1024]{1,0:T(8,128)(2,1)S(1)}) custom-call(s32[4]{0:T(128)S(1)} %pad_add_fusion.info, f32[2,192,1024]{2,1,0:T(8,128)} %update.2.r, bf16[2,192,1024]{2,1,0:T(8,128)(2,1)S(1)} %collective-permute-done.19.a, bf16[2,16,160,1024]{3,2,1,0:T(8,128)(2,1)} %bitcast.26, bf16[2,512,512]{2,1,0:T(8,128)(2,1)S(1)} %copy-done.4, ...), custom_call_target="tpu_custom_call" | custom-call | flops 800000000 | bytes 1024 | tf_op jit(solution)/shard_map/finish3/pallas_call | solution.py:373
  181.3 3.2 %collective-permute-start.21 = (bf16[192,1024]{1,0:T(8,128)(2,1)S(1)}, bf16[192,1024]{1,0:T(8,128)(2,1)S(1)}, u32[]{:S(2)}, u32[]{:S(2)}) collective-permute-start(bf16[192,1024]{1,0:T(8,128)(2,1)S(1)} %get-tuple-element.30), channel_id=1, source_target_pairs={{0,1},{1,0},{2,3},{3,2},{4,5},{5,4},{6,7},{7,6},{8,9},{9,8},{10,11... | collective-permute-start | bytes 1179656 | tf_op jit(solution)/shard_map/ppermute | solution.py:276
  184.5 6.6 %update.3.r = f32[2,192,1024]{2,1,0:T(8,128)} custom-call(s32[4]{0:T(128)S(1)} %pad_add_fusion.info, f32[2,192,1024]{2,1,0:T(8,128)} %copy-done.6, bf16[2,192,1024]{2,1,0:T(8,128)(2,1)} %collective-permute-done.22.to_3, bf16[2,192,1024]{2,1,0:T(8,128)(2,1)} %collective-permute-done.23.before.to_2, bf16[4,128,1024]{2,1,0:T(8,128)(2,1)S(1)} %copy-done.3, ...), custom_call_target="tpu_custom_call" | custom-call | bytes 1024 | tf_op jit(solution)/shard_map/update/pallas_call | solution.py:416
  191.1 8.4 %finish3.3 = (bf16[192,1024]{1,0:T(8,128)(2,1)S(1)}, bf16[192,1024]{1,0:T(8,128)(2,1)S(1)}) custom-call(s32[4]{0:T(128)S(1)} %pad_add_fusion.info, f32[2,192,1024]{2,1,0:T(8,128)} %update.3.r, bf16[2,192,1024]{2,1,0:T(8,128)(2,1)S(1)} %collective-permute-done.25.a, bf16[2,16,160,1024]{3,2,1,0:T(8,128)(2,1)} %bitcast.27, bf16[2,512,512]{2,1,0:T(8,128)(2,1)S(1)} %copy-done.4, ...), custom_call_target="tpu_custom_call" | custom-call | flops 800000000 | bytes 1024 | tf_op jit(solution)/shard_map/finish3/pallas_call | solution.py:373
  199.9 1.4 collective-permute-done.27
  201.4 1.3 pad_maximum_fusion
  (57 shorter events, 1.0 us)
Async XLA Ops:
  6.5 2.8 %copy-start.13 = (bf16[1024,16,32]{0,2,1:T(8,128)(2,1)S(1)}, bf16[1024,16,32]{0,2,1:T(8,128)(2,1)}, u32[]{:S(2)}) copy-start(bf16[1024,16,32]{0,2,1:T(8,128)(2,1)} %param.6) | copy-start | bytes 3145732
  6.5 78.0 %all-gather.5.cloned.1.call-start = ((), (), s32[]{:S(2)}) async-start(), calls=%async_computation | async-start | bytes 10813440 | tf_op jit(solution)/shard_map/all_gather | solution.py:303
  9.2 136.6 %all-gather.7.cloned.1.call-start = ((), (), s32[]{:S(2)}) async-start(), calls=%async_computation.1 | async-start | bytes 8650752 | tf_op jit(solution)/shard_map/all_gather | solution.py:303
  9.3 9.5 %collective-permute-start = (bf16[128,1024]{1,0:T(8,128)(2,1)S(1)}, bf16[128,1024]{1,0:T(8,128)(2,1)S(1)}, u32[]{:S(2)}, u32[]{:S(2)}) collective-permute-start(bf16[128,1024]{1,0:T(8,128)(2,1)S(1)} %bitcast.35), channel_id=1, source_target_pairs={{10,2},{35,3},{12,4},{37,5},{14,6},{39,7},{18,10},{43,11},{20,12},... | collective-permute-start | bytes 786440 | tf_op jit(solution)/shard_map/ppermute | solution.py:286
  14.0 8.9 %collective-permute-start.1 = (bf16[128,1024]{1,0:T(8,128)(2,1)S(1)}, bf16[128,1024]{1,0:T(8,128)(2,1)S(1)}, u32[]{:S(2)}, u32[]{:S(2)}) collective-permute-start(bf16[128,1024]{1,0:T(8,128)(2,1)S(1)} %bitcast.36), channel_id=1, source_target_pairs={{18,2},{67,3},{20,4},{69,5},{22,6},{71,7},{26,10},{75,11},{28,12},... | collective-permute-start | bytes 786440 | tf_op jit(solution)/shard_map/ppermute | solution.py:286
  16.3 10.3 %collective-permute-start.2 = (bf16[128,1024]{1,0:T(8,128)(2,1)S(1)}, bf16[128,1024]{1,0:T(8,128)(2,1)S(1)}, u32[]{:S(2)}, u32[]{:S(2)}) collective-permute-start(bf16[128,1024]{1,0:T(8,128)(2,1)S(1)} %bitcast.37), channel_id=1, source_target_pairs={{26,2},{99,3},{28,4},{101,5},{30,6},{103,7},{2,10},{107,11},{4,12}... | collective-permute-start | bytes 786440 | tf_op jit(solution)/shard_map/ppermute | solution.py:286
  26.7 9.1 %copy-start = (bf16[4,128,1024]{2,1,0:T(8,128)(2,1)}, bf16[4,128,1024]{2,1,0:T(8,128)(2,1)S(1)}, u32[]{:S(2)}) copy-start(bf16[4,128,1024]{2,1,0:T(8,128)(2,1)S(1)} %pad_maximum_fusion.1.refs_1_.refs_0_) | copy-start | bytes 3145732
  26.7 17.5 %collective-permute-start.3 = (bf16[4,128,1024]{2,1,0:T(8,128)(2,1)S(1)}, bf16[4,128,1024]{2,1,0:T(8,128)(2,1)}, u32[]{:S(2)}, u32[]{:S(2)}) collective-permute-start(bf16[4,128,1024]{2,1,0:T(8,128)(2,1)S(1)} %pad_maximum_fusion.1.refs_1_.refs_0_), channel_id=1, source_target_pairs={{34,2},{11,3},{36,4},{13,5},{38,6},{15,7},{42,10},{19,11},{44,12},... | collective-permute-start | bytes 3145736 | tf_op jit(solution)/shard_map/ppermute | solution.py:286
  31.2 19.5 %collective-permute-start.4 = (bf16[4,128,1024]{2,1,0:T(8,128)(2,1)S(1)}, bf16[4,128,1024]{2,1,0:T(8,128)(2,1)}, u32[]{:S(2)}, u32[]{:S(2)}) collective-permute-start(bf16[4,128,1024]{2,1,0:T(8,128)(2,1)S(1)} %pad_maximum_fusion.1.refs_1_.refs_0_), channel_id=1, source_target_pairs={{98,2},{27,3},{100,4},{29,5},{102,6},{31,7},{106,10},{3,11},{108,1... | collective-permute-start | bytes 3145736 | tf_op jit(solution)/shard_map/ppermute | solution.py:286
  33.2 17.5 %collective-permute-start.18 = (bf16[4,32,1024]{2,1,0:T(8,128)(2,1)S(1)}, bf16[4,32,1024]{2,1,0:T(8,128)(2,1)S(1)}, u32[]{:S(2)}, u32[]{:S(2)}) collective-permute-start(bf16[4,32,1024]{2,1,0:T(8,128)(2,1)S(1)} %get-tuple-element.37), channel_id=1, source_target_pairs={{6,2},{7,3},{14,10},{15,11},{22,18},{23,19},{30,26},{31,27},{38,34... | collective-permute-start | bytes 786440 | tf_op jit(solution)/shard_map/ppermute | solution.py:273
  35.9 17.4 %copy-start.4 = (bf16[2,512,512]{2,1,0:T(8,128)(2,1)S(1)}, bf16[2,512,512]{2,1,0:T(8,128)(2,1)}, u32[]{:S(2)}) copy-start(bf16[2,512,512]{2,1,0:T(8,128)(2,1)} %dt_own.15) | copy-start | bytes 3145732
  50.7 0.7 copy-start.14
  51.4 24.1 %copy-start.1 = (bf16[4,128,1024]{2,1,0:T(8,128)(2,1)S(1)}, bf16[4,128,1024]{2,1,0:T(8,128)(2,1)}, u32[]{:S(2)}) copy-start(bf16[4,128,1024]{2,1,0:T(8,128)(2,1)} %copy-done) | copy-start | bytes 3145732
  53.3 31.3 %collective-permute-start.7 = (bf16[2,512,512]{2,1,0:T(8,128)(2,1)S(1)}, bf16[2,512,512]{2,1,0:T(8,128)(2,1)S(1)}, u32[]{:S(2)}, u32[]{:S(2)}) collective-permute-start(bf16[2,512,512]{2,1,0:T(8,128)(2,1)S(1)} %copy-done.4), channel_id=1, source_target_pairs={{0,1},{1,0},{2,3},{3,2},{4,5},{5,4},{6,7},{7,6},{8,9},{9,8},{10,11... | collective-permute-start | bytes 3145736 | tf_op jit(solution)/shard_map/ppermute | solution.py:276
  69.1 10.3 %collective-permute-start.5 = (bf16[2,128,1024]{2,1,0:T(8,128)(2,1)S(1)}, bf16[2,128,1024]{2,1,0:T(8,128)(2,1)}, u32[]{:S(2)}, u32[]{:S(2)}) collective-permute-start(bf16[2,128,1024]{2,1,0:T(8,128)(2,1)S(1)} %slice.17), channel_id=1, source_target_pairs={{34,2},{11,3},{36,4},{13,5},{38,6},{15,7},{42,10},{19,11},{44,12},... | collective-permute-start | bytes 1572872 | tf_op jit(solution)/shard_map/ppermute | solution.py:286
  72.2 11.5 %collective-permute-start.6 = (bf16[2,128,1024]{2,1,0:T(8,128)(2,1)S(1)}, bf16[2,128,1024]{2,1,0:T(8,128)(2,1)}, u32[]{:S(2)}, u32[]{:S(2)}) collective-permute-start(bf16[2,128,1024]{2,1,0:T(8,128)(2,1)S(1)} %slice.18), channel_id=1, source_target_pairs={{98,2},{27,3},{100,4},{29,5},{102,6},{31,7},{106,10},{3,11},{108,1... | collective-permute-start | bytes 1572872 | tf_op jit(solution)/shard_map/ppermute | solution.py:286
  75.5 25.1 %collective-permute-start.14 = (bf16[4,128,1024]{2,1,0:T(8,128)(2,1)S(1)}, bf16[4,128,1024]{2,1,0:T(8,128)(2,1)}, u32[]{:S(2)}, u32[]{:S(2)}) collective-permute-start(bf16[4,128,1024]{2,1,0:T(8,128)(2,1)S(1)} %copy-done.1), channel_id=1, source_target_pairs={{0,1},{1,0},{2,3},{3,2},{4,5},{5,4},{6,7},{7,6},{8,9},{9,8},{10,11... | collective-permute-start | bytes 3145736 | tf_op jit(solution)/shard_map/ppermute | solution.py:276
  79.4 13.7 %collective-permute-start.8 = (bf16[2,128,1024]{2,1,0:T(8,128)(2,1)}, bf16[2,128,1024]{2,1,0:T(8,128)(2,1)}, u32[]{:S(2)}, u32[]{:S(2)}) collective-permute-start(bf16[2,128,1024]{2,1,0:T(8,128)(2,1)} %collective-permute-done.5.refs_1_.refs_3_), channel_id=1, source_target_pairs={{0,1},{1,0},{2,3},{3,2},{4,5},{5,4},{6,7},{7,6},{8,9},{9,8},{10,11... | collective-permute-start | bytes 1572872 | tf_op jit(solution)/shard_map/ppermute | solution.py:276
  83.7 9.9 %collective-permute-start.9 = (bf16[2,128,1024]{2,1,0:T(8,128)(2,1)}, bf16[2,128,1024]{2,1,0:T(8,128)(2,1)}, u32[]{:S(2)}, u32[]{:S(2)}) collective-permute-start(bf16[2,128,1024]{2,1,0:T(8,128)(2,1)} %collective-permute-done.6.refs_2_.refs_4_), channel_id=1, source_target_pairs={{0,1},{1,0},{2,3},{3,2},{4,5},{5,4},{6,7},{7,6},{8,9},{9,8},{10,11... | collective-permute-start | bytes 1572872 | tf_op jit(solution)/shard_map/ppermute | solution.py:276
  84.6 61.3 %copy-start.5 = (bf16[2,512,512]{2,1,0:T(8,128)(2,1)}, bf16[2,512,512]{2,1,0:T(8,128)(2,1)S(1)}, u32[]{:S(2)}) copy-start(bf16[2,512,512]{2,1,0:T(8,128)(2,1)S(1)} %collective-permute-done.7.dt_oth) | copy-start | bytes 3145732
  84.6 0.6 copy-start.11
  85.2 1.5 copy-start.12
  91.2 1.1 copy-start.8
  92.3 9.8 %collective-permute-start.13 = (bf16[2,192,1024]{2,1,0:T(8,128)(2,1)}, bf16[2,192,1024]{2,1,0:T(8,128)(2,1)S(1)}, u32[]{:S(2)}, u32[]{:S(2)}) collective-permute-start(bf16[2,192,1024]{2,1,0:T(8,128)(2,1)} %get-tuple-element.22.refs_2_), channel_id=1, source_target_pairs={{0,2},{1,3},{8,10},{9,11},{16,18},{17,19},{24,26},{25,27},{32,34},... | collective-permute-start | bytes 2359304 | tf_op jit(solution)/shard_map/ppermute | solution.py:273
  93.0 24.4 %collective-permute-start.15 = (bf16[4,128,1024]{2,1,0:T(8,128)(2,1)}, bf16[4,128,1024]{2,1,0:T(8,128)(2,1)}, u32[]{:S(2)}, u32[]{:S(2)}) collective-permute-start(bf16[4,128,1024]{2,1,0:T(8,128)(2,1)} %collective-permute-done.3.refs_1_), channel_id=1, source_target_pairs={{0,1},{1,0},{2,3},{3,2},{4,5},{5,4},{6,7},{7,6},{8,9},{9,8},{10,11... | collective-permute-start | bytes 3145736 | tf_op jit(solution)/shard_map/ppermute | solution.py:276
  93.1 24.3 %collective-permute-start.16 = (bf16[4,128,1024]{2,1,0:T(8,128)(2,1)}, bf16[4,128,1024]{2,1,0:T(8,128)(2,1)}, u32[]{:S(2)}, u32[]{:S(2)}) collective-permute-start(bf16[4,128,1024]{2,1,0:T(8,128)(2,1)} %collective-permute-done.4.refs_2_), channel_id=1, source_target_pairs={{0,1},{1,0},{2,3},{3,2},{4,5},{5,4},{6,7},{7,6},{8,9},{9,8},{10,11... | collective-permute-start | bytes 3145736 | tf_op jit(solution)/shard_map/ppermute | solution.py:276
  93.6 22.5 %collective-permute-start.10 = (bf16[2,192,1024]{2,1,0:T(8,128)(2,1)}, bf16[2,192,1024]{2,1,0:T(8,128)(2,1)}, u32[]{:S(2)}, u32[]{:S(2)}) collective-permute-start(bf16[2,192,1024]{2,1,0:T(8,128)(2,1)} %get-tuple-element.22.refs_2_), channel_id=1, source_target_pairs={{0,6},{1,7},{8,14},{9,15},{16,22},{17,23},{24,30},{25,31},{32,38},... | collective-permute-start | bytes 2359304 | tf_op jit(solution)/shard_map/ppermute | solution.py:273
  99.4 1.1 copy-start.6
  100.6 20.1 %collective-permute-start.12 = (bf16[2,192,1024]{2,1,0:T(8,128)(2,1)}, bf16[2,192,1024]{2,1,0:T(8,128)(2,1)}, u32[]{:S(2)}, u32[]{:S(2)}) collective-permute-start(bf16[2,192,1024]{2,1,0:T(8,128)(2,1)} %get-tuple-element.24.refs_1_.refs_2_), channel_id=1, source_target_pairs={{0,2},{1,3},{8,10},{9,11},{16,18},{17,19},{24,26},{25,27},{32,34},... | collective-permute-start | bytes 2359304 | tf_op jit(solution)/shard_map/ppermute | solution.py:273
  102.1 0.9 copy-start.9
  103.0 30.0 %collective-permute-start.22 = (bf16[2,192,1024]{2,1,0:T(8,128)(2,1)}, bf16[2,192,1024]{2,1,0:T(8,128)(2,1)}, u32[]{:S(2)}, u32[]{:S(2)}) collective-permute-start(bf16[2,192,1024]{2,1,0:T(8,128)(2,1)} %get-tuple-element.24.refs_1_.refs_2_), channel_id=1, source_target_pairs={{0,6},{1,7},{8,14},{9,15},{16,22},{17,23},{24,30},{25,31},{32,38},... | collective-permute-start | bytes 2359304 | tf_op jit(solution)/shard_map/ppermute | solution.py:273
  104.3 13.2 %copy-start.10 = (bf16[2,192,1024]{2,1,0:T(8,128)(2,1)S(1)}, bf16[2,192,1024]{2,1,0:T(8,128)(2,1)}, u32[]{:S(2)}) copy-start(bf16[2,192,1024]{2,1,0:T(8,128)(2,1)} %copy-done.9) | copy-start | bytes 2359300
  116.1 23.0 %collective-permute-start.11 = (bf16[2,192,1024]{2,1,0:T(8,128)(2,1)}, bf16[2,192,1024]{2,1,0:T(8,128)(2,1)S(1)}, u32[]{:S(2)}, u32[]{:S(2)}) collective-permute-start(bf16[2,192,1024]{2,1,0:T(8,128)(2,1)} %collective-permute-done.10.to_3), channel_id=1, source_target_pairs={{6,4},{7,5},{14,12},{15,13},{22,20},{23,21},{30,28},{31,29},{38,36... | collective-permute-start | bytes 2359304 | tf_op jit(solution)/shard_map/ppermute | solution.py:273
  119.1 26.8 %collective-permute-start.17 = (bf16[2,192,1024]{2,1,0:T(8,128)(2,1)}, bf16[2,192,1024]{2,1,0:T(8,128)(2,1)}, u32[]{:S(2)}, u32[]{:S(2)}) collective-permute-start(bf16[2,192,1024]{2,1,0:T(8,128)(2,1)} %finish1.2.own.refs_3_), channel_id=1, source_target_pairs={{2,4},{3,5},{10,12},{11,13},{18,20},{19,21},{26,28},{27,29},{34,36... | collective-permute-start | bytes 2359304 | tf_op jit(solution)/shard_map/ppermute | solution.py:273
  133.0 19.4 %collective-permute-start.23 = (bf16[2,192,1024]{2,1,0:T(8,128)(2,1)}, bf16[2,192,1024]{2,1,0:T(8,128)(2,1)}, u32[]{:S(2)}, u32[]{:S(2)}) collective-permute-start(bf16[2,192,1024]{2,1,0:T(8,128)(2,1)} %collective-permute-done.22.to_3), channel_id=1, source_target_pairs={{6,4},{7,5},{14,12},{15,13},{22,20},{23,21},{30,28},{31,29},{38,36... | collective-permute-start | bytes 2359304 | tf_op jit(solution)/shard_map/ppermute | solution.py:273
  135.2 4.0 %copy-start.2 = (bf16[4,128,1024]{2,1,0:T(8,128)(2,1)S(1)}, bf16[4,128,1024]{2,1,0:T(8,128)(2,1)}, u32[]{:S(2)}) copy-start(bf16[4,128,1024]{2,1,0:T(8,128)(2,1)} %copy-done) | copy-start | bytes 3145732
  137.6 14.8 %collective-permute-start.24 = (bf16[2,192,1024]{2,1,0:T(8,128)(2,1)}, bf16[2,192,1024]{2,1,0:T(8,128)(2,1)}, u32[]{:S(2)}, u32[]{:S(2)}) collective-permute-start(bf16[2,192,1024]{2,1,0:T(8,128)(2,1)} %finish1.3.own.refs_3_), channel_id=1, source_target_pairs={{2,4},{3,5},{10,12},{11,13},{18,20},{19,21},{26,28},{27,29},{34,36... | collective-permute-start | bytes 2359304 | tf_op jit(solution)/shard_map/ppermute | solution.py:273
  145.9 1.4 copy-start.7
  148.6 20.6 %collective-permute-start.19 = (bf16[2,192,1024]{2,1,0:T(8,128)(2,1)S(1)}, bf16[2,192,1024]{2,1,0:T(8,128)(2,1)S(1)}, u32[]{:S(2)}, u32[]{:S(2)}) collective-permute-start(bf16[2,192,1024]{2,1,0:T(8,128)(2,1)S(1)} %finish2.1.refs_4_), channel_id=1, source_target_pairs={{4,6},{5,7},{12,14},{13,15},{20,22},{21,23},{28,30},{29,31},{36,38... | collective-permute-start | bytes 2359304 | tf_op jit(solution)/shard_map/ppermute | solution.py:273
  151.1 21.6 %collective-permute-start.20 = (bf16[2,192,1024]{2,1,0:T(8,128)(2,1)S(1)}, bf16[2,192,1024]{2,1,0:T(8,128)(2,1)S(1)}, u32[]{:S(2)}, u32[]{:S(2)}) collective-permute-start(bf16[2,192,1024]{2,1,0:T(8,128)(2,1)S(1)} %partial.2), channel_id=1, source_target_pairs={{2,6},{3,7},{10,14},{11,15},{18,22},{19,23},{26,30},{27,31},{34,38... | collective-permute-start | bytes 2359304 | tf_op jit(solution)/shard_map/ppermute | solution.py:273
  154.0 37.1 %collective-permute-start.25 = (bf16[2,192,1024]{2,1,0:T(8,128)(2,1)S(1)}, bf16[2,192,1024]{2,1,0:T(8,128)(2,1)S(1)}, u32[]{:S(2)}, u32[]{:S(2)}) collective-permute-start(bf16[2,192,1024]{2,1,0:T(8,128)(2,1)S(1)} %both2.1.refs_4_), channel_id=1, source_target_pairs={{4,6},{5,7},{12,14},{13,15},{20,22},{21,23},{28,30},{29,31},{36,38... | collective-permute-start | bytes 2359304 | tf_op jit(solution)/shard_map/ppermute | solution.py:273
  156.6 27.9 %copy-start.3 = (bf16[4,128,1024]{2,1,0:T(8,128)(2,1)S(1)}, bf16[4,128,1024]{2,1,0:T(8,128)(2,1)}, u32[]{:S(2)}) copy-start(bf16[4,128,1024]{2,1,0:T(8,128)(2,1)} %copy-done) | copy-start | bytes 3145732
  156.6 34.5 %collective-permute-start.26 = (bf16[2,192,1024]{2,1,0:T(8,128)(2,1)S(1)}, bf16[2,192,1024]{2,1,0:T(8,128)(2,1)S(1)}, u32[]{:S(2)}, u32[]{:S(2)}) collective-permute-start(bf16[2,192,1024]{2,1,0:T(8,128)(2,1)S(1)} %partial.3), channel_id=1, source_target_pairs={{2,6},{3,7},{10,14},{11,15},{18,22},{19,23},{26,30},{27,31},{34,38... | collective-permute-start | bytes 2359304 | tf_op jit(solution)/shard_map/ppermute | solution.py:273
  181.3 18.5 %collective-permute-start.21 = (bf16[192,1024]{1,0:T(8,128)(2,1)S(1)}, bf16[192,1024]{1,0:T(8,128)(2,1)S(1)}, u32[]{:S(2)}, u32[]{:S(2)}) collective-permute-start(bf16[192,1024]{1,0:T(8,128)(2,1)S(1)} %get-tuple-element.30), channel_id=1, source_target_pairs={{0,1},{1,0},{2,3},{3,2},{4,5},{5,4},{6,7},{7,6},{8,9},{9,8},{10,11... | collective-permute-start | bytes 1179656 | tf_op jit(solution)/shard_map/ppermute | solution.py:276
  199.5 1.8 collective-permute-start.27
Sparse Core Ops, SparseCore 0:
  9.6 66.5 all-gather.4
  78.5 50.3 all-gather.6
